TPU v7x, 256 devices: a whole 4x4x8 slice. The times are simulated.
256 devices in a mesh: queue: 32 (over y_hi, z, core), mp: 8 (over y_lo, x).
Axes of the slice: x: 4, y: 4 (y_hi: 2, y_lo: 2; y = y_hi * 2 + y_lo), z: 8, core: 2. Of those that a mesh axis runs over, the one named last changes fastest.
Arguments:
- latents: bfloat16 [16384, 3072], P('queue', 'mp'), may hold values from -6 to 6
- step_index: int32 [64], P('queue'), may hold values from 1 to 50
- head_index: int32 [1], replicated, may hold values from 0 to 63
- band: int32 [24], P('mp'), may hold values from 1 to 4, as said below
- mod_table: bfloat16 [50, 2, 3072], replicated, may hold values from -3 to 3
- gate_table: bfloat16 [50, 3072], P(None, 'mp'), may hold values from -4 to 4
- qkv_weight: bfloat16 [3, 3072, 3072], P(None, None, 'mp')
- out_weight: bfloat16 [3072, 3072], P('mp'), may hold values from -0.109375 to 0.109375
Outputs:
- velocity: bfloat16 [16384, 3072], P('queue', 'mp')
- head_frame: bfloat16 [256, 3072], P('queue', 'mp')
Inputs may be any that keep to these rules, and one draw needn't show every extreme that they name: band is at most 4 and equals it for some head.
All inputs are finite; a program needn't handle non-finite values.
Results may differ from a plain program's by a relative error of at most 0.03.
Values may be sent and summed in bfloat16 or wider, within the bound.
No kernel may reach another device: no remote copies, remote signals or barrier semaphores. Data moves between devices by JAX's collectives and lax.ppermute only.
A program may use at most 128 MiB of HBM per device.

v0:
```python
import jax
import jax.numpy as jnp
from jax import lax
from jax.sharding import PartitionSpec as P

STEPS = 50


def passed_along(value, axis, steps):
    count = lax.axis_size(axis)
    pairs = [(source, (source + steps) % count) for source in range(count)]
    return lax.ppermute(value, axis, pairs)


def from_root(block, axis, source):
    block = jnp.where(lax.axis_index(axis) == source, block, jnp.zeros_like(block))
    return lax.psum(block, axis)


def on_device(latents, step_index, head_index, band, mod_table, gate_table, qkv_weight, out_weight):
    rows = latents.shape[0]
    frames = step_index.shape[0]
    tokf = rows // frames
    width = mod_table.shape[2]
    local_heads = band.shape[0]
    head_size = qkv_weight.shape[2] // local_heads
    count = lax.axis_size("queue")
    me_index = lax.axis_index("queue")
    frames_all = frames * count
    whole = lax.all_gather(latents, "mp", axis=1, tiled=True)
    latent_f = whole.astype(jnp.float32).reshape(frames, tokf, width)
    mean = jnp.mean(latent_f, axis=-1, keepdims=True)
    var = jnp.mean(jnp.square(latent_f - mean), axis=-1, keepdims=True)
    normed = (latent_f - mean) / jnp.sqrt(var + 1e-06)
    onehot = (step_index[:, None] == (jnp.arange(STEPS, dtype=jnp.int32) + 1)[None, :]).astype(
        jnp.bfloat16
    )
    modul = jnp.dot(
        onehot, mod_table.reshape(STEPS, 2 * width), preferred_element_type=jnp.float32
    ).reshape(frames, 2, width)
    modulated = (
        (normed * (1.0 + modul[:, 1][:, None, :]) + modul[:, 0][:, None, :])
        .astype(jnp.bfloat16)
        .reshape(rows, width)
    )
    packed = jnp.einsum(
        "rd,cde->cre", modulated, qkv_weight, preferred_element_type=jnp.float32
    ).astype(jnp.bfloat16)
    query = packed[0]
    own_kv = packed[1:]
    lower = [own_kv]
    upper = [own_kv]
    for distance in (1, 2):
        lower.append(passed_along(own_kv, "queue", distance))
        upper.append(passed_along(own_kv, "queue", -distance))
    window_kv = jnp.concatenate([lower[2], lower[1], own_kv, upper[1], upper[2]], axis=1)
    head = head_index[0]
    start_slot = me_index * frames
    query_pos = jnp.mod(start_slot + jnp.arange(frames, dtype=jnp.int32) - head, frames_all)
    key_pos = jnp.mod(
        start_slot - 2 * frames + jnp.arange(5 * frames, dtype=jnp.int32) - head, frames_all
    )
    distance_pos = jnp.abs(key_pos[None, :] - query_pos[:, None])
    allowed = distance_pos[None, :, :] <= band[:, None, None]
    qshaped = query.reshape(frames, tokf, local_heads, head_size)
    kshaped = window_kv[0].reshape(5 * frames, tokf, local_heads, head_size)
    vshaped = window_kv[1].reshape(5 * frames, tokf, local_heads, head_size)
    scores = jnp.einsum(
        "fthd,gshd->hftgs", qshaped, kshaped, preferred_element_type=jnp.float32
    ) / jnp.sqrt(jnp.float32(head_size))
    scores = jnp.where(allowed[:, :, None, :, None], scores, jnp.float32(-1e30))
    top = jnp.max(scores, axis=(3, 4), keepdims=True)
    expd = jnp.exp(scores - top)
    total = jnp.sum(expd, axis=(3, 4))
    weights = expd.astype(jnp.bfloat16)
    summed = jnp.einsum("hftgs,gshd->fthd", weights, vshaped, preferred_element_type=jnp.float32)
    attended = (
        (summed / total.transpose(1, 2, 0)[..., None])
        .astype(jnp.bfloat16)
        .reshape(rows, local_heads * head_size)
    )
    term = jnp.dot(attended, out_weight, preferred_element_type=jnp.float32)
    projected = lax.psum_scatter(
        term.astype(jnp.bfloat16), "mp", scatter_dimension=1, tiled=True
    ).astype(jnp.float32)
    gate = jnp.dot(onehot, gate_table, preferred_element_type=jnp.float32)
    columns = latents.shape[1]
    own_latent = latents.astype(jnp.float32).reshape(frames, tokf, columns)
    velocity = (own_latent + gate[:, None, :] * projected.reshape(frames, tokf, columns)).astype(
        jnp.bfloat16
    )
    level = step_index.astype(jnp.float32) / STEPS
    sigma = 3.0 * level / (1.0 + 2.0 * level)
    owner = head // frames
    local_frame = jnp.mod(head, frames)
    head_latent = lax.dynamic_index_in_dim(own_latent, local_frame, 0, keepdims=False)
    head_velocity = lax.dynamic_index_in_dim(velocity, local_frame, 0, keepdims=False).astype(
        jnp.float32
    )
    head_sigma = lax.dynamic_index_in_dim(sigma, local_frame, 0, keepdims=False)
    candidate = (head_latent - head_sigma * head_velocity).astype(jnp.bfloat16)
    share_rows = tokf // count
    copied = from_root(candidate, "queue", owner)
    head_frame = lax.dynamic_slice_in_dim(copied, me_index * share_rows, share_rows, 0)
    return (velocity.reshape(rows, columns), head_frame)


def solution(mesh):
    placed = (
        P("queue", "mp"),
        P("queue"),
        P(),
        P("mp"),
        P(),
        P(None, "mp"),
        P(None, None, "mp"),
        P("mp", None),
    )
    return jax.shard_map(
        on_device,
        mesh=mesh,
        in_specs=placed,
        out_specs=(P("queue", "mp"), P("queue", "mp")),
        check_vma=False,
    )
```

profile of v0, /device:TPU:6, one launch (start us, length us, event | category | flops | bytes accessed | tf_op | source)
XLA Modules:
  0.0 466.8 jit_solution(637113803911944447)
XLA Ops:
  7.2 0.7 all-gather.2.cloned.1.call-update
  8.0 1.6 pad
  9.6 1.0 copy.43
  10.5 2.3 dot_general.24
  12.8 0.3 fusion.40
  13.2 44.6 %all-gather.2.cloned.1.call-done = bf16[512,3072]{1,0:T(8,128)(2,1)} async-done(((bf16[512,384]{1,0:T(8,128)(2,1)}), bf16[512,3072]{1,0:T(8,128)(2,1)}) %all-gather.2.cloned.1.call-update) | async-done | bytes 3145744 | tf_op jit(solution)/shard_map/all_gather | solution.py:30
  57.8 2.5 convert_reduce_fusion
  60.4 0.3 copy-done.1
  60.7 1.0 fusion.8
  61.6 1.9 fusion.11
  63.5 0.1 copy-done.7
  63.7 4.3 fusion.20
  68.0 1.0 slice.26
  68.9 1.5 collective-permute-start
  71.1 0.1 collective-permute-start.1
  71.2 5.4 %collective-permute-start.2 = (bf16[2,512,384]{2,1,0:T(8,128)(2,1)}, bf16[2,512,384]{2,1,0:T(8,128)(2,1)}, u32[]{:S(2)}, u32[]{:S(2)}) collective-permute-start(bf16[2,512,384]{2,1,0:T(8,128)(2,1)} %slice.26), channel_id=1, source_target_pairs={{0,248},{8,0},{16,8},{24,16},{32,24},{40,32},{48,40},{56,48},{64,5... | collective-permute-start | bytes 2359304 | tf_op jit(solution)/shard_map/ppermute | solution.py:12
  76.6 0.1 subtract_abs_fusion
  76.7 0.6 collective-permute-start.3
  77.3 0.1 broadcast_compare_fusion
  77.4 0.8 slice.28
  78.1 2.0 reshape.136
  80.2 13.2 %collective-permute-done = bf16[2,512,384]{2,1,0:T(8,128)(2,1)} collective-permute-done((bf16[2,512,384]{2,1,0:T(8,128)(2,1)}, bf16[2,512,384]{2,1,0:T(8,128)(2,1)}, u32[]{:S(2)}, u32[]{:S(2)}) %collective-permute-start) | collective-permute-done | bytes 786464 | tf_op jit(solution)/shard_map/ppermute | solution.py:12
  93.4 1.2 constant_dynamic-update-slice_fusion.4
  94.6 3.9 collective-permute-done.1
  98.5 1.3 constant_dynamic-update-slice_fusion.3
  99.8 0.2 constant_dynamic-update-slice_fusion.2
  99.9 1.3 constant_dynamic-update-slice_fusion.1
  101.2 1.8 collective-permute-done.3
  103.0 1.3 constant_dynamic-update-slice_fusion
  104.3 2.3 fusion.58
  106.6 6.2 %reshape_squeeze.11 = bf16[10,256,3,128]{3,2,1,0:T(4,128)(2,1)} reshape(bf16[1,2560,384]{2,1,0:T(8,128)(2,1)} %get-tuple-element.3) | data formatting | bytes 3932160 | tf_op jit(solution)/shard_map/reshape;squeeze | solution.py:66
  112.7 6.1 %reshape_squeeze.9 = bf16[10,256,3,128]{3,2,1,0:T(4,128)(2,1)} reshape(bf16[1,2560,384]{2,1,0:T(8,128)(2,1)} %get-tuple-element.2) | data formatting | bytes 3932160 | tf_op jit(solution)/shard_map/reshape;squeeze | solution.py:67
  118.8 8.6 %fusion = (f32[3,2,256]{2,1,0:T(2,128)S(1)}, f32[3,2,256,10,256]{2,4,3,1,0:T(8,128)}) fusion(pred[3,2,10]{2,1,0:T(4,128)(4,1)S(1)} %broadcast_compare_fusion, bf16[10,256,3,128,1]{3,2,1,0,4:T(4,128)(2,1)} %bitcast.76, bf16[2,256,3,128,1]{3,2,1,0,4:T(4,128)(2,1)S(1)} %bitcast.82), kind=kOutput, calls=%fused_computation.2 | convolution fusion | flops 1018427904 | bytes 18094140 | tf_op jit(solution)/shard_map/fthd,gshd->hftgs/dot_general | solution.py:68
  127.4 9.2 %fusion.1 = f32[3,2,256]{2,1,0:T(2,128)S(1)} fusion(f32[3,2,256,10,256]{2,4,3,1,0:T(8,128)} %get-tuple-element.7, f32[3,2,256]{2,1,0:T(2,128)S(1)} %get-tuple-element.6, pred[3,2,10]{2,1,0:T(4,128)(4,1)S(1)} %broadcast_compare_fusion), kind=kLoop, calls=%fused_computation.3 | loop fusion | flops 15727104 | bytes 15740988 | tf_op jit(solution)/shard_map/reduce_sum | solution.py:74
  136.6 7.4 %fusion.33 = bf16[2,256,3,128]{1,3,0,2:T(8,128)(2,1)S(1)} fusion(f32[3,2,256,10,256]{2,4,3,1,0:T(8,128)} %get-tuple-element.7, f32[3,2,256]{2,1,0:T(2,128)S(1)} %get-tuple-element.6, pred[3,2,10]{2,1,0:T(4,128)(4,1)S(1)} %broadcast_compare_fusion, bf16[10,256,3,128,1]{3,2,1,0,4:T(4,128)(2,1)S(1)} %bitcast.81, f32[2,256,3]{1,0,2:T(2,128)S(1)} %bitcast.86), kind=kOutput, calls=%fused_computation.25 | convolution fusion | flops 1022754816 | bytes 18100284 | tf_op jit(solution)/shard_map/hftgs,gshd->fthd/dot_general | solution.py:76
  144.1 0.4 copy.27
  144.5 0.1 copy.44
  144.5 3.5 convolution_convert_fusion
  148.1 4.7 %copy.41 = bf16[512,3072]{0,1:T(8,128)(2,1)} copy(bf16[512,3072]{1,0:T(8,128)(2,1)} %convolution_convert_fusion) | data formatting | bytes 6291456
  152.9 0.9 convert.1
  153.8 0.6 dynamic_slice.16
  154.4 0.2 fusion.48
  154.6 45.5 %reduce-scatter.4.cloned.1.call-done = bf16[384,512]{1,0:T(8,128)(2,1)} async-done(((bf16[3072,512]{1,0:T(8,128)(2,1)}), bf16[384,512]{1,0:T(8,128)(2,1)}) %reduce-scatter.4.cloned.1.call-update) | async-done | bytes 393232
  200.1 1.2 copy.42
  201.4 2.4 fusion.46
  203.8 0.9 fusion.39
  204.7 254.3 %all-reduce.2.cloned.1.call-done = bf16[256,384]{1,0:T(8,128)(2,1)} async-done(((bf16[256,384]{1,0:T(8,128)(2,1)}), bf16[256,384]{1,0:T(8,128)(2,1)}) %all-reduce.2.cloned.1.call-update) | async-done | bytes 196624 | tf_op jit(solution)/shard_map/psum | solution.py:17
  458.9 1.3 constant_dynamic-slice_fusion
  (31 shorter events, 0.3 us)
Async XLA Ops:
  7.2 137.4 %copy-start = (bf16[384,3072]{1,0:T(8,128)(2,1)S(1)}, bf16[384,3072]{1,0:T(8,128)(2,1)}, u32[]{:S(2)}) copy-start(bf16[384,3072]{1,0:T(8,128)(2,1)} %param.15) | copy-start | bytes 7077892
  7.2 5.6 %copy-start.6 = (s32[2]{0:T(128)S(1)}, s32[2]{0:T(128)}, u32[]{:S(2)}) copy-start(s32[2]{0:T(128)} %param.9) | copy-start | bytes 28
  7.2 50.6 %all-gather.2.cloned.1.call-start = ((), (), s32[]{:S(2)}) async-start(), calls=%async_computation.1 | async-start | bytes 3538944 | tf_op jit(solution)/shard_map/all_gather | solution.py:30
  7.9 192.2 %reduce-scatter.4.cloned.1.call-start = ((), (), s32[]{:S(2)}) async-start(), calls=%async_computation.3 | async-start | bytes 3538944
  57.8 2.8 copy-start.1
  60.7 3.0 copy-start.7
  63.7 13.6 %copy-start.5 = (s32[3]{0:T(128)S(1)}, s32[3]{0:T(128)}, u32[]{:S(2)}) copy-start(s32[3]{0:T(128)} %param.11) | copy-start | bytes 40
  68.9 24.5 %collective-permute-start = (bf16[2,512,384]{2,1,0:T(8,128)(2,1)}, bf16[2,512,384]{2,1,0:T(8,128)(2,1)}, u32[]{:S(2)}, u32[]{:S(2)}) collective-permute-start(bf16[2,512,384]{2,1,0:T(8,128)(2,1)} %slice.26), channel_id=1, source_target_pairs={{0,16},{8,24},{16,32},{24,40},{32,48},{40,56},{48,64},{56,72},{64,... | collective-permute-start | bytes 2359304 | tf_op jit(solution)/shard_map/ppermute | solution.py:12
  71.1 27.4 %collective-permute-start.1 = (bf16[2,512,384]{2,1,0:T(8,128)(2,1)}, bf16[2,512,384]{2,1,0:T(8,128)(2,1)}, u32[]{:S(2)}, u32[]{:S(2)}) collective-permute-start(bf16[2,512,384]{2,1,0:T(8,128)(2,1)} %slice.26), channel_id=1, source_target_pairs={{0,8},{8,16},{16,24},{24,32},{32,40},{40,48},{48,56},{56,64},{64,7... | collective-permute-start | bytes 2359304 | tf_op jit(solution)/shard_map/ppermute | solution.py:12
  71.2 28.7 %collective-permute-start.2 = (bf16[2,512,384]{2,1,0:T(8,128)(2,1)}, bf16[2,512,384]{2,1,0:T(8,128)(2,1)}, u32[]{:S(2)}, u32[]{:S(2)}) collective-permute-start(bf16[2,512,384]{2,1,0:T(8,128)(2,1)} %slice.26), channel_id=1, source_target_pairs={{0,248},{8,0},{16,8},{24,16},{32,24},{40,32},{48,40},{56,48},{64,5... | collective-permute-start | bytes 2359304 | tf_op jit(solution)/shard_map/ppermute | solution.py:12
  76.7 26.3 %collective-permute-start.3 = (bf16[2,512,384]{2,1,0:T(8,128)(2,1)}, bf16[2,512,384]{2,1,0:T(8,128)(2,1)}, u32[]{:S(2)}, u32[]{:S(2)}) collective-permute-start(bf16[2,512,384]{2,1,0:T(8,128)(2,1)} %slice.26), channel_id=1, source_target_pairs={{0,240},{8,248},{16,0},{24,8},{32,16},{40,24},{48,32},{56,40},{64,... | collective-permute-start | bytes 2359304 | tf_op jit(solution)/shard_map/ppermute | solution.py:12
  106.6 12.3 %copy-start.4 = (bf16[2,256,3,128]{3,2,1,0:T(4,128)(2,1)S(1)}, bf16[2,256,3,128]{3,2,1,0:T(4,128)(2,1)}, u32[]{:S(2)}) copy-start(bf16[2,256,3,128]{3,2,1,0:T(4,128)(2,1)} %reshape.136) | copy-start | bytes 1179652
  127.4 9.2 %copy-start.3 = (bf16[10,256,3,128]{3,2,1,0:T(4,128)(2,1)S(1)}, bf16[10,256,3,128]{3,2,1,0:T(4,128)(2,1)}, u32[]{:S(2)}) copy-start(bf16[10,256,3,128]{3,2,1,0:T(4,128)(2,1)} %reshape_squeeze.9) | copy-start | bytes 5898244
  148.1 4.8 %copy-start.2 = (bf16[512,384]{1,0:T(8,128)(2,1)S(1)}, bf16[512,384]{1,0:T(8,128)(2,1)}, u32[]{:S(2)}) copy-start(bf16[512,384]{1,0:T(8,128)(2,1)} %param.8) | copy-start | bytes 1179652
  148.1 6.4 %copy-start.8 = (bf16[50,384]{1,0:T(8,128)(2,1)S(1)}, bf16[50,384]{1,0:T(8,128)(2,1)}, u32[]{:S(2)}) copy-start(bf16[50,384]{1,0:T(8,128)(2,1)} %param.13) | copy-start | bytes 115204
  152.8 306.1 %all-reduce.2.cloned.1.call-start = ((), (), s32[]{:S(2)}) async-start(), calls=%async_computation.2 | async-start | bytes 393216 | tf_op jit(solution)/shard_map/psum | solution.py:17
Sparse Core Ops, SparseCore 0:
  9.8 47.9 all-gather.1
  152.9 47.1 reduce-scatter.3
  203.9 254.9 all-reduce.1
where the time goes:
time: 468 us; the launch traced here: 467 us
  waiting for transfers between devices  364 us (78%)
  local copies, waits for them, and re-layouts  37.1 us (8%)
  matrix products  24.3 us (5%)
  other arithmetic  19.1 us (4%)
  between operations  14.6 us (3%)
  starting transfers between devices  7.71 us (2%)
    psum x1, waiting for transfers between devices, from_root(): return lax.psum(block, axis)  254 us
    unnamed x4, waiting for transfers between devices  46.2 us
    all_gather x1, waiting for transfers between devices, on_device(): whole = lax.all_gather(latents, 'mp', axis=1, tiled=True)  44.6 us
    ppermute x4, waiting for transfers between devices, passed_along(): return lax.ppermute(value, axis, pairs)  18.9 us
    unnamed x27, local copies, waits for them, and re-layouts  12.9 us
  transfers between devices with their start and end apart: 7, of which 6 were waited for; matrix products, arithmetic and copies ran while one was open for 3% of the time, Pallas kernels for 0%

commit v1 on v0

v1 whole, which is shorter than its diff:
```python
import functools

import jax
import jax.numpy as jnp
from jax import lax
from jax.experimental import pallas as pl
from jax.experimental.pallas import tpu as pltpu
from jax.sharding import PartitionSpec as P

STEPS = 50
EPS = 1e-06
BIG = 1e30
LOG2E = 1.4426950408889634
VMEM_LIMIT = 48 * 1024 * 1024


def ring(value, distance):
    return lax.ppermute(value, "mp", [(s, s // 4 * 4 + (s + distance) % 4) for s in range(8)])


def across(value):
    return lax.ppermute(value, "mp", [(s, s ^ 4) for s in range(8)])


def shifted(value, distance):
    count = lax.axis_size("queue")
    return lax.ppermute(value, "queue", [(s, (s + distance) % count) for s in range(count)])


def flipped(value, bit):
    return lax.ppermute(value, "queue", [(s, s ^ bit) for s in range(lax.axis_size("queue"))])


def vmem():
    return pl.BlockSpec(memory_space=pltpu.VMEM)


def smem():
    return pl.BlockSpec(memory_space=pltpu.SMEM)


def qkv_kernel(place, own, far, low, high, two_a, two_b, two_c, three_a, three_b, three_c, modul, weight, query, kv, opposite, made):
    rows, part = own.shape
    half = rows // 2
    width = weight.shape[1]
    first, second = three_a.shape[0], three_a.shape[0] + three_b.shape[0]
    opposite[:first] = three_a[...]
    opposite[first:second] = three_b[...]
    opposite[second:] = three_c[...]
    starts = [pl.multiple_of(place[i] * part, 128) for i in range(8)]
    chunk = 64
    for frame in range(2):
        if frame == 0:
            parts = [(own, 0), (far, 0), (low, 0), (high, 0), (two_a, 0), (two_a, half), (two_c, half), (opposite, 0)]
        else:
            parts = [(own, half), (far, half), (low, half), (high, half), (two_b, 0), (two_c, 0), (two_b, half), (opposite, half)]
        for at in range(0, half, chunk):
            def load(i):
                ref, base = parts[i]
                return ref[base + at : base + at + chunk, :].astype(jnp.float32)

            total = load(0)
            for i in range(1, 8):
                total = total + load(i)
            mean = jnp.sum(total, axis=1, keepdims=True) * (1.0 / width)
            square = jnp.square(load(0) - mean)
            for i in range(1, 8):
                square = square + jnp.square(load(i) - mean)
            var = jnp.sum(square, axis=1, keepdims=True) * (1.0 / width)
            inverse = lax.rsqrt(var + EPS)
            for i in range(8):
                columns = pl.ds(starts[i], part)
                shift = modul[frame, 0:1, columns].astype(jnp.float32)
                scale = modul[frame, 1:2, columns].astype(jnp.float32) + 1.0
                value = (load(i) - mean) * inverse * scale + shift
                made[frame * half + at : frame * half + at + chunk, columns] = value.astype(jnp.bfloat16)
        left = made[frame * half : (frame + 1) * half, :]
        for which in (1, 2, 0):
            result = jnp.dot(left, weight[which], preferred_element_type=jnp.float32).astype(jnp.bfloat16)
            for h in range(3):
                piece = result[:, h * 128 : (h + 1) * 128]
                if which == 0:
                    query[h, frame * half : (frame + 1) * half, :] = piece
                else:
                    kv[which - 1, h, frame * half : (frame + 1) * half, :] = piece


def attend_kernel(allowed, query, lower2, lower1, own, upper1, upper2, out, scores):
    head = pl.program_id(0)
    size = query.shape[2]
    tokf = query.shape[1] // 2
    factor = LOG2E / size**0.5
    frames = [(ref, f) for ref in (lower2, lower1, own, upper1, upper2) for f in range(2)]
    ones = jnp.ones((tokf, size), jnp.bfloat16)
    for f in range(2):
        q = query[0, f * tokf : (f + 1) * tokf, :]
        seen = [allowed[(head * 2 + f) * 9 + d] > 0 for d in range(9)]
        top = jnp.full((tokf, size), -BIG, jnp.float32)
        for d in range(9):
            ref, g = frames[f + d]
            k = ref[0, 0, g * tokf : (g + 1) * tokf, :]
            s = lax.dot_general(q, k, (((1,), (1,)), ((), ())), preferred_element_type=jnp.float32)
            scores[d] = s
            top = jnp.maximum(top, jnp.where(seen[d], jnp.maximum(s[:, :size], s[:, size:]), -BIG))
        largest = jnp.max(top, axis=1, keepdims=True) * factor
        total = jnp.zeros((tokf, 2 * size), jnp.float32)
        for d in range(9):
            ref, g = frames[f + d]
            v = jnp.concatenate([ref[1, 0, g * tokf : (g + 1) * tokf, :], ones], axis=1)
            base = jnp.where(seen[d], largest, BIG)
            weights = jnp.exp2(scores[d] * factor - base).astype(jnp.bfloat16)
            total = total + jnp.dot(weights, v, preferred_element_type=jnp.float32)
        out[f * tokf : (f + 1) * tokf, :] = (total[:, :size] / total[:, size:]).astype(jnp.bfloat16)


def project_kernel(slots, place, attended, weight, *outs):
    part = attended.shape[1]
    left = attended[...]
    for out, slot in zip(outs, slots):
        columns = pl.ds(pl.multiple_of(place[slot] * part, 128), part)
        out[...] = jnp.dot(left, weight[:, columns], preferred_element_type=jnp.float32).astype(jnp.bfloat16)


def project(place, attended, weight, slots):
    rows, part = attended.shape
    return pl.pallas_call(
        functools.partial(project_kernel, slots),
        out_shape=[jax.ShapeDtypeStruct((rows, part), jnp.bfloat16)] * len(slots),
        in_specs=[smem(), vmem(), vmem()],
        out_specs=[vmem()] * len(slots),
        compiler_params=pltpu.CompilerParams(vmem_limit_bytes=VMEM_LIMIT),
        cost_estimate=pl.CostEstimate(
            flops=2 * rows * part * part * len(slots), bytes_accessed=2 * part * (rows + part) * len(slots), transcendentals=0
        ),
    )(place, attended, weight)


def on_device(latents, step_index, head_index, band, mod_table, gate_table, qkv_weight, out_weight):
    rows, part = latents.shape
    frames = step_index.shape[0]
    tokf = rows // frames
    width = mod_table.shape[2]
    heads = band.shape[0]
    size = part // heads
    count = lax.axis_size("queue")
    me = lax.axis_index("queue")
    member = lax.axis_index("mp")
    frames_all = frames * count
    half = rows // 2
    x, y = member % 4, member // 4
    place = jnp.stack([yy * 4 + xx for yy, xx in (
        (y, x), (1 - y, x), (y, (x + 3) % 4), (y, (x + 1) % 4),
        (y, (x + 2) % 4), (1 - y, (x + 3) % 4), (1 - y, (x + 1) % 4), (1 - y, (x + 2) % 4),
    )]).astype(jnp.int32)

    cuts = (0, 176, 336, rows)
    far, low, high = across(latents), ring(latents, 1), ring(latents, -1)
    two_a = ring(jnp.concatenate([low[:half], far[:half]]), 1)
    two_b = ring(jnp.concatenate([high[half:], far[half:]]), -1)
    two_c = across(jnp.concatenate([low[half:], high[:half]]))
    far_low_top, far_low_bottom = two_a[half:], two_c[:half]
    far_high_top, far_high_bottom = two_c[half:], two_b[half:]
    three_a = ring(far_low_top[: cuts[1]], 1)
    three_b = across(jnp.concatenate([two_a[cuts[1] : half], two_b[: cuts[2] - half]]))
    three_c = ring(far_high_bottom[cuts[2] - half :], -1)

    modul = jnp.stack([lax.dynamic_index_in_dim(mod_table, step_index[f] - 1, 0, keepdims=False) for f in range(frames)])
    query, kv = pl.pallas_call(
        qkv_kernel,
        out_shape=[
            jax.ShapeDtypeStruct((heads, rows, size), jnp.bfloat16),
            jax.ShapeDtypeStruct((2, heads, rows, size), jnp.bfloat16),
        ],
        in_specs=[smem()] + [vmem()] * 12,
        out_specs=[vmem()] * 2,
        scratch_shapes=[pltpu.VMEM((rows, part), jnp.bfloat16), pltpu.VMEM((rows, width), jnp.bfloat16)],
        compiler_params=pltpu.CompilerParams(vmem_limit_bytes=VMEM_LIMIT),
        cost_estimate=pl.CostEstimate(flops=6 * rows * width * part, bytes_accessed=6 * width * part, transcendentals=0),
    )(place, latents, far, low, high, two_a, two_b, two_c, three_a, three_b, three_c, modul, qkv_weight)

    lower2, upper2 = shifted(kv, 2), shifted(kv, -2)
    partner = flipped(kv, 1)
    odd = me % 2 == 1
    passed = flipped(jnp.where(odd, lower2, upper2), 1)
    lower1 = jnp.where(odd, partner, passed)
    upper1 = jnp.where(odd, passed, partner)

    head = head_index[0]
    position = jnp.mod(me * frames + jnp.arange(frames, dtype=jnp.int32) - head, frames_all)
    offset = jnp.arange(-4, 5, dtype=jnp.int32)
    other = position[:, None] + offset[None, :]
    inside = (other >= 0) & (other < frames_all)
    near = jnp.abs(offset)[None, :] <= band[:, None]
    allowed = (inside[None, :, :] & near[:, None, :]).astype(jnp.int32).reshape(-1)

    block = pl.BlockSpec((2, 1, rows, size), lambda h: (0, h, 0, 0))
    attended = pl.pallas_call(
        attend_kernel,
        grid=(heads,),
        out_shape=jax.ShapeDtypeStruct((rows, part), jnp.bfloat16),
        in_specs=[smem(), pl.BlockSpec((1, rows, size), lambda h: (h, 0, 0))] + [block] * 5,
        out_specs=pl.BlockSpec((rows, size), lambda h: (0, h)),
        scratch_shapes=[pltpu.VMEM((9, tokf, tokf), jnp.float32)],
        compiler_params=pltpu.CompilerParams(vmem_limit_bytes=VMEM_LIMIT),
        cost_estimate=pl.CostEstimate(
            flops=8 * heads * rows * 9 * tokf * size, bytes_accessed=24 * heads * rows * size, transcendentals=heads * rows * 9 * tokf
        ),
    )(allowed, query, lower2, lower1, kv, upper1, upper2)

    (opp_far,) = project(place, attended, out_weight, (7,))
    to_low = ring(opp_far[: cuts[1]], -1)
    to_far = across(opp_far[cuts[1] : cuts[2]])
    to_high = ring(opp_far[cuts[2] :], 1)
    p_opp, p_far_low, p_far_high = project(place, attended, out_weight, (4, 5, 6))

    def added(*terms):
        total = terms[0].astype(jnp.float32)
        for term in terms[1:]:
            total = total + term.astype(jnp.float32)
        return total

    bf = jnp.bfloat16
    far_low_top = jnp.concatenate([added(p_far_low[: cuts[1]], to_low).astype(bf), p_far_low[cuts[1] : half]])
    far_high_bottom = jnp.concatenate([p_far_high[half : cuts[2]], added(p_far_high[cuts[2] :], to_high).astype(bf)])
    opp_top = jnp.concatenate([p_opp[: cuts[1]], added(p_opp[cuts[1] : half], to_far[: half - cuts[1]]).astype(bf)])
    opp_bottom = jnp.concatenate([added(p_opp[half : cuts[2]], to_far[half - cuts[1] :]).astype(bf), p_opp[cuts[2] :]])
    got_a = ring(jnp.concatenate([opp_top, far_low_top]), -1)
    got_b = ring(jnp.concatenate([opp_bottom, far_high_bottom]), 1)
    got_c = across(jnp.concatenate([p_far_low[half:], p_far_high[:half]]))
    p_own, p_far, p_low, p_high = project(place, attended, out_weight, (0, 1, 2, 3))
    sum_low = jnp.concatenate([added(p_low[:half], got_a[:half]), added(p_low[half:], got_c[:half])]).astype(bf)
    sum_high = jnp.concatenate([added(p_high[:half], got_c[half:]), added(p_high[half:], got_b[:half])]).astype(bf)
    sum_far = jnp.concatenate([added(p_far[:half], got_a[half:]), added(p_far[half:], got_b[half:])]).astype(bf)
    projected = added(p_own, across(sum_far), ring(sum_low, -1), ring(sum_high, 1))

    gate = jnp.stack([lax.dynamic_index_in_dim(gate_table, step_index[f] - 1, 0, keepdims=False) for f in range(frames)])
    own_latent = latents.astype(jnp.float32).reshape(frames, tokf, part)
    velocity = (own_latent + gate.astype(jnp.float32)[:, None, :] * projected.reshape(frames, tokf, part)).astype(bf)

    level = step_index.astype(jnp.float32) / STEPS
    sigma = 3.0 * level / (1.0 + 2.0 * level)
    owner = head // frames
    local_frame = jnp.mod(head, frames)
    head_latent = lax.dynamic_index_in_dim(own_latent, local_frame, 0, keepdims=False)
    head_velocity = lax.dynamic_index_in_dim(velocity, local_frame, 0, keepdims=False).astype(jnp.float32)
    head_sigma = lax.dynamic_index_in_dim(sigma, local_frame, 0, keepdims=False)
    held = (head_latent - head_sigma * head_velocity).astype(bf)
    holder = owner
    bit = count // 2
    while bit:
        n = held.shape[0] // 2
        side = (me & bit) != 0
        mine = jnp.where(side, held[n:], held[:n])
        got = flipped(jnp.where(side, held[:n], held[n:]), bit)
        held = jnp.where((holder & bit) == (me & bit), mine, got)
        bit //= 2
    return (velocity.reshape(rows, part), held)


def solution(mesh):
    placed = (
        P("queue", "mp"),
        P("queue"),
        P(),
        P("mp"),
        P(),
        P(None, "mp"),
        P(None, None, "mp"),
        P("mp", None),
    )
    return jax.shard_map(
        on_device,
        mesh=mesh,
        in_specs=placed,
        out_specs=(P("queue", "mp"), P("queue", "mp")),
        check_vma=False,
    )
```

time: 468 us -> 161 us (0.34)
  the two profiles are of different devices: /device:TPU:6 before, /device:TPU:1 now
where the time goes in v1:
time: 161 us; the launch traced here: 160 us
  waiting for transfers between devices  66.2 us (41%)
  starting transfers between devices  50.9 us (32%)
  Pallas kernels  23.1 us (14%)
  local copies, waits for them, and re-layouts  8.35 us (5%)
  other arithmetic  7.37 us (5%)
  between operations  4.42 us (3%)
    ppermute x7, waiting for transfers between devices, flipped(): lax.ppermute(value, 'queue', [(s, s ^ bit) for s in range(lax.axis_size('...  20.6 us
    ppermute x12, starting transfers between devices, ring(): lax.ppermute(value, 'mp', [(s, s // 4 * 4 + (s + distance) % 4) for s in...  19.2 us
    ppermute x7, starting transfers between devices, flipped(): lax.ppermute(value, 'queue', [(s, s ^ bit) for s in range(lax.axis_size('...  17.3 us
    ppermute x12, waiting for transfers between devices, ring(): lax.ppermute(value, 'mp', [(s, s // 4 * 4 + (s + distance) % 4) for s in...  17.1 us
    ppermute x6, waiting for transfers between devices, across(): return lax.ppermute(value, 'mp', [(s, s ^ 4) for s in range(8)])  14.3 us
    ppermute x2, waiting for transfers between devices, shifted(): lax.ppermute(value, 'queue', [(s, (s + distance) % count) for s in range(...  14.2 us
    pallas_call x1, Pallas kernels, on_device(): pl.pallas_call(qkv_kernel, out_shape=[jax.ShapeDtypeStruct((heads, rows,...  11.3 us
    ppermute x2, starting transfers between devices, shifted(): lax.ppermute(value, 'queue', [(s, (s + distance) % count) for s in range(...  7.91 us
  transfers between devices with their start and end apart: 27, of which 19 were waited for; matrix products, arithmetic and copies ran while one was open for 4% of the time, Pallas kernels for 1%

profile of v1, /device:TPU:1, one launch (start us, length us, event | category | flops | bytes accessed | tf_op | source)
XLA Modules:
  0.0 160.2 jit_solution(9770834264081520306)
XLA Ops:
  0.6 2.1 %collective-permute-start.1 = (bf16[512,384]{1,0:T(8,128)(2,1)}, bf16[512,384]{1,0:T(8,128)(2,1)S(1)}, u32[]{:S(2)}, u32[]{:S(2)}) collective-permute-start(bf16[512,384]{1,0:T(8,128)(2,1)} %own.1), channel_id=1, source_target_pairs={{0,1},{1,2},{2,3},{3,0},{4,5},{5,6},{6,7},{7,4},{8,9},{9,10},{10,1... | collective-permute-start | bytes 1179656 | tf_op jit(solution)/shard_map/ppermute | solution.py:18
  2.7 1.3 collective-permute-start
  4.0 1.5 collective-permute-start.2
  5.5 1.3 fusion.11
  9.4 1.4 collective-permute-done.1.low
  10.8 1.4 collective-permute-done.far
  12.4 1.7 %collective-permute-start.3 = (bf16[512,384]{1,0:T(8,128)(2,1)S(1)}, bf16[512,384]{1,0:T(8,128)(2,1)S(1)}, u32[]{:S(2)}, u32[]{:S(2)}) collective-permute-start(bf16[512,384]{1,0:T(8,128)(2,1)S(1)} %pad_maximum_fusion), channel_id=1, source_target_pairs={{0,1},{1,2},{2,3},{3,0},{4,5},{5,6},{6,7},{7,4},{8,9},{9,10},{10,1... | collective-permute-start | bytes 1179656 | tf_op jit(solution)/shard_map/ppermute | solution.py:18
  14.1 2.2 %collective-permute-start.4 = (bf16[512,384]{1,0:T(8,128)(2,1)S(1)}, bf16[512,384]{1,0:T(8,128)(2,1)S(1)}, u32[]{:S(2)}, u32[]{:S(2)}) collective-permute-start(bf16[512,384]{1,0:T(8,128)(2,1)S(1)} %pad_maximum_fusion.1), channel_id=1, source_target_pairs={{0,3},{1,0},{2,1},{3,2},{4,7},{5,4},{6,5},{7,6},{8,11},{9,8},{10,9... | collective-permute-start | bytes 1179656 | tf_op jit(solution)/shard_map/ppermute | solution.py:18
  16.3 0.7 constant_dynamic-slice_fusion.2
  17.1 1.1 collective-permute-start.5
  18.2 3.8 %collective-permute-done.3.two_a = bf16[512,384]{1,0:T(8,128)(2,1)S(1)} collective-permute-done((bf16[512,384]{1,0:T(8,128)(2,1)S(1)}, bf16[512,384]{1,0:T(8,128)(2,1)S(1)}, u32[]{:S(2)}, u32[]{:S(2)}) %collective-permute-start.3) | collective-permute-done | bytes 393248 | tf_op jit(solution)/shard_map/ppermute | solution.py:18
  23.3 2.1 %collective-permute-start.7 = (bf16[160,384]{1,0:T(8,128)(2,1)}, bf16[160,384]{1,0:T(8,128)(2,1)S(1)}, u32[]{:S(2)}, u32[]{:S(2)}) collective-permute-start(bf16[160,384]{1,0:T(8,128)(2,1)} %pad_maximum_fusion.9), channel_id=1, source_target_pairs={{0,4},{1,5},{2,6},{3,7},{4,0},{5,1},{6,2},{7,3},{8,12},{9,13},{10,... | collective-permute-start | bytes 368648 | tf_op jit(solution)/shard_map/ppermute | solution.py:22
  25.6 2.8 %collective-permute-start.8 = (bf16[176,384]{1,0:T(8,128)(2,1)S(1)}, bf16[176,384]{1,0:T(8,128)(2,1)S(1)}, u32[]{:S(2)}, u32[]{:S(2)}) collective-permute-start(bf16[176,384]{1,0:T(8,128)(2,1)S(1)} %slice.229), channel_id=1, source_target_pairs={{0,3},{1,0},{2,1},{3,2},{4,7},{5,4},{6,5},{7,6},{8,11},{9,8},{10,9... | collective-permute-start | bytes 405512 | tf_op jit(solution)/shard_map/ppermute | solution.py:18
  28.7 0.9 collective-permute-done.7.three_b
  30.6 1.0 copy-done.1
  31.6 0.9 copy-done.4
  32.5 11.3 %shard_map.95 = (bf16[3,512,128]{2,1,0:T(8,128)(2,1)S(1)}, bf16[2,3,512,128]{3,2,1,0:T(8,128)(2,1)S(1)}) custom-call(s32[8]{0:T(128)S(1)} %stack.46.place, bf16[512,384]{1,0:T(8,128)(2,1)S(1)} %copy-done.1, bf16[512,384]{1,0:T(8,128)(2,1)S(1)} %collective-permute-done.far, bf16[512,384]{1,0:T(8,128)(2,1)S(1)} %collective-permute-done.1.low, ...), custom_call_target="tpu_custom_call" | custom-call | flops 3623878656 | bytes 7077888 | tf_op jit(solution)/shard_map/pallas_call | solution.py:168
  44.5 7.9 %collective-permute-start.11 = (bf16[2,3,512,128]{3,2,1,0:T(8,128)(2,1)S(1)}, bf16[2,3,512,128]{3,2,1,0:T(8,128)(2,1)S(1)}, u32[]{:S(2)}, u32[]{:S(2)}) collective-permute-start(bf16[2,3,512,128]{3,2,1,0:T(8,128)(2,1)S(1)} %get-tuple-element.12.own), channel_id=1, source_target_pairs={{0,240},{8,248},{16,0},{24,8},{32,16},{40,24},{48,32},{56,40},{64,... | collective-permute-start | bytes 2359304 | tf_op jit(solution)/shard_map/ppermute | solution.py:27
  52.4 4.2 %collective-permute-start.10 = (bf16[2,3,512,128]{3,2,1,0:T(8,128)(2,1)S(1)}, bf16[2,3,512,128]{3,2,1,0:T(8,128)(2,1)}, u32[]{:S(2)}, u32[]{:S(2)}) collective-permute-start(bf16[2,3,512,128]{3,2,1,0:T(8,128)(2,1)S(1)} %get-tuple-element.12.own), channel_id=1, source_target_pairs={{0,8},{8,0},{16,24},{24,16},{32,40},{40,32},{48,56},{56,48},{64,72... | collective-permute-start | bytes 2359304 | tf_op jit(solution)/shard_map/ppermute | solution.py:31
  56.7 8.7 %collective-permute-done.11.upper2 = bf16[2,3,512,128]{3,2,1,0:T(8,128)(2,1)S(1)} collective-permute-done((bf16[2,3,512,128]{3,2,1,0:T(8,128)(2,1)S(1)}, bf16[2,3,512,128]{3,2,1,0:T(8,128)(2,1)S(1)}, u32[]{:S(2)}, u32[]{:S(2)}) %collective-permute-start.11) | collective-permute-done | bytes 786464 | tf_op jit(solution)/shard_map/ppermute | solution.py:27
  65.3 5.5 %collective-permute-done.9.lower2 = bf16[2,3,512,128]{3,2,1,0:T(8,128)(2,1)S(1)} collective-permute-done((bf16[2,3,512,128]{3,2,1,0:T(8,128)(2,1)S(1)}, bf16[2,3,512,128]{3,2,1,0:T(8,128)(2,1)S(1)}, u32[]{:S(2)}, u32[]{:S(2)}) %collective-permute-start.9) | collective-permute-done | bytes 786464 | tf_op jit(solution)/shard_map/ppermute | solution.py:27
  70.9 1.0 broadcast_select_fusion.2
  71.9 5.1 %collective-permute-start.12 = (bf16[2,3,512,128]{3,2,1,0:T(8,128)(2,1)}, bf16[2,3,512,128]{3,2,1,0:T(8,128)(2,1)}, u32[]{:S(2)}, u32[]{:S(2)}) collective-permute-start(bf16[2,3,512,128]{3,2,1,0:T(8,128)(2,1)} %broadcast_select_fusion.2), channel_id=1, source_target_pairs={{0,8},{8,0},{16,24},{24,16},{32,40},{40,32},{48,56},{56,48},{64,72... | collective-permute-start | bytes 2359304 | tf_op jit(solution)/shard_map/ppermute | solution.py:31
  77.9 1.3 collective-permute-done.12
  79.2 1.5 broadcast_select_fusion
  80.7 1.1 copy-done.6
  81.9 7.8 %shard_map.96.attended = bf16[512,384]{1,0:T(8,128)(2,1)S(1)} custom-call(s32[54]{0:T(128)S(1)} %reshape.126.allowed, bf16[3,512,128]{2,1,0:T(8,128)(2,1)S(1)} %copy-done.6, bf16[2,3,512,128]{3,2,1,0:T(8,128)(2,1)S(1)} %collective-permute-done.9.lower2, bf16[2,3,512,128]{3,2,1,0:T(8,128)(2,1)S(1)} %get-tuple-element.23.lower1, ...), custom_call_target="tpu_custom_call" | custom-call | flops 3623878656 | bytes 4718592 | tf_op jit(solution)/shard_map/pallas_call | solution.py:197
  89.7 1.4 shard_map.98
  91.1 0.9 shard_map.99
  92.4 1.4 collective-permute-start.16
  93.7 1.4 collective-permute-start.13
  95.1 1.7 %collective-permute-start.14 = (bf16[176,384]{1,0:T(8,128)(2,1)S(1)}, bf16[176,384]{1,0:T(8,128)(2,1)S(1)}, u32[]{:S(2)}, u32[]{:S(2)}) collective-permute-start(bf16[176,384]{1,0:T(8,128)(2,1)S(1)} %get-tuple-element.36), channel_id=1, source_target_pairs={{0,3},{1,0},{2,1},{3,2},{4,7},{5,4},{6,5},{7,6},{8,11},{9,8},{10,9... | collective-permute-start | bytes 405512 | tf_op jit(solution)/shard_map/ppermute | solution.py:18
  96.8 8.5 %collective-permute-done.13 = bf16[160,384]{1,0:T(8,128)(2,1)S(1)} collective-permute-done((bf16[160,384]{1,0:T(8,128)(2,1)S(1)}, bf16[160,384]{1,0:T(8,128)(2,1)S(1)}, u32[]{:S(2)}, u32[]{:S(2)}) %collective-permute-start.13) | collective-permute-done | bytes 122912 | tf_op jit(solution)/shard_map/ppermute | solution.py:22
  105.5 1.4 collective-permute-start.17
  106.9 1.8 %collective-permute-start.15 = (bf16[512,384]{1,0:T(8,128)(2,1)S(1)}, bf16[512,384]{1,0:T(8,128)(2,1)S(1)}, u32[]{:S(2)}, u32[]{:S(2)}) collective-permute-start(bf16[512,384]{1,0:T(8,128)(2,1)S(1)} %pad_maximum_fusion.3), channel_id=1, source_target_pairs={{0,3},{1,0},{2,1},{3,2},{4,7},{5,4},{6,5},{7,6},{8,11},{9,8},{10,9... | collective-permute-start | bytes 1179656 | tf_op jit(solution)/shard_map/ppermute | solution.py:18
  108.7 1.7 %shard_map.97 = (bf16[512,384]{1,0:T(8,128)(2,1)S(1)}, bf16[512,384]{1,0:T(8,128)(2,1)S(1)}, bf16[512,384]{1,0:T(8,128)(2,1)S(1)}, bf16[512,384]{1,0:T(8,128)(2,1)S(1)}) custom-call(s32[8]{0:T(128)S(1)} %stack.46.place, bf16[512,384]{1,0:T(8,128)(2,1)S(1)} %shard_map.96.attended, bf16[384,3072]{1,0:T(8,128)(2,1)S(1)} %copy-done), custom_call_target="tpu_custom_call" | custom-call | flops 603979776 | bytes 2752512 | tf_op jit(solution)/shard_map/pallas_call | solution.py:126
  110.4 6.4 %collective-permute-done.17 = bf16[512,384]{1,0:T(8,128)(2,1)S(1)} collective-permute-done((bf16[512,384]{1,0:T(8,128)(2,1)S(1)}, bf16[512,384]{1,0:T(8,128)(2,1)S(1)}, u32[]{:S(2)}, u32[]{:S(2)}) %collective-permute-start.17) | collective-permute-done | bytes 393248 | tf_op jit(solution)/shard_map/ppermute | solution.py:18
  117.6 2.6 %collective-permute-start.20 = (bf16[512,384]{1,0:T(8,128)(2,1)S(1)}, bf16[512,384]{1,0:T(8,128)(2,1)S(1)}, u32[]{:S(2)}, u32[]{:S(2)}) collective-permute-start(bf16[512,384]{1,0:T(8,128)(2,1)S(1)} %pad_maximum_fusion.7), channel_id=1, source_target_pairs={{0,3},{1,0},{2,1},{3,2},{4,7},{5,4},{6,5},{7,6},{8,11},{9,8},{10,9... | collective-permute-start | bytes 1179656 | tf_op jit(solution)/shard_map/ppermute | solution.py:18
  120.2 0.8 pad_maximum_fusion.8
  122.5 3.4 %collective-permute-done.18 = bf16[512,384]{1,0:T(8,128)(2,1)S(1)} collective-permute-done((bf16[512,384]{1,0:T(8,128)(2,1)S(1)}, bf16[512,384]{1,0:T(8,128)(2,1)S(1)}, u32[]{:S(2)}, u32[]{:S(2)}) %collective-permute-start.18) | collective-permute-done | bytes 393248 | tf_op jit(solution)/shard_map/ppermute | solution.py:22
  126.4 4.1 %collective-permute-done.21 = bf16[512,384]{1,0:T(8,128)(2,1)S(1)} collective-permute-done((bf16[512,384]{1,0:T(8,128)(2,1)}, bf16[512,384]{1,0:T(8,128)(2,1)S(1)}, u32[]{:S(2)}, u32[]{:S(2)}) %collective-permute-start.21) | collective-permute-done | bytes 393248 | tf_op jit(solution)/shard_map/ppermute | solution.py:18
  130.5 1.0 fusion.1
  132.5 4.9 %collective-permute-done.22 = bf16[128,384]{1,0:T(8,128)(2,1)S(1)} collective-permute-done((bf16[128,384]{1,0:T(8,128)(2,1)S(1)}, bf16[128,384]{1,0:T(8,128)(2,1)S(1)}, u32[]{:S(2)}, u32[]{:S(2)}) %collective-permute-start.22) | collective-permute-done | bytes 98336 | tf_op jit(solution)/shard_map/ppermute | solution.py:31
  137.5 7.2 %collective-permute-done.23 = bf16[64,384]{1,0:T(8,128)(2,1)S(1)} collective-permute-done((bf16[64,384]{1,0:T(8,128)(2,1)S(1)}, bf16[64,384]{1,0:T(8,128)(2,1)S(1)}, u32[]{:S(2)}, u32[]{:S(2)}) %collective-permute-start.23) | collective-permute-done | bytes 49184 | tf_op jit(solution)/shard_map/ppermute | solution.py:31
  144.8 3.8 %collective-permute-done.24 = bf16[32,384]{1,0:T(8,128)(2,1)S(1)} collective-permute-done((bf16[32,384]{1,0:T(8,128)(2,1)S(1)}, bf16[32,384]{1,0:T(8,128)(2,1)S(1)}, u32[]{:S(2)}, u32[]{:S(2)}) %collective-permute-start.24) | collective-permute-done | bytes 24608 | tf_op jit(solution)/shard_map/ppermute | solution.py:31
  148.8 2.5 %collective-permute-done.25 = bf16[16,384]{1,0:T(8,128)(2,1)S(1)} collective-permute-done((bf16[16,384]{1,0:T(8,128)(2,1)S(1)}, bf16[16,384]{1,0:T(8,128)(2,1)S(1)}, u32[]{:S(2)}, u32[]{:S(2)}) %collective-permute-start.25) | collective-permute-done | bytes 12320 | tf_op jit(solution)/shard_map/ppermute | solution.py:31
  151.3 7.5 %collective-permute-start.26 = (bf16[8,384]{1,0:T(8,128)(2,1)S(1)}, bf16[8,384]{1,0:T(8,128)(2,1)S(1)}, u32[]{:S(2)}, u32[]{:S(2)}) collective-permute-start(bf16[8,384]{1,0:T(8,128)(2,1)S(1)} %broadcast_select_fusion.6), channel_id=1, source_target_pairs={{0,8},{8,0},{16,24},{24,16},{32,40},{40,32},{48,56},{56,48},{64,72... | collective-permute-start | bytes 18440 | tf_op jit(solution)/shard_map/ppermute | solution.py:31
  158.8 0.8 collective-permute-done.26
  (88 shorter events, 9.0 us)
Async XLA Ops:
  0.6 10.1 %collective-permute-start.1 = (bf16[512,384]{1,0:T(8,128)(2,1)}, bf16[512,384]{1,0:T(8,128)(2,1)S(1)}, u32[]{:S(2)}, u32[]{:S(2)}) collective-permute-start(bf16[512,384]{1,0:T(8,128)(2,1)} %own.1), channel_id=1, source_target_pairs={{0,1},{1,2},{2,3},{3,0},{4,5},{5,6},{6,7},{7,4},{8,9},{9,10},{10,1... | collective-permute-start | bytes 1179656 | tf_op jit(solution)/shard_map/ppermute | solution.py:18
  2.7 9.5 %collective-permute-start = (bf16[512,384]{1,0:T(8,128)(2,1)}, bf16[512,384]{1,0:T(8,128)(2,1)S(1)}, u32[]{:S(2)}, u32[]{:S(2)}) collective-permute-start(bf16[512,384]{1,0:T(8,128)(2,1)} %own.1), channel_id=1, source_target_pairs={{0,4},{1,5},{2,6},{3,7},{4,0},{5,1},{6,2},{7,3},{8,12},{9,13},{10,... | collective-permute-start | bytes 1179656 | tf_op jit(solution)/shard_map/ppermute | solution.py:22
  4.0 10.0 %collective-permute-start.2 = (bf16[512,384]{1,0:T(8,128)(2,1)}, bf16[512,384]{1,0:T(8,128)(2,1)S(1)}, u32[]{:S(2)}, u32[]{:S(2)}) collective-permute-start(bf16[512,384]{1,0:T(8,128)(2,1)} %own.1), channel_id=1, source_target_pairs={{0,3},{1,0},{2,1},{3,2},{4,7},{5,4},{6,5},{7,6},{8,11},{9,8},{10,9... | collective-permute-start | bytes 1179656 | tf_op jit(solution)/shard_map/ppermute | solution.py:18
  12.4 9.7 %collective-permute-start.3 = (bf16[512,384]{1,0:T(8,128)(2,1)S(1)}, bf16[512,384]{1,0:T(8,128)(2,1)S(1)}, u32[]{:S(2)}, u32[]{:S(2)}) collective-permute-start(bf16[512,384]{1,0:T(8,128)(2,1)S(1)} %pad_maximum_fusion), channel_id=1, source_target_pairs={{0,1},{1,2},{2,3},{3,0},{4,5},{5,6},{6,7},{7,4},{8,9},{9,10},{10,1... | collective-permute-start | bytes 1179656 | tf_op jit(solution)/shard_map/ppermute | solution.py:18
  14.1 8.5 %collective-permute-start.4 = (bf16[512,384]{1,0:T(8,128)(2,1)S(1)}, bf16[512,384]{1,0:T(8,128)(2,1)S(1)}, u32[]{:S(2)}, u32[]{:S(2)}) collective-permute-start(bf16[512,384]{1,0:T(8,128)(2,1)S(1)} %pad_maximum_fusion.1), channel_id=1, source_target_pairs={{0,3},{1,0},{2,1},{3,2},{4,7},{5,4},{6,5},{7,6},{8,11},{9,8},{10,9... | collective-permute-start | bytes 1179656 | tf_op jit(solution)/shard_map/ppermute | solution.py:18
  17.1 11.6 %collective-permute-start.5 = (bf16[512,384]{1,0:T(8,128)(2,1)S(1)}, bf16[512,384]{1,0:T(8,128)(2,1)S(1)}, u32[]{:S(2)}, u32[]{:S(2)}) collective-permute-start(bf16[512,384]{1,0:T(8,128)(2,1)S(1)} %pad_maximum_fusion.2), channel_id=1, source_target_pairs={{0,4},{1,5},{2,6},{3,7},{4,0},{5,1},{6,2},{7,3},{8,12},{9,13},{10,... | collective-permute-start | bytes 1179656 | tf_op jit(solution)/shard_map/ppermute | solution.py:22
  23.3 6.3 %collective-permute-start.7 = (bf16[160,384]{1,0:T(8,128)(2,1)}, bf16[160,384]{1,0:T(8,128)(2,1)S(1)}, u32[]{:S(2)}, u32[]{:S(2)}) collective-permute-start(bf16[160,384]{1,0:T(8,128)(2,1)} %pad_maximum_fusion.9), channel_id=1, source_target_pairs={{0,4},{1,5},{2,6},{3,7},{4,0},{5,1},{6,2},{7,3},{8,12},{9,13},{10,... | collective-permute-start | bytes 368648 | tf_op jit(solution)/shard_map/ppermute | solution.py:22
  25.4 5.2 %collective-permute-start.6 = (bf16[176,384]{1,0:T(8,128)(2,1)S(1)}, bf16[176,384]{1,0:T(8,128)(2,1)S(1)}, u32[]{:S(2)}, u32[]{:S(2)}) collective-permute-start(bf16[176,384]{1,0:T(8,128)(2,1)S(1)} %slice.226), channel_id=1, source_target_pairs={{0,1},{1,2},{2,3},{3,0},{4,5},{5,6},{6,7},{7,4},{8,9},{9,10},{10,1... | collective-permute-start | bytes 405512 | tf_op jit(solution)/shard_map/ppermute | solution.py:18
  25.6 5.0 %collective-permute-start.8 = (bf16[176,384]{1,0:T(8,128)(2,1)S(1)}, bf16[176,384]{1,0:T(8,128)(2,1)S(1)}, u32[]{:S(2)}, u32[]{:S(2)}) collective-permute-start(bf16[176,384]{1,0:T(8,128)(2,1)S(1)} %slice.229), channel_id=1, source_target_pairs={{0,3},{1,0},{2,1},{3,2},{4,7},{5,4},{6,5},{7,6},{8,11},{9,8},{10,9... | collective-permute-start | bytes 405512 | tf_op jit(solution)/shard_map/ppermute | solution.py:18
  28.6 49.1 %copy-start.8 = (s32[3]{0:T(128)S(1)}, s32[3]{0:T(128)}, u32[]{:S(2)}) copy-start(s32[3]{0:T(128)} %param.11) | copy-start | bytes 40
  29.6 0.6 copy-start.3
  30.6 1.0 copy-start.1
  31.6 0.9 copy-start.4
  43.8 0.7 copy-start.5
  44.5 20.8 %collective-permute-start.11 = (bf16[2,3,512,128]{3,2,1,0:T(8,128)(2,1)S(1)}, bf16[2,3,512,128]{3,2,1,0:T(8,128)(2,1)S(1)}, u32[]{:S(2)}, u32[]{:S(2)}) collective-permute-start(bf16[2,3,512,128]{3,2,1,0:T(8,128)(2,1)S(1)} %get-tuple-element.12.own), channel_id=1, source_target_pairs={{0,240},{8,248},{16,0},{24,8},{32,16},{40,24},{48,32},{56,40},{64,... | collective-permute-start | bytes 2359304 | tf_op jit(solution)/shard_map/ppermute | solution.py:27
  52.4 18.4 %collective-permute-start.9 = (bf16[2,3,512,128]{3,2,1,0:T(8,128)(2,1)S(1)}, bf16[2,3,512,128]{3,2,1,0:T(8,128)(2,1)S(1)}, u32[]{:S(2)}, u32[]{:S(2)}) collective-permute-start(bf16[2,3,512,128]{3,2,1,0:T(8,128)(2,1)S(1)} %get-tuple-element.12.own), channel_id=1, source_target_pairs={{0,16},{8,24},{16,32},{24,40},{32,48},{40,56},{48,64},{56,72},{64,... | collective-permute-start | bytes 2359304 | tf_op jit(solution)/shard_map/ppermute | solution.py:27
  52.4 25.5 %collective-permute-start.10 = (bf16[2,3,512,128]{3,2,1,0:T(8,128)(2,1)S(1)}, bf16[2,3,512,128]{3,2,1,0:T(8,128)(2,1)}, u32[]{:S(2)}, u32[]{:S(2)}) collective-permute-start(bf16[2,3,512,128]{3,2,1,0:T(8,128)(2,1)S(1)} %get-tuple-element.12.own), channel_id=1, source_target_pairs={{0,8},{8,0},{16,24},{24,16},{32,40},{40,32},{48,56},{56,48},{64,72... | collective-permute-start | bytes 2359304 | tf_op jit(solution)/shard_map/ppermute | solution.py:31
  71.9 7.4 %collective-permute-start.12 = (bf16[2,3,512,128]{3,2,1,0:T(8,128)(2,1)}, bf16[2,3,512,128]{3,2,1,0:T(8,128)(2,1)}, u32[]{:S(2)}, u32[]{:S(2)}) collective-permute-start(bf16[2,3,512,128]{3,2,1,0:T(8,128)(2,1)} %broadcast_select_fusion.2), channel_id=1, source_target_pairs={{0,8},{8,0},{16,24},{24,16},{32,40},{40,32},{48,56},{56,48},{64,72... | collective-permute-start | bytes 2359304 | tf_op jit(solution)/shard_map/ppermute | solution.py:31
  80.7 9.0 %copy-start = (bf16[384,3072]{1,0:T(8,128)(2,1)S(1)}, bf16[384,3072]{1,0:T(8,128)(2,1)}, u32[]{:S(2)}) copy-start(bf16[384,3072]{1,0:T(8,128)(2,1)} %weight.7) | copy-start | bytes 7077892
  80.7 1.1 copy-start.6
  92.1 29.0 %copy-start.7 = (s32[2]{0:T(128)S(1)}, s32[2]{0:T(128)}, u32[]{:S(2)}) copy-start(s32[2]{0:T(128)} %param.9) | copy-start | bytes 28
  92.1 29.0 %copy-start.2 = (bf16[512,384]{1,0:T(8,128)(2,1)S(1)}, bf16[512,384]{1,0:T(8,128)(2,1)}, u32[]{:S(2)}) copy-start(bf16[512,384]{1,0:T(8,128)(2,1)} %own.1) | copy-start | bytes 1179652
  92.3 18.1 %collective-permute-start.19 = (bf16[512,384]{1,0:T(8,128)(2,1)S(1)}, bf16[512,384]{1,0:T(8,128)(2,1)S(1)}, u32[]{:S(2)}, u32[]{:S(2)}) collective-permute-start(bf16[512,384]{1,0:T(8,128)(2,1)S(1)} %pad_maximum_fusion.6), channel_id=1, source_target_pairs={{0,4},{1,5},{2,6},{3,7},{4,0},{5,1},{6,2},{7,3},{8,12},{9,13},{10,... | collective-permute-start | bytes 1179656 | tf_op jit(solution)/shard_map/ppermute | solution.py:22
  92.4 13.0 %collective-permute-start.16 = (bf16[176,384]{1,0:T(8,128)(2,1)S(1)}, bf16[176,384]{1,0:T(8,128)(2,1)S(1)}, u32[]{:S(2)}, u32[]{:S(2)}) collective-permute-start(bf16[176,384]{1,0:T(8,128)(2,1)S(1)} %get-tuple-element.37), channel_id=1, source_target_pairs={{0,1},{1,2},{2,3},{3,0},{4,5},{5,6},{6,7},{7,4},{8,9},{9,10},{10,1... | collective-permute-start | bytes 405512 | tf_op jit(solution)/shard_map/ppermute | solution.py:18
  93.7 11.6 %collective-permute-start.13 = (bf16[160,384]{1,0:T(8,128)(2,1)S(1)}, bf16[160,384]{1,0:T(8,128)(2,1)S(1)}, u32[]{:S(2)}, u32[]{:S(2)}) collective-permute-start(bf16[160,384]{1,0:T(8,128)(2,1)S(1)} %slice.230), channel_id=1, source_target_pairs={{0,4},{1,5},{2,6},{3,7},{4,0},{5,1},{6,2},{7,3},{8,12},{9,13},{10,... | collective-permute-start | bytes 368648 | tf_op jit(solution)/shard_map/ppermute | solution.py:22
  95.1 11.7 %collective-permute-start.14 = (bf16[176,384]{1,0:T(8,128)(2,1)S(1)}, bf16[176,384]{1,0:T(8,128)(2,1)S(1)}, u32[]{:S(2)}, u32[]{:S(2)}) collective-permute-start(bf16[176,384]{1,0:T(8,128)(2,1)S(1)} %get-tuple-element.36), channel_id=1, source_target_pairs={{0,3},{1,0},{2,1},{3,2},{4,7},{5,4},{6,5},{7,6},{8,11},{9,8},{10,9... | collective-permute-start | bytes 405512 | tf_op jit(solution)/shard_map/ppermute | solution.py:18
  105.5 11.3 %collective-permute-start.17 = (bf16[512,384]{1,0:T(8,128)(2,1)S(1)}, bf16[512,384]{1,0:T(8,128)(2,1)S(1)}, u32[]{:S(2)}, u32[]{:S(2)}) collective-permute-start(bf16[512,384]{1,0:T(8,128)(2,1)S(1)} %pad_maximum_fusion.4), channel_id=1, source_target_pairs={{0,1},{1,2},{2,3},{3,0},{4,5},{5,6},{6,7},{7,4},{8,9},{9,10},{10,1... | collective-permute-start | bytes 1179656 | tf_op jit(solution)/shard_map/ppermute | solution.py:18
  106.9 9.8 %collective-permute-start.15 = (bf16[512,384]{1,0:T(8,128)(2,1)S(1)}, bf16[512,384]{1,0:T(8,128)(2,1)S(1)}, u32[]{:S(2)}, u32[]{:S(2)}) collective-permute-start(bf16[512,384]{1,0:T(8,128)(2,1)S(1)} %pad_maximum_fusion.3), channel_id=1, source_target_pairs={{0,3},{1,0},{2,1},{3,2},{4,7},{5,4},{6,5},{7,6},{8,11},{9,8},{10,9... | collective-permute-start | bytes 1179656 | tf_op jit(solution)/shard_map/ppermute | solution.py:18
  117.1 8.9 %collective-permute-start.18 = (bf16[512,384]{1,0:T(8,128)(2,1)S(1)}, bf16[512,384]{1,0:T(8,128)(2,1)S(1)}, u32[]{:S(2)}, u32[]{:S(2)}) collective-permute-start(bf16[512,384]{1,0:T(8,128)(2,1)S(1)} %pad_maximum_fusion.5), channel_id=1, source_target_pairs={{0,4},{1,5},{2,6},{3,7},{4,0},{5,1},{6,2},{7,3},{8,12},{9,13},{10,... | collective-permute-start | bytes 1179656 | tf_op jit(solution)/shard_map/ppermute | solution.py:22
  117.6 8.8 %collective-permute-start.20 = (bf16[512,384]{1,0:T(8,128)(2,1)S(1)}, bf16[512,384]{1,0:T(8,128)(2,1)S(1)}, u32[]{:S(2)}, u32[]{:S(2)}) collective-permute-start(bf16[512,384]{1,0:T(8,128)(2,1)S(1)} %pad_maximum_fusion.7), channel_id=1, source_target_pairs={{0,3},{1,0},{2,1},{3,2},{4,7},{5,4},{6,5},{7,6},{8,11},{9,8},{10,9... | collective-permute-start | bytes 1179656 | tf_op jit(solution)/shard_map/ppermute | solution.py:18
  121.0 9.5 %collective-permute-start.21 = (bf16[512,384]{1,0:T(8,128)(2,1)}, bf16[512,384]{1,0:T(8,128)(2,1)S(1)}, u32[]{:S(2)}, u32[]{:S(2)}) collective-permute-start(bf16[512,384]{1,0:T(8,128)(2,1)} %pad_maximum_fusion.8), channel_id=1, source_target_pairs={{0,1},{1,2},{2,3},{3,0},{4,5},{5,6},{6,7},{7,4},{8,9},{9,10},{10,1... | collective-permute-start | bytes 1179656 | tf_op jit(solution)/shard_map/ppermute | solution.py:18
  132.3 5.1 %collective-permute-start.22 = (bf16[128,384]{1,0:T(8,128)(2,1)S(1)}, bf16[128,384]{1,0:T(8,128)(2,1)S(1)}, u32[]{:S(2)}, u32[]{:S(2)}) collective-permute-start(bf16[128,384]{1,0:T(8,128)(2,1)S(1)} %select_bitcast_fusion), channel_id=1, source_target_pairs={{0,128},{8,136},{16,144},{24,152},{32,160},{40,168},{48,176},{56,1... | collective-permute-start | bytes 294920 | tf_op jit(solution)/shard_map/ppermute | solution.py:31
  137.4 7.3 %collective-permute-start.23 = (bf16[64,384]{1,0:T(8,128)(2,1)S(1)}, bf16[64,384]{1,0:T(8,128)(2,1)S(1)}, u32[]{:S(2)}, u32[]{:S(2)}) collective-permute-start(bf16[64,384]{1,0:T(8,128)(2,1)S(1)} %broadcast_select_fusion.3), channel_id=1, source_target_pairs={{0,64},{8,72},{16,80},{24,88},{32,96},{40,104},{48,112},{56,120},{... | collective-permute-start | bytes 147464 | tf_op jit(solution)/shard_map/ppermute | solution.py:31
  144.7 4.0 %collective-permute-start.24 = (bf16[32,384]{1,0:T(8,128)(2,1)S(1)}, bf16[32,384]{1,0:T(8,128)(2,1)S(1)}, u32[]{:S(2)}, u32[]{:S(2)}) collective-permute-start(bf16[32,384]{1,0:T(8,128)(2,1)S(1)} %broadcast_select_fusion.4), channel_id=1, source_target_pairs={{0,32},{8,40},{16,48},{24,56},{32,0},{40,8},{48,16},{56,24},{64,96... | collective-permute-start | bytes 73736 | tf_op jit(solution)/shard_map/ppermute | solution.py:31
  148.7 2.6 %collective-permute-start.25 = (bf16[16,384]{1,0:T(8,128)(2,1)S(1)}, bf16[16,384]{1,0:T(8,128)(2,1)S(1)}, u32[]{:S(2)}, u32[]{:S(2)}) collective-permute-start(bf16[16,384]{1,0:T(8,128)(2,1)S(1)} %broadcast_select_fusion.5), channel_id=1, source_target_pairs={{0,16},{8,24},{16,0},{24,8},{32,48},{40,56},{48,32},{56,40},{64,80... | collective-permute-start | bytes 36872 | tf_op jit(solution)/shard_map/ppermute | solution.py:31
  151.3 8.3 %collective-permute-start.26 = (bf16[8,384]{1,0:T(8,128)(2,1)S(1)}, bf16[8,384]{1,0:T(8,128)(2,1)S(1)}, u32[]{:S(2)}, u32[]{:S(2)}) collective-permute-start(bf16[8,384]{1,0:T(8,128)(2,1)S(1)} %broadcast_select_fusion.6), channel_id=1, source_target_pairs={{0,8},{8,0},{16,24},{24,16},{32,40},{40,32},{48,56},{56,48},{64,72... | collective-permute-start | bytes 18440 | tf_op jit(solution)/shard_map/ppermute | solution.py:31

commit v2 on v0

v2 whole, which is shorter than its diff:
```python
import functools

import jax
import jax.numpy as jnp
from jax import lax
from jax.experimental import pallas as pl
from jax.experimental.pallas import tpu as pltpu
from jax.sharding import PartitionSpec as P

STEPS = 50
EPS = 1e-06
BIG = 1e30
SEEN, WINDOW, HEAD, OWN_STEP, MARKS = 8, 68, 70, 73, 75
LOG2E = 1.4426950408889634
VMEM_LIMIT = 48 * 1024 * 1024
SMALL_LIMIT = 12 * 1024 * 1024


def ring(value, distance):
    return lax.ppermute(value, "mp", [(s, s // 4 * 4 + (s + distance) % 4) for s in range(8)])


def across(value):
    return lax.ppermute(value, "mp", [(s, s ^ 4) for s in range(8)])


def shifted(value, distance):
    count = lax.axis_size("queue")
    return lax.ppermute(value, "queue", [(s, (s + distance) % count) for s in range(count)])


def flipped(value, bit):
    return lax.ppermute(value, "queue", [(s, s ^ bit) for s in range(lax.axis_size("queue"))])


def vmem():
    return pl.BlockSpec(memory_space=pltpu.VMEM)


def anywhere():
    return pl.BlockSpec(memory_space=pl.ANY)


def smem():
    return pl.BlockSpec(memory_space=pltpu.SMEM)


def qkv_kernel(place, own_at, far, low, high, far_opp, two_a, two_b, two_c, modul, weight_at, kv, made, own, weight, sems):
    rows, part = own.shape
    half = rows // 2
    width = weight.shape[1]
    cut = two_a.shape[0] - half
    copies = [
        pltpu.make_async_copy(source, target, sems.at[i])
        for i, (source, target) in enumerate(((own_at, own), (weight_at.at[1], weight.at[0]), (weight_at.at[2], weight.at[1])))
    ]
    for copy in copies:
        copy.start()
    copies[0].wait()
    starts = [pl.multiple_of(place[i] * part, 128) for i in range(8)]
    chunk = 32
    for frame in range(2):
        for at in range(frame * half, (frame + 1) * half, chunk):
            parts = [
                (own, at), (far, at), (low, at), (high, at),
                (two_a, at) if at < half else (two_b, at - half),
                (two_a, half + at) if at < cut else (two_c, at - cut),
                (two_c, rows - cut + at) if at < rows - cut else (two_b, half + at - (rows - cut)),
                (far_opp, at),
            ]

            def load(i):
                ref, base = parts[i]
                return ref[base : base + chunk, :].astype(jnp.float32)

            total = load(0)
            for i in range(1, 8):
                total = total + load(i)
            mean = jnp.sum(total, axis=1, keepdims=True) * (1.0 / width)
            square = jnp.square(load(0) - mean)
            for i in range(1, 8):
                square = square + jnp.square(load(i) - mean)
            var = jnp.sum(square, axis=1, keepdims=True) * (1.0 / width)
            inverse = lax.rsqrt(var + EPS)
            for i in range(8):
                columns = pl.ds(starts[i], part)
                shift = modul[frame, 0:1, columns].astype(jnp.float32)
                scale = modul[frame, 1:2, columns].astype(jnp.float32) + 1.0
                value = (load(i) - mean) * inverse * scale + shift
                made[at : at + chunk, columns] = value.astype(jnp.bfloat16)
        left = made[frame * half : (frame + 1) * half, :]
        for which in range(2):
            if frame == 0:
                copies[1 + which].wait()
            result = jnp.dot(left, weight[which], preferred_element_type=jnp.float32).astype(jnp.bfloat16)
            for h in range(3):
                kv[which, h, frame * half : (frame + 1) * half, :] = result[:, h * 128 : (h + 1) * 128]


def query_kernel(made_at, weight_at, query, made, weight, sems):
    copies = [pltpu.make_async_copy(weight_at.at[0], weight, sems.at[0]), pltpu.make_async_copy(made_at, made, sems.at[1])]
    for copy in copies:
        copy.start()
    for copy in copies:
        copy.wait()
    result = jnp.dot(made[...], weight[...], preferred_element_type=jnp.float32).astype(jnp.bfloat16)
    for h in range(3):
        query[h] = result[:, h * 128 : (h + 1) * 128]


def attend_kernel(shape, allowed, query, *rest):
    blocks, first, last = shape
    keys, rest = rest[: len(blocks)], rest[len(blocks) :]
    if not first:
        top_in, sum_in, *rest = rest
    if last:
        out, scores = rest
    else:
        top_out, sum_out, scores = rest
    size = query.shape[2]
    tokf = query.shape[1] // 2
    factor = LOG2E / size**0.5
    ones = jnp.ones((tokf, size), jnp.bfloat16)
    for head, f in [(head, f) for head in range(query.shape[0]) for f in range(2)]:
        rows = slice(f * tokf, (f + 1) * tokf)
        q = query[head, rows, :]
        tiles = []
        for ref, slot in zip(keys, blocks):
            for g in range(2):
                if (slot, g, f) in ((0, 0, 1), (4, 1, 0)):
                    continue
                place = allowed[WINDOW + slot - 5] if slot >= 5 else slot
                tiles.append((ref, slice(g * tokf, (g + 1) * tokf), allowed[SEEN + (head * 2 + f) * 10 + place * 2 + g] > 0))
        top = jnp.full((tokf, size), -BIG, jnp.float32)
        for t, (ref, at, seen) in enumerate(tiles):
            s = lax.dot_general(q, ref[0, head, at, :], (((1,), (1,)), ((), ())), preferred_element_type=jnp.float32)
            scores[(head + f) % 2, t] = s
            top = jnp.maximum(top, jnp.where(seen, jnp.maximum(s[:, :size], s[:, size:]), -BIG))
        largest = jnp.broadcast_to(jnp.max(top, axis=1, keepdims=True) * factor, (tokf, size))
        total = jnp.zeros((tokf, 2 * size), jnp.float32)
        if not first:
            before = top_in[head, rows, :]
            largest = jnp.maximum(largest, before)
            fade = jnp.exp2(before - largest)
            total = sum_in[head, rows, :] * jnp.concatenate([fade, fade], axis=1)
        for t, (ref, at, seen) in enumerate(tiles):
            v = jnp.concatenate([ref[1, head, at, :], ones], axis=1)
            base = jnp.where(seen, largest, BIG)
            weights = jnp.concatenate(
                [jnp.exp2(scores[(head + f) % 2, t, :, i * size : (i + 1) * size] * factor - base) for i in range(2)], axis=1
            ).astype(jnp.bfloat16)
            total = total + jnp.dot(weights, v, preferred_element_type=jnp.float32)
        if last:
            out[rows, head * size : (head + 1) * size] = (total[:, :size] / total[:, size:]).astype(jnp.bfloat16)
        else:
            top_out[head, rows, :] = largest
            sum_out[head, rows, :] = total


def attend(blocks, allowed, query, keys, state=(), last=False):
    heads, rows, size = query.shape
    tokf = rows // 2
    if last:
        out_shape = jax.ShapeDtypeStruct((rows, heads * size), jnp.bfloat16)
    else:
        out_shape = [jax.ShapeDtypeStruct((heads, rows, n * size), jnp.float32) for n in (1, 2)]
    tiles = 4 * len(blocks)
    return pl.pallas_call(
        functools.partial(attend_kernel, (blocks, not state, last)),
        out_shape=out_shape,
        in_specs=[smem()] + [vmem()] * (1 + len(keys) + len(state)),
        out_specs=vmem() if last else [vmem()] * 2,
        scratch_shapes=[pltpu.VMEM((2, 2 * len(blocks), tokf, tokf), jnp.float32)],
        compiler_params=pltpu.CompilerParams(vmem_limit_bytes=SMALL_LIMIT),
        cost_estimate=pl.CostEstimate(
            flops=6 * heads * tiles * tokf * tokf * size, bytes_accessed=4 * tiles * tokf * size, transcendentals=heads * tiles * tokf * tokf
        ),
    )(allowed, query, *keys, *state)


def added(*terms):
    total = terms[0].astype(jnp.float32)
    for term in terms[1:]:
        total = total + term.astype(jnp.float32)
    return total


def product(place, slot, left, weight):
    part = weight.shape[0]
    columns = pl.ds(pl.multiple_of(place[slot] * part, 128), part)
    return jnp.dot(left, weight[:, columns], preferred_element_type=jnp.float32).astype(jnp.bfloat16)


def first_kernel(cut, place, attended, weight, far_opp, two_a, two_b, two_c):
    rows = attended.shape[0]
    half = rows // 2
    left = attended[...]
    far_opp[...] = product(place, 7, left, weight)
    opp, far_low, far_high = (product(place, slot, left, weight) for slot in (4, 5, 6))
    two_a[:half] = opp[:half]
    two_a[half:] = far_low[:cut]
    two_b[:half] = opp[half:]
    two_b[half:] = far_high[rows - cut :]
    two_c[: rows - cut] = far_low[cut:]
    two_c[rows - cut :] = far_high[: rows - cut]


def second_kernel(cut, place, attended, weight, got_opp, got_a, got_b, got_c, sum_far, sum_low, sum_high, own):
    rows = attended.shape[0]
    half = rows // 2
    bf = jnp.bfloat16
    left = attended[...]
    far, low, high = (product(place, slot, left, weight) for slot in (1, 2, 3))
    sum_far[:cut] = added(far[:cut], got_opp[:cut], got_a[half:]).astype(bf)
    sum_far[cut : rows - cut] = added(far[cut : rows - cut], got_opp[cut : rows - cut]).astype(bf)
    sum_far[rows - cut :] = added(far[rows - cut :], got_opp[rows - cut :], got_b[half:]).astype(bf)
    sum_low[:cut] = added(low[:cut], got_a[:cut]).astype(bf)
    sum_low[cut:half] = added(low[cut:half], got_a[cut:half], got_c[: half - cut]).astype(bf)
    sum_low[half:] = added(low[half:], got_c[half - cut : rows - cut]).astype(bf)
    sum_high[:half] = added(high[:half], got_c[rows - cut : rows - cut + half]).astype(bf)
    sum_high[half : rows - cut] = added(high[half : rows - cut], got_b[: half - cut], got_c[rows - cut + half :]).astype(bf)
    sum_high[rows - cut :] = added(high[rows - cut :], got_b[half - cut : half]).astype(bf)
    own[...] = product(place, 0, left, weight)


def summed(kernel, place, attended, weight, terms, heights):
    rows, part = attended.shape
    return pl.pallas_call(
        kernel,
        out_shape=[jax.ShapeDtypeStruct((height, part), jnp.bfloat16) for height in heights],
        in_specs=[smem()] + [vmem()] * (2 + len(terms)),
        out_specs=[vmem()] * len(heights),
        compiler_params=pltpu.CompilerParams(vmem_limit_bytes=SMALL_LIMIT),
        cost_estimate=pl.CostEstimate(flops=8 * rows * part * part, bytes_accessed=18 * rows * part, transcendentals=0),
    )(place, attended, weight, *terms)


def split_kernel(at, marks, kept, got, send, keep):
    mine = marks[at + 1]
    for i in range(send.shape[0]):
        for out, side in ((send, 1 - mine), (keep, mine)):
            row = 2 * i + side
            out[i] = jnp.where(marks[at] > 0, kept[row].astype(jnp.float32), got[row].astype(jnp.float32)).astype(jnp.bfloat16)


def split(step, facts, kept, got):
    count, share, columns = kept.shape
    return pl.pallas_call(
        functools.partial(split_kernel, MARKS + 2 * step),
        out_shape=[jax.ShapeDtypeStruct((count // 2, share, columns), jnp.bfloat16)] * 2,
        in_specs=[smem(), vmem(), vmem()],
        out_specs=[vmem()] * 2,
        compiler_params=pltpu.CompilerParams(vmem_limit_bytes=SMALL_LIMIT),
        cost_estimate=pl.CostEstimate(flops=count * share * columns, bytes_accessed=6 * count * share * columns, transcendentals=0),
    )(facts, kept, got)


def turned(index):
    return index ^ (((index >> 3) & 1) << 2)


def head_kernel(marks, attended, latents, send, keep, scratch):
    part = attended.shape[1]
    tokf = scratch.shape[0]
    rows = pl.ds(pl.multiple_of(marks[HEAD] * tokf, tokf), tokf)
    scratch[:, :part] = attended[rows, :].astype(jnp.float32)
    scratch[:, part : 2 * part] = latents[rows, :].astype(jnp.float32)
    scratch[:, 2 * part :] = jnp.full((tokf, scratch.shape[1] - 2 * part), marks[HEAD + 2].astype(jnp.float32))
    share = send.shape[1]
    for i in range(send.shape[0]):
        for out, side in ((send, 1 - marks[HEAD + 1]), (keep, marks[HEAD + 1])):
            row = pl.multiple_of((turned(2 * i) + side) * share, share)
            out[i] = scratch[pl.ds(row, share), :].astype(jnp.bfloat16)


def share_kernel(place, kept, got, weight, rows, own, far):
    part = weight.shape[0]
    chosen = jnp.where(place[MARKS + 8] > 0, kept[0].astype(jnp.float32), got[0].astype(jnp.float32))
    rows[...] = chosen
    left = jnp.concatenate([chosen[:, :part]] * 2, axis=0).astype(jnp.bfloat16)
    for out, slots in ((own, (0, 2, 3, 4)), (far, (1, 5, 6, 7))):
        for i, slot in enumerate(slots):
            columns = pl.ds(pl.multiple_of(place[slot] * part, 128), part)
            result = jnp.dot(left, weight[:, columns], preferred_element_type=jnp.float32)
            out[i] = result[: out.shape[1]].astype(jnp.bfloat16)


def pass_kernel(own, far, *outs):
    for i, out in enumerate(outs):
        out[...] = added(own[i], far[i]).astype(jnp.bfloat16)


def estimate_kernel(rows, own, low, high, opposite, gates, out):
    part = own.shape[1]
    latent = rows[:, part : 2 * part]
    step = rows[0:1, 2 * part : 2 * part + 1]
    index = lax.broadcasted_iota(jnp.int32, gates.shape, 0).astype(jnp.float32) + 1.0
    gate = jnp.sum(jnp.where(index == step, gates[...].astype(jnp.float32), 0.0), axis=0, keepdims=True)
    velocity = (latent + gate * added(own[...], low[...], high[...], opposite[...])).astype(jnp.bfloat16)
    level = step / STEPS
    sigma = 3.0 * level / (1.0 + 2.0 * level)
    out[...] = (latent - sigma * velocity.astype(jnp.float32)).astype(jnp.bfloat16)


def velocity_kernel(facts, own, far, low, high, latents, gates, velocity):
    tokf = own.shape[0] // 2
    index = lax.broadcasted_iota(jnp.int32, gates.shape, 0) + 1
    for frame in range(2):
        at = slice(frame * tokf, (frame + 1) * tokf)
        gate = jnp.sum(jnp.where(index == facts[OWN_STEP + frame], gates[...].astype(jnp.float32), 0.0), axis=0, keepdims=True)
        projected = added(own[at, :], far[at, :], low[at, :], high[at, :])
        velocity[at, :] = (latents[at, :].astype(jnp.float32) + gate * projected).astype(jnp.bfloat16)


def small_call(kernel, in_specs, shapes, args, scratch=()):
    return pl.pallas_call(
        kernel,
        out_shape=shapes,
        in_specs=in_specs,
        out_specs=[vmem()] * len(shapes),
        scratch_shapes=list(scratch),
        compiler_params=pltpu.CompilerParams(vmem_limit_bytes=SMALL_LIMIT),
        cost_estimate=pl.CostEstimate(flops=1 << 20, bytes_accessed=1 << 20, transcendentals=0),
    )(*args)


def on_device(latents, step_index, head_index, band, mod_table, gate_table, qkv_weight, out_weight):
    rows, part = latents.shape
    frames = step_index.shape[0]
    tokf = rows // frames
    width = mod_table.shape[2]
    heads = band.shape[0]
    size = part // heads
    count = lax.axis_size("queue")
    me = lax.axis_index("queue")
    member = lax.axis_index("mp")
    frames_all = frames * count
    half = rows // 2
    x, y = member & 3, member >> 2
    slots = [yy * 4 + xx for yy, xx in (
        (y, x), (1 - y, x), (y, (x + 3) & 3), (y, (x + 1) & 3),
        (y, x ^ 2), (1 - y, (x + 3) & 3), (1 - y, (x + 1) & 3), (1 - y, x ^ 2),
    )]
    odd = me & 1 == 1
    head = head_index[0]
    position = (me * frames + jnp.arange(frames, dtype=jnp.int32) - head) & (frames_all - 1)
    offset = jnp.arange(5 * frames, dtype=jnp.int32)[None, :] - 2 * frames - jnp.arange(frames, dtype=jnp.int32)[:, None]
    other = position[:, None] + offset
    inside = (other >= 0) & (other < frames_all)
    near = jnp.abs(offset)[None, :, :] <= band[:, None, None]
    allowed = (inside[None, :, :] & near).reshape(-1)
    local_frame = head & 1
    mine, source = turned(me), turned(head >> 1)
    small = [jnp.where(odd, 1, 3), jnp.where(odd, 3, 1), local_frame, me & 1, lax.dynamic_index_in_dim(step_index, local_frame, 0, keepdims=False)]
    small += [step_index[f] for f in range(frames)]
    for bit in (1, 2, 4, 8, 16):
        small += [((source ^ mine) & bit) == 0, (mine & (2 * bit)) != 0]
    facts = jnp.concatenate([jnp.stack([jnp.asarray(v, jnp.int32) for v in slots]), allowed.astype(jnp.int32), jnp.stack([jnp.asarray(v, jnp.int32) for v in small])])

    cut = 96
    bf = jnp.bfloat16
    far, low, high = across(latents), ring(latents, 1), ring(latents, -1)
    far_opp = ring(far, 2)
    two_a = ring(jnp.concatenate([low[:half], far[:cut]]), 1)
    two_b = ring(jnp.concatenate([high[half:], far[rows - cut :]]), -1)
    two_c = across(jnp.concatenate([low[cut:], high[: rows - cut]]))

    modul = jnp.concatenate([lax.dynamic_index_in_dim(mod_table, step_index[f] - 1, 0) for f in range(frames)])
    kv, modulated = pl.pallas_call(
        qkv_kernel,
        out_shape=[jax.ShapeDtypeStruct((2, heads, rows, size), bf), jax.ShapeDtypeStruct((rows, width), bf)],
        in_specs=[smem(), anywhere()] + [vmem()] * 8 + [anywhere()],
        out_specs=[vmem()] * 2,
        scratch_shapes=[pltpu.VMEM((rows, part), bf), pltpu.VMEM((2, width, part), bf), pltpu.SemaphoreType.DMA((3,))],
        compiler_params=pltpu.CompilerParams(vmem_limit_bytes=VMEM_LIMIT),
        cost_estimate=pl.CostEstimate(flops=4 * rows * width * part, bytes_accessed=6 * width * part, transcendentals=0),
    )(facts, latents, far, low, high, far_opp, two_a, two_b, two_c, modul, qkv_weight)

    upper2 = shifted(kv, -2)
    lower2 = shifted(kv, 2)
    partner = flipped(kv, 1)
    query = pl.pallas_call(
        query_kernel,
        out_shape=jax.ShapeDtypeStruct((heads, rows, size), bf),
        in_specs=[anywhere()] * 2,
        out_specs=vmem(),
        scratch_shapes=[pltpu.VMEM((rows, width), bf), pltpu.VMEM((width, part), bf), pltpu.SemaphoreType.DMA((2,))],
        compiler_params=pltpu.CompilerParams(vmem_limit_bytes=VMEM_LIMIT),
        cost_estimate=pl.CostEstimate(flops=2 * rows * width * part, bytes_accessed=2 * width * part, transcendentals=0),
    )(modulated, qkv_weight)

    state = attend((2, 5), facts, query, (kv, partner))
    upper2, lower2, *state = lax.optimization_barrier((upper2, lower2, *state))
    passed = flipped(jnp.where(odd, lower2, upper2), 1)
    state = attend((4, 0), facts, query, (upper2, lower2), state)
    attended = attend((6,), facts, query, (passed,), state, last=True)

    sent_opp, two_a, two_b, two_c = summed(
        functools.partial(first_kernel, cut), facts, attended, out_weight, (), (rows, half + cut, half + cut, 2 * (rows - cut))
    )
    got = ring(sent_opp, 2), ring(two_a, -1), ring(two_b, 1), across(two_c)

    share = tokf // count
    wide = 2 * part + 128

    def shape(*dims, kind=bf):
        return jax.ShapeDtypeStruct(dims, kind)

    send, kept = small_call(
        head_kernel,
        [smem()] + [vmem()] * 2,
        [shape(count // 2, share, wide)] * 2,
        (facts, lax.optimization_barrier((attended, sent_opp))[0], latents),
        [pltpu.VMEM((tokf, wide), jnp.float32)],
    )
    moved = flipped(send, 1)
    for step in (0, 1, 2):
        send, kept = split(step, facts, kept, moved)
        moved = flipped(send, turned(2 << step))
    *got, moved = lax.optimization_barrier((*got, moved))
    sum_far, sum_low, sum_high, p_own = summed(functools.partial(second_kernel, cut), facts, attended, out_weight, got, (rows,) * 4)
    last = across(sum_far), ring(sum_low, -1), ring(sum_high, 1)
    send, kept = split(3, facts, kept, moved)
    moved = flipped(send, 16)
    held, mini_own, mini_far = small_call(
        share_kernel,
        [smem()] + [vmem()] * 3,
        [shape(share, wide, kind=jnp.float32)] + [shape(4, share, part)] * 2,
        (facts, kept, moved, out_weight),
    )
    *last, mini_far = lax.optimization_barrier((*last, across(mini_far)))
    own, low, high, opposite = small_call(pass_kernel, [vmem()] * 2, [shape(share, part)] * 4, (mini_own, mini_far))
    (head_frame,) = small_call(
        estimate_kernel,
        [vmem()] * 6,
        [shape(share, part)],
        (held, own, ring(low, -1), ring(high, 1), ring(opposite, 2), gate_table),
    )

    (velocity,) = small_call(
        velocity_kernel, [smem()] + [vmem()] * 6, [shape(rows, part)], (facts, p_own, *last, latents, gate_table)
    )
    return (velocity, head_frame)


def solution(mesh):
    placed = (
        P("queue", "mp"),
        P("queue"),
        P(),
        P("mp"),
        P(),
        P(None, "mp"),
        P(None, None, "mp"),
        P("mp", None),
    )
    return jax.shard_map(
        on_device,
        mesh=mesh,
        in_specs=placed,
        out_specs=(P("queue", "mp"), P("queue", "mp")),
        check_vma=False,
    )
```

time: 468 us -> 125 us (0.27)
  waiting for transfers between devices: 364 us -> 48.1 us
  local copies, waits for them, and re-layouts: 37.1 us -> 5.63 us
  starting transfers between devices: 7.71 us -> 37.1 us
  Pallas kernels: 0 us -> 28.9 us
  matrix products: 24.3 us -> 0 us
  other arithmetic: 19.1 us -> 1.07 us
  between operations: 14.6 us -> 4.21 us
    psum x1 -> x0, waiting for transfers between devices: 254 us -> none  [from_root(): return lax.psum(block, axis)]
    unnamed x4 -> x0, waiting for transfers between devices: 46.2 us -> none
    all_gather x1 -> x0, waiting for transfers between devices: 44.6 us -> none  [on_device(): whole = lax.all_gather(latents, 'mp', axis=1, tiled=True)]
    ppermute x4 -> x27, starting transfers between devices: 7.59 us -> 37.1 us  [the longest x13 17.6 us: ring(): lax.ppermute(value, 'mp', [(s, s // 4 * 4 + (s + distance) % 4) for s in...]
    ppermute x4 -> x27, waiting for transfers between devices: 18.9 us -> 48.1 us  [the longest x13 19 us: ring(): lax.ppermute(value, 'mp', [(s, s // 4 * 4 + (s + distance) % 4) for s in...]
    pallas_call x0 -> x16, Pallas kernels: none -> 28.9 us  [the longest x3 8.26 us: attend(): pl.pallas_call(functools.partial(attend_kernel, (blocks, not state, last)...]
    dot_general x6 -> x0, matrix products: 24.3 us -> none  [the longest x1 8.55 us: on_device(): jnp.einsum('fthd,gshd->hftgs', qshaped, kshaped, preferred_element_type=j...]
    another operation x3 -> x0, local copies, waits for them, and re-layouts: 14.3 us -> none  [the longest x1 6.17 us: on_device(): kshaped = window_kv[0].reshape(5 * frames, tokf, local_heads, head_size)]
  transfers between devices with their start and end apart: 7 -> 27, of which waited for: 6 -> 10; matrix products, arithmetic and copies ran while one was open for 3% -> 4% of each run, Pallas kernels for 0% -> 12%
where the time goes in v2:
time: 125 us
  waiting for transfers between devices  48.1 us (38%)
  starting transfers between devices  37.1 us (30%)
  Pallas kernels  28.9 us (23%)
  local copies, waits for them, and re-layouts  5.63 us (5%)
  between operations  4.21 us (3%)
    ppermute x13, waiting for transfers between devices, ring(): lax.ppermute(value, 'mp', [(s, s // 4 * 4 + (s + distance) % 4) for s in...  19 us
    ppermute x13, starting transfers between devices, ring(): lax.ppermute(value, 'mp', [(s, s // 4 * 4 + (s + distance) % 4) for s in...  17.6 us
    ppermute x7, waiting for transfers between devices, flipped(): lax.ppermute(value, 'queue', [(s, s ^ bit) for s in range(lax.axis_size('...  16.3 us
    ppermute x2, waiting for transfers between devices, shifted(): lax.ppermute(value, 'queue', [(s, (s + distance) % count) for s in range(...  9.29 us
    ppermute x2, starting transfers between devices, shifted(): lax.ppermute(value, 'queue', [(s, (s + distance) % count) for s in range(...  8.36 us
    pallas_call x3, Pallas kernels, attend(): pl.pallas_call(functools.partial(attend_kernel, (blocks, not state, last)...  8.26 us
    pallas_call x1, Pallas kernels, on_device(): pl.pallas_call(qkv_kernel, out_shape=[jax.ShapeDtypeStruct((2, heads, row...  7.46 us
    ppermute x7, starting transfers between devices, flipped(): lax.ppermute(value, 'queue', [(s, s ^ bit) for s in range(lax.axis_size('...  5.81 us
  transfers between devices with their start and end apart: 27, of which 10 were waited for; matrix products, arithmetic and copies ran while one was open for 4% of the time, Pallas kernels for 12%

profile of v2, /device:TPU:6, one launch (start us, length us, event | category | flops | bytes accessed | tf_op | source)
XLA Modules:
  0.0 124.9 jit_solution(11534220416777328913)
XLA Ops:
  0.6 0.9 collective-permute-start.2
  1.5 2.4 %collective-permute-start.1 = (bf16[512,384]{1,0:T(8,128)(2,1)}, bf16[512,384]{1,0:T(8,128)(2,1)S(1)}, u32[]{:S(2)}, u32[]{:S(2)}) collective-permute-start(bf16[512,384]{1,0:T(8,128)(2,1)} %latents.3), channel_id=1, source_target_pairs={{0,1},{1,2},{2,3},{3,0},{4,5},{5,6},{6,7},{7,4},{8,9},{9,10},{10,1... | collective-permute-start | bytes 1179656 | tf_op jit(solution)/shard_map/ppermute | solution.py:20
  3.9 1.6 %collective-permute-start = (bf16[512,384]{1,0:T(8,128)(2,1)}, bf16[512,384]{1,0:T(8,128)(2,1)S(1)}, u32[]{:S(2)}, u32[]{:S(2)}) collective-permute-start(bf16[512,384]{1,0:T(8,128)(2,1)} %latents.3), channel_id=1, source_target_pairs={{0,4},{1,5},{2,6},{3,7},{4,0},{5,1},{6,2},{7,3},{8,12},{9,13},{10,... | collective-permute-start | bytes 1179656 | tf_op jit(solution)/shard_map/ppermute | solution.py:24
  6.3 0.7 and_convert_fusion
  7.0 1.4 %fusion.2 = (s32[1]{0:T(128)}, s32[1]{0:T(128)}, s32[1]{0:T(128)}) fusion(s32[2]{0:T(128)} %param.9, s32[]{:T(128)S(6)} %select_n.28), kind=kLoop, calls=%fused_computation.14 | loop fusion | bytes 28 | tf_op jit(solution)/shard_map/slice | solution.py:355
  11.1 1.4 %concatenate.15.place.allowed.marks.facts = s32[85]{0:T(128)S(1)} concatenate(s32[1]{0:T(128)} %bitcast, s32[1]{0:T(128)} %bitcast.1, s32[1]{0:T(128)} %bitcast.2, s32[1]{0:T(128)} %bitcast.3, s32[1]{0:T(128)} %bitcast.4, s32[1]{0:T(128)} %bitcast.5, s32[1]{0:T(128)} %bitcast.6, s32[1]{0:T(128)} %bitcast.7, s32[60]{0:T(128)S(1)} %reshape.87, s32[1]{0:T(128)} %bitcast.9, ...), dimensions={0} | concatenate | bytes 680 | tf_op jit(solution)/shard_map/concatenate | solution.py:358
  12.5 0.7 constant_dynamic-slice_fusion.1
  13.4 1.4 %collective-permute-start.6 = (bf16[832,384]{1,0:T(8,128)(2,1)S(1)}, bf16[832,384]{1,0:T(8,128)(2,1)S(1)}, u32[]{:S(2)}, u32[]{:S(2)}) collective-permute-start(bf16[832,384]{1,0:T(8,128)(2,1)S(1)} %pad_maximum_fusion), channel_id=1, source_target_pairs={{0,4},{1,5},{2,6},{3,7},{4,0},{5,1},{6,2},{7,3},{8,12},{9,13},{10,... | collective-permute-start | bytes 1916936 | tf_op jit(solution)/shard_map/ppermute | solution.py:24
  14.9 3.0 %collective-permute-start.4 = (bf16[352,384]{1,0:T(8,128)(2,1)S(1)}, bf16[352,384]{1,0:T(8,128)(2,1)S(1)}, u32[]{:S(2)}, u32[]{:S(2)}) collective-permute-start(bf16[352,384]{1,0:T(8,128)(2,1)S(1)} %pad_maximum_fusion.1), channel_id=1, source_target_pairs={{0,1},{1,2},{2,3},{3,0},{4,5},{5,6},{6,7},{7,4},{8,9},{9,10},{10,1... | collective-permute-start | bytes 811016 | tf_op jit(solution)/shard_map/ppermute | solution.py:20
  18.1 0.9 collective-permute-start.5
  19.0 11.6 %collective-permute-done.4.two_a = bf16[352,384]{1,0:T(8,128)(2,1)S(1)} collective-permute-done((bf16[352,384]{1,0:T(8,128)(2,1)S(1)}, bf16[352,384]{1,0:T(8,128)(2,1)S(1)}, u32[]{:S(2)}, u32[]{:S(2)}) %collective-permute-start.4) | collective-permute-done | bytes 270368 | tf_op jit(solution)/shard_map/ppermute | solution.py:20
  30.6 3.6 %collective-permute-done.5.two_b = bf16[352,384]{1,0:T(8,128)(2,1)S(1)} collective-permute-done((bf16[352,384]{1,0:T(8,128)(2,1)S(1)}, bf16[352,384]{1,0:T(8,128)(2,1)S(1)}, u32[]{:S(2)}, u32[]{:S(2)}) %collective-permute-start.5) | collective-permute-done | bytes 270368 | tf_op jit(solution)/shard_map/ppermute | solution.py:20
  34.3 7.5 %shard_map.95 = (bf16[2,3,512,128]{3,2,1,0:T(8,128)(2,1)S(1)}, bf16[512,3072]{1,0:T(8,128)(2,1)}) custom-call(s32[85]{0:T(128)S(1)} %concatenate.15.place.allowed.marks.facts, bf16[512,384]{1,0:T(8,128)(2,1)S(1)} %copy-done.1, bf16[512,384]{1,0:T(8,128)(2,1)S(1)} %collective-permute-done.far, bf16[512,384]{1,0:T(8,128)(2,1)S(1)} %collective-permute-done.1.low, ...), custom_call_target="tpu_custom_call" | custom-call | flops 2415919104 | bytes 7077888 | tf_op jit(solution)/shard_map/pallas_call | solution.py:369
  42.0 2.0 %collective-permute-start.8 = (bf16[2,3,512,128]{3,2,1,0:T(8,128)(2,1)S(1)}, bf16[2,3,512,128]{3,2,1,0:T(8,128)(2,1)S(1)}, u32[]{:S(2)}, u32[]{:S(2)}) collective-permute-start(bf16[2,3,512,128]{3,2,1,0:T(8,128)(2,1)S(1)} %get-tuple-element.48.rest_0_), channel_id=1, source_target_pairs={{0,16},{8,24},{16,32},{24,40},{32,48},{40,56},{48,64},{56,72},{64,... | collective-permute-start | bytes 2359304 | tf_op jit(solution)/shard_map/ppermute | solution.py:29
  44.0 6.4 %collective-permute-start.7 = (bf16[2,3,512,128]{3,2,1,0:T(8,128)(2,1)S(1)}, bf16[2,3,512,128]{3,2,1,0:T(8,128)(2,1)S(1)}, u32[]{:S(2)}, u32[]{:S(2)}) collective-permute-start(bf16[2,3,512,128]{3,2,1,0:T(8,128)(2,1)S(1)} %get-tuple-element.48.rest_0_), channel_id=1, source_target_pairs={{0,240},{8,248},{16,0},{24,8},{32,16},{40,24},{48,32},{56,40},{64,... | collective-permute-start | bytes 2359304 | tf_op jit(solution)/shard_map/ppermute | solution.py:29
  50.4 1.9 %copy-done.2 = bf16[512,3072]{1,0:T(8,128)(2,1)S(1)} copy-done((bf16[512,3072]{1,0:T(8,128)(2,1)S(1)}, bf16[512,3072]{1,0:T(8,128)(2,1)}, u32[]{:S(2)}) %copy-start.2) | copy-done | bytes 3145752
  52.3 3.5 %shard_map.96.query = bf16[3,512,128]{2,1,0:T(8,128)(2,1)S(1)} custom-call(bf16[512,3072]{1,0:T(8,128)(2,1)S(1)} %copy-done.2, bf16[3,3072,384]{2,1,0:T(8,128)(2,1)} %weight_at.3), custom_call_target="tpu_custom_call" | custom-call | flops 1207959552 | bytes 2359296 | tf_op jit(solution)/shard_map/pallas_call | solution.py:382
  55.7 3.4 %shard_map.97 = (f32[3,512,128]{2,1,0:T(8,128)S(1)}, f32[3,512,256]{2,1,0:T(8,128)S(1)}) custom-call(s32[85]{0:T(128)S(1)} %concatenate.15.place.allowed.marks.facts, bf16[3,512,128]{2,1,0:T(8,128)(2,1)S(1)} %shard_map.96.query, bf16[2,3,512,128]{3,2,1,0:T(8,128)(2,1)S(1)} %get-tuple-element.48.rest_0_, ...), custom_call_target="tpu_custom_call" | custom-call | flops 1207959552 | bytes 1048576 | tf_op jit(solution)/shard_map/pallas_call | solution.py:168
  59.1 9.3 %collective-permute-done.8.rest_1_ = bf16[2,3,512,128]{3,2,1,0:T(8,128)(2,1)S(1)} collective-permute-done((bf16[2,3,512,128]{3,2,1,0:T(8,128)(2,1)S(1)}, bf16[2,3,512,128]{3,2,1,0:T(8,128)(2,1)S(1)}, u32[]{:S(2)}, u32[]{:S(2)}) %collective-permute-start.8) | collective-permute-done | bytes 786464 | tf_op jit(solution)/shard_map/ppermute | solution.py:29
  68.6 2.8 %shard_map.98 = (f32[3,512,128]{2,1,0:T(8,128)S(1)}, f32[3,512,256]{2,1,0:T(8,128)S(1)}) custom-call(s32[85]{0:T(128)S(1)} %concatenate.15.place.allowed.marks.facts, bf16[3,512,128]{2,1,0:T(8,128)(2,1)S(1)} %shard_map.96.query, bf16[2,3,512,128]{3,2,1,0:T(8,128)(2,1)S(1)} %collective-permute-done.7.rest_0_, ...), custom_call_target="tpu_custom_call" | custom-call | flops 1207959552 | bytes 1048576 | tf_op jit(solution)/shard_map/pallas_call | solution.py:168
  71.4 2.1 %shard_map.99.attended = bf16[512,384]{1,0:T(8,128)(2,1)S(1)} custom-call(s32[85]{0:T(128)S(1)} %concatenate.15.place.allowed.marks.facts, bf16[3,512,128]{2,1,0:T(8,128)(2,1)S(1)} %shard_map.96.query, bf16[2,3,512,128]{3,2,1,0:T(8,128)(2,1)S(1)} %collective-permute-done.10.rest_0_, f32[3,512,128]{2,1,0:T(8,128)S(1)} %get-tuple-element.55.rest_1_, ...), custom_call_target="tpu_custom_call" | custom-call | flops 603979776 | bytes 524288 | tf_op jit(solution)/shard_map/pallas_call | solution.py:168
  73.5 1.7 %shard_map.100 = (bf16[512,384]{1,0:T(8,128)(2,1)S(1)}, bf16[352,384]{1,0:T(8,128)(2,1)S(1)}, bf16[352,384]{1,0:T(8,128)(2,1)S(1)}, bf16[832,384]{1,0:T(8,128)(2,1)S(1)}) custom-call(s32[85]{0:T(128)S(1)} %concatenate.15.place.allowed.marks.facts, bf16[512,384]{1,0:T(8,128)(2,1)S(1)} %shard_map.99.attended, bf16[384,3072]{1,0:T(8,128)(2,1)S(1)} %copy-done), custom_call_target="tpu_custom_call" | custom-call | flops 603979776 | bytes 3538944 | tf_op jit(solution)/shard_map/pallas_call | solution.py:228
  75.4 0.7 shard_map.101
  76.1 0.5 collective-permute-start.15
  76.6 0.4 collective-permute-start.11
  77.0 1.2 collective-permute-start.12
  78.2 2.1 %collective-permute-start.13 = (bf16[352,384]{1,0:T(8,128)(2,1)S(1)}, bf16[352,384]{1,0:T(8,128)(2,1)S(1)}, u32[]{:S(2)}, u32[]{:S(2)}) collective-permute-start(bf16[352,384]{1,0:T(8,128)(2,1)S(1)} %get-tuple-element.59), channel_id=1, source_target_pairs={{0,1},{1,2},{2,3},{3,0},{4,5},{5,6},{6,7},{7,4},{8,9},{9,10},{10,1... | collective-permute-start | bytes 811016 | tf_op jit(solution)/shard_map/ppermute | solution.py:20
  80.2 0.6 shard_map.102
  81.0 4.8 %collective-permute-done.16.got = bf16[8,8,896]{2,1,0:T(8,128)(2,1)S(1)} collective-permute-done((bf16[8,8,896]{2,1,0:T(8,128)(2,1)S(1)}, bf16[8,8,896]{2,1,0:T(8,128)(2,1)S(1)}, u32[]{:S(2)}, u32[]{:S(2)}) %collective-permute-start.16) | collective-permute-done | bytes 114720 | tf_op jit(solution)/shard_map/ppermute | solution.py:33
  85.7 0.6 shard_map.103
  86.3 1.0 collective-permute-start.17
  87.3 4.2 %collective-permute-done.17.got = bf16[4,8,896]{2,1,0:T(8,128)(2,1)S(1)} collective-permute-done((bf16[4,8,896]{2,1,0:T(8,128)(2,1)S(1)}, bf16[4,8,896]{2,1,0:T(8,128)(2,1)S(1)}, u32[]{:S(2)}, u32[]{:S(2)}) %collective-permute-start.17) | collective-permute-done | bytes 57376 | tf_op jit(solution)/shard_map/ppermute | solution.py:33
  91.6 0.6 shard_map.104
  92.1 2.6 %collective-permute-start.18 = (bf16[2,8,896]{2,1,0:T(8,128)(2,1)S(1)}, bf16[2,8,896]{2,1,0:T(8,128)(2,1)S(1)}, u32[]{:S(2)}, u32[]{:S(2)}) collective-permute-start(bf16[2,8,896]{2,1,0:T(8,128)(2,1)S(1)} %get-tuple-element.68), channel_id=1, source_target_pairs={{0,96},{8,104},{16,112},{24,120},{32,64},{40,72},{48,80},{56,88},{... | collective-permute-start | bytes 86024 | tf_op jit(solution)/shard_map/ppermute | solution.py:33
  95.0 3.2 %collective-permute-done.18.got = bf16[2,8,896]{2,1,0:T(8,128)(2,1)S(1)} collective-permute-done((bf16[2,8,896]{2,1,0:T(8,128)(2,1)S(1)}, bf16[2,8,896]{2,1,0:T(8,128)(2,1)S(1)}, u32[]{:S(2)}, u32[]{:S(2)}) %collective-permute-start.18) | collective-permute-done | bytes 28704 | tf_op jit(solution)/shard_map/ppermute | solution.py:33
  98.2 1.8 %shard_map.105 = (bf16[512,384]{1,0:T(8,128)(2,1)S(1)}, bf16[512,384]{1,0:T(8,128)(2,1)S(1)}, bf16[512,384]{1,0:T(8,128)(2,1)S(1)}, bf16[512,384]{1,0:T(8,128)(2,1)S(1)}) custom-call(s32[85]{0:T(128)S(1)} %concatenate.15.place.allowed.marks.facts, bf16[512,384]{1,0:T(8,128)(2,1)S(1)} %shard_map.99.attended, bf16[384,3072]{1,0:T(8,128)(2,1)S(1)} %copy-done, ...), custom_call_target="tpu_custom_call" | custom-call | flops 603979776 | bytes 3538944 | tf_op jit(solution)/shard_map/pallas_call | solution.py:228
  100.0 1.8 %collective-permute-start.19 = (bf16[512,384]{1,0:T(8,128)(2,1)S(1)}, bf16[512,384]{1,0:T(8,128)(2,1)S(1)}, u32[]{:S(2)}, u32[]{:S(2)}) collective-permute-start(bf16[512,384]{1,0:T(8,128)(2,1)S(1)} %get-tuple-element.74), channel_id=1, source_target_pairs={{0,4},{1,5},{2,6},{3,7},{4,0},{5,1},{6,2},{7,3},{8,12},{9,13},{10,... | collective-permute-start | bytes 1179656 | tf_op jit(solution)/shard_map/ppermute | solution.py:24
  101.9 3.2 %collective-permute-start.21 = (bf16[512,384]{1,0:T(8,128)(2,1)S(1)}, bf16[512,384]{1,0:T(8,128)(2,1)S(1)}, u32[]{:S(2)}, u32[]{:S(2)}) collective-permute-start(bf16[512,384]{1,0:T(8,128)(2,1)S(1)} %get-tuple-element.76), channel_id=1, source_target_pairs={{0,1},{1,2},{2,3},{3,0},{4,5},{5,6},{6,7},{7,4},{8,9},{9,10},{10,1... | collective-permute-start | bytes 1179656 | tf_op jit(solution)/shard_map/ppermute | solution.py:20
  105.0 0.6 shard_map.106
  105.6 1.3 %collective-permute-start.22 = (bf16[1,8,896]{2,1,0:T(8,128)(2,1)S(1)}, bf16[1,8,896]{2,1,0:T(8,128)(2,1)S(1)}, u32[]{:S(2)}, u32[]{:S(2)}) collective-permute-start(bf16[1,8,896]{2,1,0:T(8,128)(2,1)S(1)} %get-tuple-element.80), channel_id=1, source_target_pairs={{0,128},{8,136},{16,144},{24,152},{32,160},{40,168},{48,176},{56,1... | collective-permute-start | bytes 43016 | tf_op jit(solution)/shard_map/ppermute | solution.py:33
  106.8 4.0 %collective-permute-done.22.got = bf16[1,8,896]{2,1,0:T(8,128)(2,1)S(1)} collective-permute-done((bf16[1,8,896]{2,1,0:T(8,128)(2,1)S(1)}, bf16[1,8,896]{2,1,0:T(8,128)(2,1)S(1)}, u32[]{:S(2)}, u32[]{:S(2)}) %collective-permute-start.22) | collective-permute-done | bytes 14368 | tf_op jit(solution)/shard_map/ppermute | solution.py:33
  110.9 1.0 shard_map.107
  111.9 0.4 collective-permute-start.23
  112.3 3.5 %collective-permute-done.23.far = bf16[4,8,384]{2,1,0:T(8,128)(2,1)S(1)} collective-permute-done((bf16[4,8,384]{2,1,0:T(8,128)(2,1)S(1)}, bf16[4,8,384]{2,1,0:T(8,128)(2,1)S(1)}, u32[]{:S(2)}, u32[]{:S(2)}) %collective-permute-start.23) | collective-permute-done | bytes 24608 | tf_op jit(solution)/shard_map/ppermute | solution.py:24
  115.9 3.2 %collective-permute-start.25 = (bf16[8,384]{1,0:T(8,128)(2,1)S(1)}, bf16[8,384]{1,0:T(8,128)(2,1)S(1)}, u32[]{:S(2)}, u32[]{:S(2)}) collective-permute-start(bf16[8,384]{1,0:T(8,128)(2,1)S(1)} %get-tuple-element.90), channel_id=1, source_target_pairs={{0,1},{1,2},{2,3},{3,0},{4,5},{5,6},{6,7},{7,4},{8,9},{9,10},{10,1... | collective-permute-start | bytes 18440 | tf_op jit(solution)/shard_map/ppermute | solution.py:20
  119.1 1.6 %shard_map.108 = bf16[512,384]{1,0:T(8,128)(2,1)} custom-call(s32[85]{0:T(128)S(1)} %concatenate.15.place.allowed.marks.facts, bf16[512,384]{1,0:T(8,128)(2,1)S(1)} %get-tuple-element.73.own, bf16[512,384]{1,0:T(8,128)(2,1)S(1)} %collective-permute-done.19.far, bf16[512,384]{1,0:T(8,128)(2,1)S(1)} %collective-permute-done.20.low, ...), custom_call_target="tpu_custom_call" | custom-call | flops 1048576 | bytes 1048576 | tf_op jit(solution)/shard_map/pallas_call | solution.py:316
  120.7 3.5 %collective-permute-done.26.opposite = bf16[8,384]{1,0:T(8,128)(2,1)S(1)} collective-permute-done((bf16[8,384]{1,0:T(8,128)(2,1)S(1)}, bf16[8,384]{1,0:T(8,128)(2,1)S(1)}, u32[]{:S(2)}, u32[]{:S(2)}) %collective-permute-start.26) | collective-permute-done | bytes 6176 | tf_op jit(solution)/shard_map/ppermute | solution.py:20
  124.2 0.7 shard_map.110
  (49 shorter events, 1.8 us)
Async XLA Ops:
  0.6 12.6 %collective-permute-start.2 = (bf16[512,384]{1,0:T(8,128)(2,1)}, bf16[512,384]{1,0:T(8,128)(2,1)S(1)}, u32[]{:S(2)}, u32[]{:S(2)}) collective-permute-start(bf16[512,384]{1,0:T(8,128)(2,1)} %latents.3), channel_id=1, source_target_pairs={{0,3},{1,0},{2,1},{3,2},{4,7},{5,4},{6,5},{7,6},{8,11},{9,8},{10,9... | collective-permute-start | bytes 1179656 | tf_op jit(solution)/shard_map/ppermute | solution.py:20
  1.5 11.8 %collective-permute-start.1 = (bf16[512,384]{1,0:T(8,128)(2,1)}, bf16[512,384]{1,0:T(8,128)(2,1)S(1)}, u32[]{:S(2)}, u32[]{:S(2)}) collective-permute-start(bf16[512,384]{1,0:T(8,128)(2,1)} %latents.3), channel_id=1, source_target_pairs={{0,1},{1,2},{2,3},{3,0},{4,5},{5,6},{6,7},{7,4},{8,9},{9,10},{10,1... | collective-permute-start | bytes 1179656 | tf_op jit(solution)/shard_map/ppermute | solution.py:20
  3.9 10.9 %collective-permute-start = (bf16[512,384]{1,0:T(8,128)(2,1)}, bf16[512,384]{1,0:T(8,128)(2,1)S(1)}, u32[]{:S(2)}, u32[]{:S(2)}) collective-permute-start(bf16[512,384]{1,0:T(8,128)(2,1)} %latents.3), channel_id=1, source_target_pairs={{0,4},{1,5},{2,6},{3,7},{4,0},{5,1},{6,2},{7,3},{8,12},{9,13},{10,... | collective-permute-start | bytes 1179656 | tf_op jit(solution)/shard_map/ppermute | solution.py:24
  13.3 20.9 %copy-start.1 = (bf16[512,384]{1,0:T(8,128)(2,1)S(1)}, bf16[512,384]{1,0:T(8,128)(2,1)}, u32[]{:S(2)}) copy-start(bf16[512,384]{1,0:T(8,128)(2,1)} %latents.3) | copy-start | bytes 1179652
  13.4 20.8 %collective-permute-start.6 = (bf16[832,384]{1,0:T(8,128)(2,1)S(1)}, bf16[832,384]{1,0:T(8,128)(2,1)S(1)}, u32[]{:S(2)}, u32[]{:S(2)}) collective-permute-start(bf16[832,384]{1,0:T(8,128)(2,1)S(1)} %pad_maximum_fusion), channel_id=1, source_target_pairs={{0,4},{1,5},{2,6},{3,7},{4,0},{5,1},{6,2},{7,3},{8,12},{9,13},{10,... | collective-permute-start | bytes 1916936 | tf_op jit(solution)/shard_map/ppermute | solution.py:24
  14.9 15.7 %collective-permute-start.4 = (bf16[352,384]{1,0:T(8,128)(2,1)S(1)}, bf16[352,384]{1,0:T(8,128)(2,1)S(1)}, u32[]{:S(2)}, u32[]{:S(2)}) collective-permute-start(bf16[352,384]{1,0:T(8,128)(2,1)S(1)} %pad_maximum_fusion.1), channel_id=1, source_target_pairs={{0,1},{1,2},{2,3},{3,0},{4,5},{5,6},{6,7},{7,4},{8,9},{9,10},{10,1... | collective-permute-start | bytes 811016 | tf_op jit(solution)/shard_map/ppermute | solution.py:20
  17.9 16.3 %collective-permute-start.3 = (bf16[512,384]{1,0:T(8,128)(2,1)S(1)}, bf16[512,384]{1,0:T(8,128)(2,1)S(1)}, u32[]{:S(2)}, u32[]{:S(2)}) collective-permute-start(bf16[512,384]{1,0:T(8,128)(2,1)S(1)} %collective-permute-done.far), channel_id=1, source_target_pairs={{0,2},{1,3},{2,0},{3,1},{4,6},{5,7},{6,4},{7,5},{8,10},{9,11},{10,... | collective-permute-start | bytes 1179656 | tf_op jit(solution)/shard_map/ppermute | solution.py:20
  18.1 16.2 %collective-permute-start.5 = (bf16[352,384]{1,0:T(8,128)(2,1)S(1)}, bf16[352,384]{1,0:T(8,128)(2,1)S(1)}, u32[]{:S(2)}, u32[]{:S(2)}) collective-permute-start(bf16[352,384]{1,0:T(8,128)(2,1)S(1)} %pad_maximum_fusion.2), channel_id=1, source_target_pairs={{0,3},{1,0},{2,1},{3,2},{4,7},{5,4},{6,5},{7,6},{8,11},{9,8},{10,9... | collective-permute-start | bytes 811016 | tf_op jit(solution)/shard_map/ppermute | solution.py:20
  41.7 14.0 %collective-permute-start.9 = (bf16[2,3,512,128]{3,2,1,0:T(8,128)(2,1)S(1)}, bf16[2,3,512,128]{3,2,1,0:T(8,128)(2,1)S(1)}, u32[]{:S(2)}, u32[]{:S(2)}) collective-permute-start(bf16[2,3,512,128]{3,2,1,0:T(8,128)(2,1)S(1)} %get-tuple-element.48.rest_0_), channel_id=1, source_target_pairs={{0,8},{8,0},{16,24},{24,16},{32,40},{40,32},{48,56},{56,48},{64,72... | collective-permute-start | bytes 2359304 | tf_op jit(solution)/shard_map/ppermute | solution.py:33
  42.0 26.4 %collective-permute-start.8 = (bf16[2,3,512,128]{3,2,1,0:T(8,128)(2,1)S(1)}, bf16[2,3,512,128]{3,2,1,0:T(8,128)(2,1)S(1)}, u32[]{:S(2)}, u32[]{:S(2)}) collective-permute-start(bf16[2,3,512,128]{3,2,1,0:T(8,128)(2,1)S(1)} %get-tuple-element.48.rest_0_), channel_id=1, source_target_pairs={{0,16},{8,24},{16,32},{24,40},{32,48},{40,56},{48,64},{56,72},{64,... | collective-permute-start | bytes 2359304 | tf_op jit(solution)/shard_map/ppermute | solution.py:29
  44.0 24.4 %collective-permute-start.7 = (bf16[2,3,512,128]{3,2,1,0:T(8,128)(2,1)S(1)}, bf16[2,3,512,128]{3,2,1,0:T(8,128)(2,1)S(1)}, u32[]{:S(2)}, u32[]{:S(2)}) collective-permute-start(bf16[2,3,512,128]{3,2,1,0:T(8,128)(2,1)S(1)} %get-tuple-element.48.rest_0_), channel_id=1, source_target_pairs={{0,240},{8,248},{16,0},{24,8},{32,16},{40,24},{48,32},{56,40},{64,... | collective-permute-start | bytes 2359304 | tf_op jit(solution)/shard_map/ppermute | solution.py:29
  50.4 1.9 %copy-start.2 = (bf16[512,3072]{1,0:T(8,128)(2,1)S(1)}, bf16[512,3072]{1,0:T(8,128)(2,1)}, u32[]{:S(2)}) copy-start(bf16[512,3072]{1,0:T(8,128)(2,1)} %get-tuple-element.47.made_at) | copy-start | bytes 9437188
  68.5 2.9 %collective-permute-start.10 = (bf16[2,3,512,128]{3,2,1,0:T(8,128)(2,1)S(1)}, bf16[2,3,512,128]{3,2,1,0:T(8,128)(2,1)S(1)}, u32[]{:S(2)}, u32[]{:S(2)}) collective-permute-start(bf16[2,3,512,128]{3,2,1,0:T(8,128)(2,1)S(1)} %broadcast_select_fusion), channel_id=1, source_target_pairs={{0,8},{8,0},{16,24},{24,16},{32,40},{40,32},{48,56},{56,48},{64,72... | collective-permute-start | bytes 2359304 | tf_op jit(solution)/shard_map/ppermute | solution.py:33
  71.4 2.1 %copy-start = (bf16[384,3072]{1,0:T(8,128)(2,1)S(1)}, bf16[384,3072]{1,0:T(8,128)(2,1)}, u32[]{:S(2)}) copy-start(bf16[384,3072]{1,0:T(8,128)(2,1)} %weight.5) | copy-start | bytes 7077892
  75.2 23.0 %collective-permute-start.14 = (bf16[832,384]{1,0:T(8,128)(2,1)S(1)}, bf16[832,384]{1,0:T(8,128)(2,1)S(1)}, u32[]{:S(2)}, u32[]{:S(2)}) collective-permute-start(bf16[832,384]{1,0:T(8,128)(2,1)S(1)} %get-tuple-element.60), channel_id=1, source_target_pairs={{0,4},{1,5},{2,6},{3,7},{4,0},{5,1},{6,2},{7,3},{8,12},{9,13},{10,... | collective-permute-start | bytes 1916936 | tf_op jit(solution)/shard_map/ppermute | solution.py:24
  76.1 4.1 %collective-permute-start.15 = (bf16[16,8,896]{2,1,0:T(8,128)(2,1)S(1)}, bf16[16,8,896]{2,1,0:T(8,128)(2,1)S(1)}, u32[]{:S(2)}, u32[]{:S(2)}) collective-permute-start(bf16[16,8,896]{2,1,0:T(8,128)(2,1)S(1)} %get-tuple-element.63), channel_id=1, source_target_pairs={{0,8},{8,0},{16,24},{24,16},{32,40},{40,32},{48,56},{56,48},{64,72... | collective-permute-start | bytes 688136 | tf_op jit(solution)/shard_map/ppermute | solution.py:33
  76.6 18.4 %collective-permute-start.11 = (bf16[512,384]{1,0:T(8,128)(2,1)S(1)}, bf16[512,384]{1,0:T(8,128)(2,1)S(1)}, u32[]{:S(2)}, u32[]{:S(2)}) collective-permute-start(bf16[512,384]{1,0:T(8,128)(2,1)S(1)} %get-tuple-element.57), channel_id=1, source_target_pairs={{0,2},{1,3},{2,0},{3,1},{4,6},{5,7},{6,4},{7,5},{8,10},{9,11},{10,... | collective-permute-start | bytes 1179656 | tf_op jit(solution)/shard_map/ppermute | solution.py:20
  77.0 18.0 %collective-permute-start.12 = (bf16[352,384]{1,0:T(8,128)(2,1)S(1)}, bf16[352,384]{1,0:T(8,128)(2,1)S(1)}, u32[]{:S(2)}, u32[]{:S(2)}) collective-permute-start(bf16[352,384]{1,0:T(8,128)(2,1)S(1)} %get-tuple-element.58), channel_id=1, source_target_pairs={{0,3},{1,0},{2,1},{3,2},{4,7},{5,4},{6,5},{7,6},{8,11},{9,8},{10,9... | collective-permute-start | bytes 811016 | tf_op jit(solution)/shard_map/ppermute | solution.py:20
  78.2 16.8 %collective-permute-start.13 = (bf16[352,384]{1,0:T(8,128)(2,1)S(1)}, bf16[352,384]{1,0:T(8,128)(2,1)S(1)}, u32[]{:S(2)}, u32[]{:S(2)}) collective-permute-start(bf16[352,384]{1,0:T(8,128)(2,1)S(1)} %get-tuple-element.59), channel_id=1, source_target_pairs={{0,1},{1,2},{2,3},{3,0},{4,5},{5,6},{6,7},{7,4},{8,9},{9,10},{10,1... | collective-permute-start | bytes 811016 | tf_op jit(solution)/shard_map/ppermute | solution.py:20
  80.9 4.9 %collective-permute-start.16 = (bf16[8,8,896]{2,1,0:T(8,128)(2,1)S(1)}, bf16[8,8,896]{2,1,0:T(8,128)(2,1)S(1)}, u32[]{:S(2)}, u32[]{:S(2)}) collective-permute-start(bf16[8,8,896]{2,1,0:T(8,128)(2,1)S(1)} %get-tuple-element.65), channel_id=1, source_target_pairs={{0,16},{8,24},{16,0},{24,8},{32,48},{40,56},{48,32},{56,40},{64,80... | collective-permute-start | bytes 344072 | tf_op jit(solution)/shard_map/ppermute | solution.py:33
  86.3 5.3 %collective-permute-start.17 = (bf16[4,8,896]{2,1,0:T(8,128)(2,1)S(1)}, bf16[4,8,896]{2,1,0:T(8,128)(2,1)S(1)}, u32[]{:S(2)}, u32[]{:S(2)}) collective-permute-start(bf16[4,8,896]{2,1,0:T(8,128)(2,1)S(1)} %get-tuple-element.67), channel_id=1, source_target_pairs={{0,32},{8,40},{16,48},{24,56},{32,0},{40,8},{48,16},{56,24},{64,96... | collective-permute-start | bytes 172040 | tf_op jit(solution)/shard_map/ppermute | solution.py:33
  92.1 6.1 %collective-permute-start.18 = (bf16[2,8,896]{2,1,0:T(8,128)(2,1)S(1)}, bf16[2,8,896]{2,1,0:T(8,128)(2,1)S(1)}, u32[]{:S(2)}, u32[]{:S(2)}) collective-permute-start(bf16[2,8,896]{2,1,0:T(8,128)(2,1)S(1)} %get-tuple-element.68), channel_id=1, source_target_pairs={{0,96},{8,104},{16,112},{24,120},{32,64},{40,72},{48,80},{56,88},{... | collective-permute-start | bytes 86024 | tf_op jit(solution)/shard_map/ppermute | solution.py:33
  100.0 19.1 %copy-start.3 = (bf16[50,384]{1,0:T(8,128)(2,1)S(1)}, bf16[50,384]{1,0:T(8,128)(2,1)}, u32[]{:S(2)}) copy-start(bf16[50,384]{1,0:T(8,128)(2,1)} %gates.3) | copy-start | bytes 115204
  100.0 15.8 %collective-permute-start.19 = (bf16[512,384]{1,0:T(8,128)(2,1)S(1)}, bf16[512,384]{1,0:T(8,128)(2,1)S(1)}, u32[]{:S(2)}, u32[]{:S(2)}) collective-permute-start(bf16[512,384]{1,0:T(8,128)(2,1)S(1)} %get-tuple-element.74), channel_id=1, source_target_pairs={{0,4},{1,5},{2,6},{3,7},{4,0},{5,1},{6,2},{7,3},{8,12},{9,13},{10,... | collective-permute-start | bytes 1179656 | tf_op jit(solution)/shard_map/ppermute | solution.py:24
  101.8 14.0 %collective-permute-start.20 = (bf16[512,384]{1,0:T(8,128)(2,1)S(1)}, bf16[512,384]{1,0:T(8,128)(2,1)S(1)}, u32[]{:S(2)}, u32[]{:S(2)}) collective-permute-start(bf16[512,384]{1,0:T(8,128)(2,1)S(1)} %get-tuple-element.75), channel_id=1, source_target_pairs={{0,3},{1,0},{2,1},{3,2},{4,7},{5,4},{6,5},{7,6},{8,11},{9,8},{10,9... | collective-permute-start | bytes 1179656 | tf_op jit(solution)/shard_map/ppermute | solution.py:20
  101.9 13.9 %collective-permute-start.21 = (bf16[512,384]{1,0:T(8,128)(2,1)S(1)}, bf16[512,384]{1,0:T(8,128)(2,1)S(1)}, u32[]{:S(2)}, u32[]{:S(2)}) collective-permute-start(bf16[512,384]{1,0:T(8,128)(2,1)S(1)} %get-tuple-element.76), channel_id=1, source_target_pairs={{0,1},{1,2},{2,3},{3,0},{4,5},{5,6},{6,7},{7,4},{8,9},{9,10},{10,1... | collective-permute-start | bytes 1179656 | tf_op jit(solution)/shard_map/ppermute | solution.py:20
  105.6 5.3 %collective-permute-start.22 = (bf16[1,8,896]{2,1,0:T(8,128)(2,1)S(1)}, bf16[1,8,896]{2,1,0:T(8,128)(2,1)S(1)}, u32[]{:S(2)}, u32[]{:S(2)}) collective-permute-start(bf16[1,8,896]{2,1,0:T(8,128)(2,1)S(1)} %get-tuple-element.80), channel_id=1, source_target_pairs={{0,128},{8,136},{16,144},{24,152},{32,160},{40,168},{48,176},{56,1... | collective-permute-start | bytes 43016 | tf_op jit(solution)/shard_map/ppermute | solution.py:33
  111.9 3.9 %collective-permute-start.23 = (bf16[4,8,384]{2,1,0:T(8,128)(2,1)S(1)}, bf16[4,8,384]{2,1,0:T(8,128)(2,1)S(1)}, u32[]{:S(2)}, u32[]{:S(2)}) collective-permute-start(bf16[4,8,384]{2,1,0:T(8,128)(2,1)S(1)} %get-tuple-element.81), channel_id=1, source_target_pairs={{0,4},{1,5},{2,6},{3,7},{4,0},{5,1},{6,2},{7,3},{8,12},{9,13},{10,... | collective-permute-start | bytes 73736 | tf_op jit(solution)/shard_map/ppermute | solution.py:24
  115.8 4.9 %collective-permute-start.24 = (bf16[8,384]{1,0:T(8,128)(2,1)S(1)}, bf16[8,384]{1,0:T(8,128)(2,1)S(1)}, u32[]{:S(2)}, u32[]{:S(2)}) collective-permute-start(bf16[8,384]{1,0:T(8,128)(2,1)S(1)} %get-tuple-element.89), channel_id=1, source_target_pairs={{0,3},{1,0},{2,1},{3,2},{4,7},{5,4},{6,5},{7,6},{8,11},{9,8},{10,9... | collective-permute-start | bytes 18440 | tf_op jit(solution)/shard_map/ppermute | solution.py:20
  115.9 4.8 %collective-permute-start.25 = (bf16[8,384]{1,0:T(8,128)(2,1)S(1)}, bf16[8,384]{1,0:T(8,128)(2,1)S(1)}, u32[]{:S(2)}, u32[]{:S(2)}) collective-permute-start(bf16[8,384]{1,0:T(8,128)(2,1)S(1)} %get-tuple-element.90), channel_id=1, source_target_pairs={{0,1},{1,2},{2,3},{3,0},{4,5},{5,6},{6,7},{7,4},{8,9},{9,10},{10,1... | collective-permute-start | bytes 18440 | tf_op jit(solution)/shard_map/ppermute | solution.py:20
  119.1 5.1 %collective-permute-start.26 = (bf16[8,384]{1,0:T(8,128)(2,1)S(1)}, bf16[8,384]{1,0:T(8,128)(2,1)S(1)}, u32[]{:S(2)}, u32[]{:S(2)}) collective-permute-start(bf16[8,384]{1,0:T(8,128)(2,1)S(1)} %get-tuple-element.91), channel_id=1, source_target_pairs={{0,2},{1,3},{2,0},{3,1},{4,6},{5,7},{6,4},{7,5},{8,10},{9,11},{10,... | collective-permute-start | bytes 18440 | tf_op jit(solution)/shard_map/ppermute | solution.py:20

commit v3 on v2

--- a/solution.py
+++ b/solution.py
@@ -357,7 +357,7 @@
         small += [((source ^ mine) & bit) == 0, (mine & (2 * bit)) != 0]
     facts = jnp.concatenate([jnp.stack([jnp.asarray(v, jnp.int32) for v in slots]), allowed.astype(jnp.int32), jnp.stack([jnp.asarray(v, jnp.int32) for v in small])])
 
-    cut = 96
+    cut = 64
     bf = jnp.bfloat16
     far, low, high = across(latents), ring(latents, 1), ring(latents, -1)
     far_opp = ring(far, 2)

time: 125 us -> 125 us (level)
  transfers between devices with their start and end apart: 27 -> 27, of which waited for: 10 -> 9; matrix products, arithmetic and copies ran while one was open for 4% -> 4% of each run, Pallas kernels for 12% -> 12%
where the time goes in v3:
time: 125 us; the launch traced here: 124 us
  waiting for transfers between devices  47.5 us (38%)
  starting transfers between devices  37.1 us (30%)
  Pallas kernels  28.8 us (23%)
  local copies, waits for them, and re-layouts  5.63 us (5%)
  between operations  4.22 us (3%)
    ppermute x13, waiting for transfers between devices, ring(): lax.ppermute(value, 'mp', [(s, s // 4 * 4 + (s + distance) % 4) for s in...  18.2 us
    ppermute x13, starting transfers between devices, ring(): lax.ppermute(value, 'mp', [(s, s // 4 * 4 + (s + distance) % 4) for s in...  17.5 us
    ppermute x7, waiting for transfers between devices, flipped(): lax.ppermute(value, 'queue', [(s, s ^ bit) for s in range(lax.axis_size('...  16.5 us
    ppermute x2, waiting for transfers between devices, shifted(): lax.ppermute(value, 'queue', [(s, (s + distance) % count) for s in range(...  9.29 us
    ppermute x2, starting transfers between devices, shifted(): lax.ppermute(value, 'queue', [(s, (s + distance) % count) for s in range(...  8.36 us
    pallas_call x3, Pallas kernels, attend(): pl.pallas_call(functools.partial(attend_kernel, (blocks, not state, last)...  8.25 us
    pallas_call x1, Pallas kernels, on_device(): pl.pallas_call(qkv_kernel, out_shape=[jax.ShapeDtypeStruct((2, heads, row...  7.46 us
    ppermute x7, starting transfers between devices, flipped(): lax.ppermute(value, 'queue', [(s, s ^ bit) for s in range(lax.axis_size('...  5.82 us
  transfers between devices with their start and end apart: 27, of which 9 were waited for; matrix products, arithmetic and copies ran while one was open for 4% of the time, Pallas kernels for 12%

profile of v3, /device:TPU:6, one launch (start us, length us, event | category | flops | bytes accessed | tf_op | source)
XLA Modules:
  0.0 124.4 jit_solution(1162439370535854651)
XLA Ops:
  0.6 0.9 collective-permute-start.2
  1.5 2.4 %collective-permute-start.1 = (bf16[512,384]{1,0:T(8,128)(2,1)}, bf16[512,384]{1,0:T(8,128)(2,1)S(1)}, u32[]{:S(2)}, u32[]{:S(2)}) collective-permute-start(bf16[512,384]{1,0:T(8,128)(2,1)} %latents.3), channel_id=1, source_target_pairs={{0,1},{1,2},{2,3},{3,0},{4,5},{5,6},{6,7},{7,4},{8,9},{9,10},{10,1... | collective-permute-start | bytes 1179656 | tf_op jit(solution)/shard_map/ppermute | solution.py:20
  3.9 1.6 %collective-permute-start = (bf16[512,384]{1,0:T(8,128)(2,1)}, bf16[512,384]{1,0:T(8,128)(2,1)S(1)}, u32[]{:S(2)}, u32[]{:S(2)}) collective-permute-start(bf16[512,384]{1,0:T(8,128)(2,1)} %latents.3), channel_id=1, source_target_pairs={{0,4},{1,5},{2,6},{3,7},{4,0},{5,1},{6,2},{7,3},{8,12},{9,13},{10,... | collective-permute-start | bytes 1179656 | tf_op jit(solution)/shard_map/ppermute | solution.py:24
  6.3 0.7 and_convert_fusion
  7.0 1.4 %fusion.2 = (s32[1]{0:T(128)}, s32[1]{0:T(128)}, s32[1]{0:T(128)}) fusion(s32[2]{0:T(128)} %param.9, s32[]{:T(128)S(6)} %select_n.28), kind=kLoop, calls=%fused_computation.14 | loop fusion | bytes 28 | tf_op jit(solution)/shard_map/slice | solution.py:355
  11.1 1.4 %concatenate.15.place.allowed.marks.facts = s32[85]{0:T(128)S(1)} concatenate(s32[1]{0:T(128)} %bitcast, s32[1]{0:T(128)} %bitcast.1, s32[1]{0:T(128)} %bitcast.2, s32[1]{0:T(128)} %bitcast.3, s32[1]{0:T(128)} %bitcast.4, s32[1]{0:T(128)} %bitcast.5, s32[1]{0:T(128)} %bitcast.6, s32[1]{0:T(128)} %bitcast.7, s32[60]{0:T(128)S(1)} %reshape.87, s32[1]{0:T(128)} %bitcast.9, ...), dimensions={0} | concatenate | bytes 680 | tf_op jit(solution)/shard_map/concatenate | solution.py:358
  12.5 0.7 constant_dynamic-slice_fusion.1
  13.4 1.4 %collective-permute-start.6 = (bf16[896,384]{1,0:T(8,128)(2,1)S(1)}, bf16[896,384]{1,0:T(8,128)(2,1)S(1)}, u32[]{:S(2)}, u32[]{:S(2)}) collective-permute-start(bf16[896,384]{1,0:T(8,128)(2,1)S(1)} %pad_maximum_fusion), channel_id=1, source_target_pairs={{0,4},{1,5},{2,6},{3,7},{4,0},{5,1},{6,2},{7,3},{8,12},{9,13},{10,... | collective-permute-start | bytes 2064392 | tf_op jit(solution)/shard_map/ppermute | solution.py:24
  14.9 3.0 %collective-permute-start.4 = (bf16[320,384]{1,0:T(8,128)(2,1)S(1)}, bf16[320,384]{1,0:T(8,128)(2,1)S(1)}, u32[]{:S(2)}, u32[]{:S(2)}) collective-permute-start(bf16[320,384]{1,0:T(8,128)(2,1)S(1)} %pad_maximum_fusion.1), channel_id=1, source_target_pairs={{0,1},{1,2},{2,3},{3,0},{4,5},{5,6},{6,7},{7,4},{8,9},{9,10},{10,1... | collective-permute-start | bytes 737288 | tf_op jit(solution)/shard_map/ppermute | solution.py:20
  18.1 0.9 collective-permute-start.5
  19.0 11.1 %collective-permute-done.4.two_a = bf16[320,384]{1,0:T(8,128)(2,1)S(1)} collective-permute-done((bf16[320,384]{1,0:T(8,128)(2,1)S(1)}, bf16[320,384]{1,0:T(8,128)(2,1)S(1)}, u32[]{:S(2)}, u32[]{:S(2)}) %collective-permute-start.4) | collective-permute-done | bytes 245792 | tf_op jit(solution)/shard_map/ppermute | solution.py:20
  30.1 3.6 %collective-permute-done.5.two_b = bf16[320,384]{1,0:T(8,128)(2,1)S(1)} collective-permute-done((bf16[320,384]{1,0:T(8,128)(2,1)S(1)}, bf16[320,384]{1,0:T(8,128)(2,1)S(1)}, u32[]{:S(2)}, u32[]{:S(2)}) %collective-permute-start.5) | collective-permute-done | bytes 245792 | tf_op jit(solution)/shard_map/ppermute | solution.py:20
  33.7 7.5 %shard_map.95 = (bf16[2,3,512,128]{3,2,1,0:T(8,128)(2,1)S(1)}, bf16[512,3072]{1,0:T(8,128)(2,1)}) custom-call(s32[85]{0:T(128)S(1)} %concatenate.15.place.allowed.marks.facts, bf16[512,384]{1,0:T(8,128)(2,1)S(1)} %copy-done.1, bf16[512,384]{1,0:T(8,128)(2,1)S(1)} %collective-permute-done.far, bf16[512,384]{1,0:T(8,128)(2,1)S(1)} %collective-permute-done.1.low, ...), custom_call_target="tpu_custom_call" | custom-call | flops 2415919104 | bytes 7077888 | tf_op jit(solution)/shard_map/pallas_call | solution.py:369
  41.5 2.0 %collective-permute-start.8 = (bf16[2,3,512,128]{3,2,1,0:T(8,128)(2,1)S(1)}, bf16[2,3,512,128]{3,2,1,0:T(8,128)(2,1)S(1)}, u32[]{:S(2)}, u32[]{:S(2)}) collective-permute-start(bf16[2,3,512,128]{3,2,1,0:T(8,128)(2,1)S(1)} %get-tuple-element.48.rest_0_), channel_id=1, source_target_pairs={{0,16},{8,24},{16,32},{24,40},{32,48},{40,56},{48,64},{56,72},{64,... | collective-permute-start | bytes 2359304 | tf_op jit(solution)/shard_map/ppermute | solution.py:29
  43.5 6.4 %collective-permute-start.7 = (bf16[2,3,512,128]{3,2,1,0:T(8,128)(2,1)S(1)}, bf16[2,3,512,128]{3,2,1,0:T(8,128)(2,1)S(1)}, u32[]{:S(2)}, u32[]{:S(2)}) collective-permute-start(bf16[2,3,512,128]{3,2,1,0:T(8,128)(2,1)S(1)} %get-tuple-element.48.rest_0_), channel_id=1, source_target_pairs={{0,240},{8,248},{16,0},{24,8},{32,16},{40,24},{48,32},{56,40},{64,... | collective-permute-start | bytes 2359304 | tf_op jit(solution)/shard_map/ppermute | solution.py:29
  49.8 1.9 %copy-done.2 = bf16[512,3072]{1,0:T(8,128)(2,1)S(1)} copy-done((bf16[512,3072]{1,0:T(8,128)(2,1)S(1)}, bf16[512,3072]{1,0:T(8,128)(2,1)}, u32[]{:S(2)}) %copy-start.2) | copy-done | bytes 3145752
  51.7 3.5 %shard_map.96.query = bf16[3,512,128]{2,1,0:T(8,128)(2,1)S(1)} custom-call(bf16[512,3072]{1,0:T(8,128)(2,1)S(1)} %copy-done.2, bf16[3,3072,384]{2,1,0:T(8,128)(2,1)} %weight_at.3), custom_call_target="tpu_custom_call" | custom-call | flops 1207959552 | bytes 2359296 | tf_op jit(solution)/shard_map/pallas_call | solution.py:382
  55.2 3.4 %shard_map.97 = (f32[3,512,128]{2,1,0:T(8,128)S(1)}, f32[3,512,256]{2,1,0:T(8,128)S(1)}) custom-call(s32[85]{0:T(128)S(1)} %concatenate.15.place.allowed.marks.facts, bf16[3,512,128]{2,1,0:T(8,128)(2,1)S(1)} %shard_map.96.query, bf16[2,3,512,128]{3,2,1,0:T(8,128)(2,1)S(1)} %get-tuple-element.48.rest_0_, ...), custom_call_target="tpu_custom_call" | custom-call | flops 1207959552 | bytes 1048576 | tf_op jit(solution)/shard_map/pallas_call | solution.py:168
  58.6 9.3 %collective-permute-done.8.rest_1_ = bf16[2,3,512,128]{3,2,1,0:T(8,128)(2,1)S(1)} collective-permute-done((bf16[2,3,512,128]{3,2,1,0:T(8,128)(2,1)S(1)}, bf16[2,3,512,128]{3,2,1,0:T(8,128)(2,1)S(1)}, u32[]{:S(2)}, u32[]{:S(2)}) %collective-permute-start.8) | collective-permute-done | bytes 786464 | tf_op jit(solution)/shard_map/ppermute | solution.py:29
  68.1 2.8 %shard_map.98 = (f32[3,512,128]{2,1,0:T(8,128)S(1)}, f32[3,512,256]{2,1,0:T(8,128)S(1)}) custom-call(s32[85]{0:T(128)S(1)} %concatenate.15.place.allowed.marks.facts, bf16[3,512,128]{2,1,0:T(8,128)(2,1)S(1)} %shard_map.96.query, bf16[2,3,512,128]{3,2,1,0:T(8,128)(2,1)S(1)} %collective-permute-done.7.rest_0_, ...), custom_call_target="tpu_custom_call" | custom-call | flops 1207959552 | bytes 1048576 | tf_op jit(solution)/shard_map/pallas_call | solution.py:168
  70.9 2.1 %shard_map.99.attended = bf16[512,384]{1,0:T(8,128)(2,1)S(1)} custom-call(s32[85]{0:T(128)S(1)} %concatenate.15.place.allowed.marks.facts, bf16[3,512,128]{2,1,0:T(8,128)(2,1)S(1)} %shard_map.96.query, bf16[2,3,512,128]{3,2,1,0:T(8,128)(2,1)S(1)} %collective-permute-done.10.rest_0_, f32[3,512,128]{2,1,0:T(8,128)S(1)} %get-tuple-element.55.rest_1_, ...), custom_call_target="tpu_custom_call" | custom-call | flops 603979776 | bytes 524288 | tf_op jit(solution)/shard_map/pallas_call | solution.py:168
  73.0 1.7 %shard_map.100 = (bf16[512,384]{1,0:T(8,128)(2,1)S(1)}, bf16[320,384]{1,0:T(8,128)(2,1)S(1)}, bf16[320,384]{1,0:T(8,128)(2,1)S(1)}, bf16[896,384]{1,0:T(8,128)(2,1)S(1)}) custom-call(s32[85]{0:T(128)S(1)} %concatenate.15.place.allowed.marks.facts, bf16[512,384]{1,0:T(8,128)(2,1)S(1)} %shard_map.99.attended, bf16[384,3072]{1,0:T(8,128)(2,1)S(1)} %copy-done), custom_call_target="tpu_custom_call" | custom-call | flops 603979776 | bytes 3538944 | tf_op jit(solution)/shard_map/pallas_call | solution.py:228
  74.9 0.7 shard_map.101
  75.6 0.5 collective-permute-start.15
  76.0 0.4 collective-permute-start.11
  76.5 1.2 collective-permute-start.12
  77.7 2.1 %collective-permute-start.13 = (bf16[320,384]{1,0:T(8,128)(2,1)S(1)}, bf16[320,384]{1,0:T(8,128)(2,1)S(1)}, u32[]{:S(2)}, u32[]{:S(2)}) collective-permute-start(bf16[320,384]{1,0:T(8,128)(2,1)S(1)} %get-tuple-element.59), channel_id=1, source_target_pairs={{0,1},{1,2},{2,3},{3,0},{4,5},{5,6},{6,7},{7,4},{8,9},{9,10},{10,1... | collective-permute-start | bytes 737288 | tf_op jit(solution)/shard_map/ppermute | solution.py:20
  79.7 0.6 shard_map.102
  80.4 4.8 %collective-permute-done.16.got = bf16[8,8,896]{2,1,0:T(8,128)(2,1)S(1)} collective-permute-done((bf16[8,8,896]{2,1,0:T(8,128)(2,1)S(1)}, bf16[8,8,896]{2,1,0:T(8,128)(2,1)S(1)}, u32[]{:S(2)}, u32[]{:S(2)}) %collective-permute-start.16) | collective-permute-done | bytes 114720 | tf_op jit(solution)/shard_map/ppermute | solution.py:33
  85.2 0.6 shard_map.103
  85.8 1.0 collective-permute-start.17
  86.8 4.2 %collective-permute-done.17.got = bf16[4,8,896]{2,1,0:T(8,128)(2,1)S(1)} collective-permute-done((bf16[4,8,896]{2,1,0:T(8,128)(2,1)S(1)}, bf16[4,8,896]{2,1,0:T(8,128)(2,1)S(1)}, u32[]{:S(2)}, u32[]{:S(2)}) %collective-permute-start.17) | collective-permute-done | bytes 57376 | tf_op jit(solution)/shard_map/ppermute | solution.py:33
  91.1 0.6 shard_map.104
  91.6 2.6 %collective-permute-start.18 = (bf16[2,8,896]{2,1,0:T(8,128)(2,1)S(1)}, bf16[2,8,896]{2,1,0:T(8,128)(2,1)S(1)}, u32[]{:S(2)}, u32[]{:S(2)}) collective-permute-start(bf16[2,8,896]{2,1,0:T(8,128)(2,1)S(1)} %get-tuple-element.68), channel_id=1, source_target_pairs={{0,96},{8,104},{16,112},{24,120},{32,64},{40,72},{48,80},{56,88},{... | collective-permute-start | bytes 86024 | tf_op jit(solution)/shard_map/ppermute | solution.py:33
  94.2 3.5 %collective-permute-done.18.got = bf16[2,8,896]{2,1,0:T(8,128)(2,1)S(1)} collective-permute-done((bf16[2,8,896]{2,1,0:T(8,128)(2,1)S(1)}, bf16[2,8,896]{2,1,0:T(8,128)(2,1)S(1)}, u32[]{:S(2)}, u32[]{:S(2)}) %collective-permute-start.18) | collective-permute-done | bytes 28704 | tf_op jit(solution)/shard_map/ppermute | solution.py:33
  97.7 1.7 %shard_map.105 = (bf16[512,384]{1,0:T(8,128)(2,1)S(1)}, bf16[512,384]{1,0:T(8,128)(2,1)S(1)}, bf16[512,384]{1,0:T(8,128)(2,1)S(1)}, bf16[512,384]{1,0:T(8,128)(2,1)S(1)}) custom-call(s32[85]{0:T(128)S(1)} %concatenate.15.place.allowed.marks.facts, bf16[512,384]{1,0:T(8,128)(2,1)S(1)} %shard_map.99.attended, bf16[384,3072]{1,0:T(8,128)(2,1)S(1)} %copy-done, ...), custom_call_target="tpu_custom_call" | custom-call | flops 603979776 | bytes 3538944 | tf_op jit(solution)/shard_map/pallas_call | solution.py:228
  99.5 1.8 %collective-permute-start.19 = (bf16[512,384]{1,0:T(8,128)(2,1)S(1)}, bf16[512,384]{1,0:T(8,128)(2,1)S(1)}, u32[]{:S(2)}, u32[]{:S(2)}) collective-permute-start(bf16[512,384]{1,0:T(8,128)(2,1)S(1)} %get-tuple-element.74), channel_id=1, source_target_pairs={{0,4},{1,5},{2,6},{3,7},{4,0},{5,1},{6,2},{7,3},{8,12},{9,13},{10,... | collective-permute-start | bytes 1179656 | tf_op jit(solution)/shard_map/ppermute | solution.py:24
  101.3 3.1 %collective-permute-start.21 = (bf16[512,384]{1,0:T(8,128)(2,1)S(1)}, bf16[512,384]{1,0:T(8,128)(2,1)S(1)}, u32[]{:S(2)}, u32[]{:S(2)}) collective-permute-start(bf16[512,384]{1,0:T(8,128)(2,1)S(1)} %get-tuple-element.76), channel_id=1, source_target_pairs={{0,1},{1,2},{2,3},{3,0},{4,5},{5,6},{6,7},{7,4},{8,9},{9,10},{10,1... | collective-permute-start | bytes 1179656 | tf_op jit(solution)/shard_map/ppermute | solution.py:20
  104.5 0.6 shard_map.106
  105.0 1.3 %collective-permute-start.22 = (bf16[1,8,896]{2,1,0:T(8,128)(2,1)S(1)}, bf16[1,8,896]{2,1,0:T(8,128)(2,1)S(1)}, u32[]{:S(2)}, u32[]{:S(2)}) collective-permute-start(bf16[1,8,896]{2,1,0:T(8,128)(2,1)S(1)} %get-tuple-element.80), channel_id=1, source_target_pairs={{0,128},{8,136},{16,144},{24,152},{32,160},{40,168},{48,176},{56,1... | collective-permute-start | bytes 43016 | tf_op jit(solution)/shard_map/ppermute | solution.py:33
  106.3 4.0 %collective-permute-done.22.got = bf16[1,8,896]{2,1,0:T(8,128)(2,1)S(1)} collective-permute-done((bf16[1,8,896]{2,1,0:T(8,128)(2,1)S(1)}, bf16[1,8,896]{2,1,0:T(8,128)(2,1)S(1)}, u32[]{:S(2)}, u32[]{:S(2)}) %collective-permute-start.22) | collective-permute-done | bytes 14368 | tf_op jit(solution)/shard_map/ppermute | solution.py:33
  110.3 1.0 shard_map.107
  111.3 0.4 collective-permute-start.23
  111.7 3.5 %collective-permute-done.23.far = bf16[4,8,384]{2,1,0:T(8,128)(2,1)S(1)} collective-permute-done((bf16[4,8,384]{2,1,0:T(8,128)(2,1)S(1)}, bf16[4,8,384]{2,1,0:T(8,128)(2,1)S(1)}, u32[]{:S(2)}, u32[]{:S(2)}) %collective-permute-start.23) | collective-permute-done | bytes 24608 | tf_op jit(solution)/shard_map/ppermute | solution.py:24
  115.3 3.2 %collective-permute-start.25 = (bf16[8,384]{1,0:T(8,128)(2,1)S(1)}, bf16[8,384]{1,0:T(8,128)(2,1)S(1)}, u32[]{:S(2)}, u32[]{:S(2)}) collective-permute-start(bf16[8,384]{1,0:T(8,128)(2,1)S(1)} %get-tuple-element.90), channel_id=1, source_target_pairs={{0,1},{1,2},{2,3},{3,0},{4,5},{5,6},{6,7},{7,4},{8,9},{9,10},{10,1... | collective-permute-start | bytes 18440 | tf_op jit(solution)/shard_map/ppermute | solution.py:20
  118.6 1.6 %shard_map.108 = bf16[512,384]{1,0:T(8,128)(2,1)} custom-call(s32[85]{0:T(128)S(1)} %concatenate.15.place.allowed.marks.facts, bf16[512,384]{1,0:T(8,128)(2,1)S(1)} %get-tuple-element.73.own, bf16[512,384]{1,0:T(8,128)(2,1)S(1)} %collective-permute-done.19.far, bf16[512,384]{1,0:T(8,128)(2,1)S(1)} %collective-permute-done.20.low, ...), custom_call_target="tpu_custom_call" | custom-call | flops 1048576 | bytes 1048576 | tf_op jit(solution)/shard_map/pallas_call | solution.py:316
  120.2 3.5 %collective-permute-done.26.opposite = bf16[8,384]{1,0:T(8,128)(2,1)S(1)} collective-permute-done((bf16[8,384]{1,0:T(8,128)(2,1)S(1)}, bf16[8,384]{1,0:T(8,128)(2,1)S(1)}, u32[]{:S(2)}, u32[]{:S(2)}) %collective-permute-start.26) | collective-permute-done | bytes 6176 | tf_op jit(solution)/shard_map/ppermute | solution.py:20
  123.7 0.7 shard_map.110
  (49 shorter events, 1.6 us)
Async XLA Ops:
  0.6 12.6 %collective-permute-start.2 = (bf16[512,384]{1,0:T(8,128)(2,1)}, bf16[512,384]{1,0:T(8,128)(2,1)S(1)}, u32[]{:S(2)}, u32[]{:S(2)}) collective-permute-start(bf16[512,384]{1,0:T(8,128)(2,1)} %latents.3), channel_id=1, source_target_pairs={{0,3},{1,0},{2,1},{3,2},{4,7},{5,4},{6,5},{7,6},{8,11},{9,8},{10,9... | collective-permute-start | bytes 1179656 | tf_op jit(solution)/shard_map/ppermute | solution.py:20
  1.5 11.8 %collective-permute-start.1 = (bf16[512,384]{1,0:T(8,128)(2,1)}, bf16[512,384]{1,0:T(8,128)(2,1)S(1)}, u32[]{:S(2)}, u32[]{:S(2)}) collective-permute-start(bf16[512,384]{1,0:T(8,128)(2,1)} %latents.3), channel_id=1, source_target_pairs={{0,1},{1,2},{2,3},{3,0},{4,5},{5,6},{6,7},{7,4},{8,9},{9,10},{10,1... | collective-permute-start | bytes 1179656 | tf_op jit(solution)/shard_map/ppermute | solution.py:20
  3.9 10.9 %collective-permute-start = (bf16[512,384]{1,0:T(8,128)(2,1)}, bf16[512,384]{1,0:T(8,128)(2,1)S(1)}, u32[]{:S(2)}, u32[]{:S(2)}) collective-permute-start(bf16[512,384]{1,0:T(8,128)(2,1)} %latents.3), channel_id=1, source_target_pairs={{0,4},{1,5},{2,6},{3,7},{4,0},{5,1},{6,2},{7,3},{8,12},{9,13},{10,... | collective-permute-start | bytes 1179656 | tf_op jit(solution)/shard_map/ppermute | solution.py:24
  13.3 20.4 %copy-start.1 = (bf16[512,384]{1,0:T(8,128)(2,1)S(1)}, bf16[512,384]{1,0:T(8,128)(2,1)}, u32[]{:S(2)}) copy-start(bf16[512,384]{1,0:T(8,128)(2,1)} %latents.3) | copy-start | bytes 1179652
  13.4 20.3 %collective-permute-start.6 = (bf16[896,384]{1,0:T(8,128)(2,1)S(1)}, bf16[896,384]{1,0:T(8,128)(2,1)S(1)}, u32[]{:S(2)}, u32[]{:S(2)}) collective-permute-start(bf16[896,384]{1,0:T(8,128)(2,1)S(1)} %pad_maximum_fusion), channel_id=1, source_target_pairs={{0,4},{1,5},{2,6},{3,7},{4,0},{5,1},{6,2},{7,3},{8,12},{9,13},{10,... | collective-permute-start | bytes 2064392 | tf_op jit(solution)/shard_map/ppermute | solution.py:24
  14.9 15.2 %collective-permute-start.4 = (bf16[320,384]{1,0:T(8,128)(2,1)S(1)}, bf16[320,384]{1,0:T(8,128)(2,1)S(1)}, u32[]{:S(2)}, u32[]{:S(2)}) collective-permute-start(bf16[320,384]{1,0:T(8,128)(2,1)S(1)} %pad_maximum_fusion.1), channel_id=1, source_target_pairs={{0,1},{1,2},{2,3},{3,0},{4,5},{5,6},{6,7},{7,4},{8,9},{9,10},{10,1... | collective-permute-start | bytes 737288 | tf_op jit(solution)/shard_map/ppermute | solution.py:20
  17.9 15.8 %collective-permute-start.3 = (bf16[512,384]{1,0:T(8,128)(2,1)S(1)}, bf16[512,384]{1,0:T(8,128)(2,1)S(1)}, u32[]{:S(2)}, u32[]{:S(2)}) collective-permute-start(bf16[512,384]{1,0:T(8,128)(2,1)S(1)} %collective-permute-done.far), channel_id=1, source_target_pairs={{0,2},{1,3},{2,0},{3,1},{4,6},{5,7},{6,4},{7,5},{8,10},{9,11},{10,... | collective-permute-start | bytes 1179656 | tf_op jit(solution)/shard_map/ppermute | solution.py:20
  18.1 15.7 %collective-permute-start.5 = (bf16[320,384]{1,0:T(8,128)(2,1)S(1)}, bf16[320,384]{1,0:T(8,128)(2,1)S(1)}, u32[]{:S(2)}, u32[]{:S(2)}) collective-permute-start(bf16[320,384]{1,0:T(8,128)(2,1)S(1)} %pad_maximum_fusion.2), channel_id=1, source_target_pairs={{0,3},{1,0},{2,1},{3,2},{4,7},{5,4},{6,5},{7,6},{8,11},{9,8},{10,9... | collective-permute-start | bytes 737288 | tf_op jit(solution)/shard_map/ppermute | solution.py:20
  41.2 14.0 %collective-permute-start.9 = (bf16[2,3,512,128]{3,2,1,0:T(8,128)(2,1)S(1)}, bf16[2,3,512,128]{3,2,1,0:T(8,128)(2,1)S(1)}, u32[]{:S(2)}, u32[]{:S(2)}) collective-permute-start(bf16[2,3,512,128]{3,2,1,0:T(8,128)(2,1)S(1)} %get-tuple-element.48.rest_0_), channel_id=1, source_target_pairs={{0,8},{8,0},{16,24},{24,16},{32,40},{40,32},{48,56},{56,48},{64,72... | collective-permute-start | bytes 2359304 | tf_op jit(solution)/shard_map/ppermute | solution.py:33
  41.5 26.4 %collective-permute-start.8 = (bf16[2,3,512,128]{3,2,1,0:T(8,128)(2,1)S(1)}, bf16[2,3,512,128]{3,2,1,0:T(8,128)(2,1)S(1)}, u32[]{:S(2)}, u32[]{:S(2)}) collective-permute-start(bf16[2,3,512,128]{3,2,1,0:T(8,128)(2,1)S(1)} %get-tuple-element.48.rest_0_), channel_id=1, source_target_pairs={{0,16},{8,24},{16,32},{24,40},{32,48},{40,56},{48,64},{56,72},{64,... | collective-permute-start | bytes 2359304 | tf_op jit(solution)/shard_map/ppermute | solution.py:29
  43.5 24.4 %collective-permute-start.7 = (bf16[2,3,512,128]{3,2,1,0:T(8,128)(2,1)S(1)}, bf16[2,3,512,128]{3,2,1,0:T(8,128)(2,1)S(1)}, u32[]{:S(2)}, u32[]{:S(2)}) collective-permute-start(bf16[2,3,512,128]{3,2,1,0:T(8,128)(2,1)S(1)} %get-tuple-element.48.rest_0_), channel_id=1, source_target_pairs={{0,240},{8,248},{16,0},{24,8},{32,16},{40,24},{48,32},{56,40},{64,... | collective-permute-start | bytes 2359304 | tf_op jit(solution)/shard_map/ppermute | solution.py:29
  49.8 1.9 %copy-start.2 = (bf16[512,3072]{1,0:T(8,128)(2,1)S(1)}, bf16[512,3072]{1,0:T(8,128)(2,1)}, u32[]{:S(2)}) copy-start(bf16[512,3072]{1,0:T(8,128)(2,1)} %get-tuple-element.47.made_at) | copy-start | bytes 9437188
  68.0 2.9 %collective-permute-start.10 = (bf16[2,3,512,128]{3,2,1,0:T(8,128)(2,1)S(1)}, bf16[2,3,512,128]{3,2,1,0:T(8,128)(2,1)S(1)}, u32[]{:S(2)}, u32[]{:S(2)}) collective-permute-start(bf16[2,3,512,128]{3,2,1,0:T(8,128)(2,1)S(1)} %broadcast_select_fusion), channel_id=1, source_target_pairs={{0,8},{8,0},{16,24},{24,16},{32,40},{40,32},{48,56},{56,48},{64,72... | collective-permute-start | bytes 2359304 | tf_op jit(solution)/shard_map/ppermute | solution.py:33
  70.8 2.1 %copy-start = (bf16[384,3072]{1,0:T(8,128)(2,1)S(1)}, bf16[384,3072]{1,0:T(8,128)(2,1)}, u32[]{:S(2)}) copy-start(bf16[384,3072]{1,0:T(8,128)(2,1)} %weight.5) | copy-start | bytes 7077892
  74.7 23.0 %collective-permute-start.14 = (bf16[896,384]{1,0:T(8,128)(2,1)S(1)}, bf16[896,384]{1,0:T(8,128)(2,1)S(1)}, u32[]{:S(2)}, u32[]{:S(2)}) collective-permute-start(bf16[896,384]{1,0:T(8,128)(2,1)S(1)} %get-tuple-element.60), channel_id=1, source_target_pairs={{0,4},{1,5},{2,6},{3,7},{4,0},{5,1},{6,2},{7,3},{8,12},{9,13},{10,... | collective-permute-start | bytes 2064392 | tf_op jit(solution)/shard_map/ppermute | solution.py:24
  75.6 4.1 %collective-permute-start.15 = (bf16[16,8,896]{2,1,0:T(8,128)(2,1)S(1)}, bf16[16,8,896]{2,1,0:T(8,128)(2,1)S(1)}, u32[]{:S(2)}, u32[]{:S(2)}) collective-permute-start(bf16[16,8,896]{2,1,0:T(8,128)(2,1)S(1)} %get-tuple-element.63), channel_id=1, source_target_pairs={{0,8},{8,0},{16,24},{24,16},{32,40},{40,32},{48,56},{56,48},{64,72... | collective-permute-start | bytes 688136 | tf_op jit(solution)/shard_map/ppermute | solution.py:33
  76.0 18.2 %collective-permute-start.11 = (bf16[512,384]{1,0:T(8,128)(2,1)S(1)}, bf16[512,384]{1,0:T(8,128)(2,1)S(1)}, u32[]{:S(2)}, u32[]{:S(2)}) collective-permute-start(bf16[512,384]{1,0:T(8,128)(2,1)S(1)} %get-tuple-element.57), channel_id=1, source_target_pairs={{0,2},{1,3},{2,0},{3,1},{4,6},{5,7},{6,4},{7,5},{8,10},{9,11},{10,... | collective-permute-start | bytes 1179656 | tf_op jit(solution)/shard_map/ppermute | solution.py:20
  76.5 17.8 %collective-permute-start.12 = (bf16[320,384]{1,0:T(8,128)(2,1)S(1)}, bf16[320,384]{1,0:T(8,128)(2,1)S(1)}, u32[]{:S(2)}, u32[]{:S(2)}) collective-permute-start(bf16[320,384]{1,0:T(8,128)(2,1)S(1)} %get-tuple-element.58), channel_id=1, source_target_pairs={{0,3},{1,0},{2,1},{3,2},{4,7},{5,4},{6,5},{7,6},{8,11},{9,8},{10,9... | collective-permute-start | bytes 737288 | tf_op jit(solution)/shard_map/ppermute | solution.py:20
  77.7 16.6 %collective-permute-start.13 = (bf16[320,384]{1,0:T(8,128)(2,1)S(1)}, bf16[320,384]{1,0:T(8,128)(2,1)S(1)}, u32[]{:S(2)}, u32[]{:S(2)}) collective-permute-start(bf16[320,384]{1,0:T(8,128)(2,1)S(1)} %get-tuple-element.59), channel_id=1, source_target_pairs={{0,1},{1,2},{2,3},{3,0},{4,5},{5,6},{6,7},{7,4},{8,9},{9,10},{10,1... | collective-permute-start | bytes 737288 | tf_op jit(solution)/shard_map/ppermute | solution.py:20
  80.3 4.9 %collective-permute-start.16 = (bf16[8,8,896]{2,1,0:T(8,128)(2,1)S(1)}, bf16[8,8,896]{2,1,0:T(8,128)(2,1)S(1)}, u32[]{:S(2)}, u32[]{:S(2)}) collective-permute-start(bf16[8,8,896]{2,1,0:T(8,128)(2,1)S(1)} %get-tuple-element.65), channel_id=1, source_target_pairs={{0,16},{8,24},{16,0},{24,8},{32,48},{40,56},{48,32},{56,40},{64,80... | collective-permute-start | bytes 344072 | tf_op jit(solution)/shard_map/ppermute | solution.py:33
  85.8 5.3 %collective-permute-start.17 = (bf16[4,8,896]{2,1,0:T(8,128)(2,1)S(1)}, bf16[4,8,896]{2,1,0:T(8,128)(2,1)S(1)}, u32[]{:S(2)}, u32[]{:S(2)}) collective-permute-start(bf16[4,8,896]{2,1,0:T(8,128)(2,1)S(1)} %get-tuple-element.67), channel_id=1, source_target_pairs={{0,32},{8,40},{16,48},{24,56},{32,0},{40,8},{48,16},{56,24},{64,96... | collective-permute-start | bytes 172040 | tf_op jit(solution)/shard_map/ppermute | solution.py:33
  91.6 6.1 %collective-permute-start.18 = (bf16[2,8,896]{2,1,0:T(8,128)(2,1)S(1)}, bf16[2,8,896]{2,1,0:T(8,128)(2,1)S(1)}, u32[]{:S(2)}, u32[]{:S(2)}) collective-permute-start(bf16[2,8,896]{2,1,0:T(8,128)(2,1)S(1)} %get-tuple-element.68), channel_id=1, source_target_pairs={{0,96},{8,104},{16,112},{24,120},{32,64},{40,72},{48,80},{56,88},{... | collective-permute-start | bytes 86024 | tf_op jit(solution)/shard_map/ppermute | solution.py:33
  99.4 19.1 %copy-start.3 = (bf16[50,384]{1,0:T(8,128)(2,1)S(1)}, bf16[50,384]{1,0:T(8,128)(2,1)}, u32[]{:S(2)}) copy-start(bf16[50,384]{1,0:T(8,128)(2,1)} %gates.3) | copy-start | bytes 115204
  99.5 15.8 %collective-permute-start.19 = (bf16[512,384]{1,0:T(8,128)(2,1)S(1)}, bf16[512,384]{1,0:T(8,128)(2,1)S(1)}, u32[]{:S(2)}, u32[]{:S(2)}) collective-permute-start(bf16[512,384]{1,0:T(8,128)(2,1)S(1)} %get-tuple-element.74), channel_id=1, source_target_pairs={{0,4},{1,5},{2,6},{3,7},{4,0},{5,1},{6,2},{7,3},{8,12},{9,13},{10,... | collective-permute-start | bytes 1179656 | tf_op jit(solution)/shard_map/ppermute | solution.py:24
  101.2 14.0 %collective-permute-start.20 = (bf16[512,384]{1,0:T(8,128)(2,1)S(1)}, bf16[512,384]{1,0:T(8,128)(2,1)S(1)}, u32[]{:S(2)}, u32[]{:S(2)}) collective-permute-start(bf16[512,384]{1,0:T(8,128)(2,1)S(1)} %get-tuple-element.75), channel_id=1, source_target_pairs={{0,3},{1,0},{2,1},{3,2},{4,7},{5,4},{6,5},{7,6},{8,11},{9,8},{10,9... | collective-permute-start | bytes 1179656 | tf_op jit(solution)/shard_map/ppermute | solution.py:20
  101.3 13.9 %collective-permute-start.21 = (bf16[512,384]{1,0:T(8,128)(2,1)S(1)}, bf16[512,384]{1,0:T(8,128)(2,1)S(1)}, u32[]{:S(2)}, u32[]{:S(2)}) collective-permute-start(bf16[512,384]{1,0:T(8,128)(2,1)S(1)} %get-tuple-element.76), channel_id=1, source_target_pairs={{0,1},{1,2},{2,3},{3,0},{4,5},{5,6},{6,7},{7,4},{8,9},{9,10},{10,1... | collective-permute-start | bytes 1179656 | tf_op jit(solution)/shard_map/ppermute | solution.py:20
  105.0 5.3 %collective-permute-start.22 = (bf16[1,8,896]{2,1,0:T(8,128)(2,1)S(1)}, bf16[1,8,896]{2,1,0:T(8,128)(2,1)S(1)}, u32[]{:S(2)}, u32[]{:S(2)}) collective-permute-start(bf16[1,8,896]{2,1,0:T(8,128)(2,1)S(1)} %get-tuple-element.80), channel_id=1, source_target_pairs={{0,128},{8,136},{16,144},{24,152},{32,160},{40,168},{48,176},{56,1... | collective-permute-start | bytes 43016 | tf_op jit(solution)/shard_map/ppermute | solution.py:33
  111.3 3.9 %collective-permute-start.23 = (bf16[4,8,384]{2,1,0:T(8,128)(2,1)S(1)}, bf16[4,8,384]{2,1,0:T(8,128)(2,1)S(1)}, u32[]{:S(2)}, u32[]{:S(2)}) collective-permute-start(bf16[4,8,384]{2,1,0:T(8,128)(2,1)S(1)} %get-tuple-element.81), channel_id=1, source_target_pairs={{0,4},{1,5},{2,6},{3,7},{4,0},{5,1},{6,2},{7,3},{8,12},{9,13},{10,... | collective-permute-start | bytes 73736 | tf_op jit(solution)/shard_map/ppermute | solution.py:24
  115.3 4.9 %collective-permute-start.24 = (bf16[8,384]{1,0:T(8,128)(2,1)S(1)}, bf16[8,384]{1,0:T(8,128)(2,1)S(1)}, u32[]{:S(2)}, u32[]{:S(2)}) collective-permute-start(bf16[8,384]{1,0:T(8,128)(2,1)S(1)} %get-tuple-element.89), channel_id=1, source_target_pairs={{0,3},{1,0},{2,1},{3,2},{4,7},{5,4},{6,5},{7,6},{8,11},{9,8},{10,9... | collective-permute-start | bytes 18440 | tf_op jit(solution)/shard_map/ppermute | solution.py:20
  115.3 4.8 %collective-permute-start.25 = (bf16[8,384]{1,0:T(8,128)(2,1)S(1)}, bf16[8,384]{1,0:T(8,128)(2,1)S(1)}, u32[]{:S(2)}, u32[]{:S(2)}) collective-permute-start(bf16[8,384]{1,0:T(8,128)(2,1)S(1)} %get-tuple-element.90), channel_id=1, source_target_pairs={{0,1},{1,2},{2,3},{3,0},{4,5},{5,6},{6,7},{7,4},{8,9},{9,10},{10,1... | collective-permute-start | bytes 18440 | tf_op jit(solution)/shard_map/ppermute | solution.py:20
  118.6 5.1 %collective-permute-start.26 = (bf16[8,384]{1,0:T(8,128)(2,1)S(1)}, bf16[8,384]{1,0:T(8,128)(2,1)S(1)}, u32[]{:S(2)}, u32[]{:S(2)}) collective-permute-start(bf16[8,384]{1,0:T(8,128)(2,1)S(1)} %get-tuple-element.91), channel_id=1, source_target_pairs={{0,2},{1,3},{2,0},{3,1},{4,6},{5,7},{6,4},{7,5},{8,10},{9,11},{10,... | collective-permute-start | bytes 18440 | tf_op jit(solution)/shard_map/ppermute | solution.py:20

commit v4 on v3

--- a/solution.py
+++ b/solution.py
@@ -45,14 +45,14 @@
     return pl.BlockSpec(memory_space=pltpu.SMEM)
 
 
-def qkv_kernel(place, own_at, far, low, high, far_opp, two_a, two_b, two_c, modul, weight_at, kv, made, own, weight, sems):
+def product_kernel(first, place, own_at, far, low, high, far_opp, two_a, two_b, two_c, modul, weight_at, out, made, own, weight, sems):
     rows, part = own.shape
     half = rows // 2
-    width = weight.shape[1]
+    width = weight.shape[0]
     cut = two_a.shape[0] - half
     copies = [
         pltpu.make_async_copy(source, target, sems.at[i])
-        for i, (source, target) in enumerate(((own_at, own), (weight_at.at[1], weight.at[0]), (weight_at.at[2], weight.at[1])))
+        for i, (source, target) in enumerate(((own_at, own), *((weight_at.at[first + which], weight.at[:, which * part : (which + 1) * part]) for which in range(out.shape[0]))))
     ]
     for copy in copies:
         copy.start()
@@ -88,24 +88,33 @@
                 scale = modul[frame, 1:2, columns].astype(jnp.float32) + 1.0
                 value = (load(i) - mean) * inverse * scale + shift
                 made[at : at + chunk, columns] = value.astype(jnp.bfloat16)
-        left = made[frame * half : (frame + 1) * half, :]
-        for which in range(2):
-            if frame == 0:
-                copies[1 + which].wait()
-            result = jnp.dot(left, weight[which], preferred_element_type=jnp.float32).astype(jnp.bfloat16)
-            for h in range(3):
-                kv[which, h, frame * half : (frame + 1) * half, :] = result[:, h * 128 : (h + 1) * 128]
-
-
-def query_kernel(made_at, weight_at, query, made, weight, sems):
-    copies = [pltpu.make_async_copy(weight_at.at[0], weight, sems.at[0]), pltpu.make_async_copy(made_at, made, sems.at[1])]
-    for copy in copies:
-        copy.start()
-    for copy in copies:
+    for copy in copies[1:]:
         copy.wait()
     result = jnp.dot(made[...], weight[...], preferred_element_type=jnp.float32).astype(jnp.bfloat16)
-    for h in range(3):
-        query[h] = result[:, h * 128 : (h + 1) * 128]
+    for which in range(out.shape[0]):
+        for h in range(3):
+            at = which * part + h * 128
+            out[which, h] = result[:, at : at + 128]
+
+
+def products(first, count, heads, facts, latents, blocks, modul, weight):
+    rows, part = latents.shape
+    width = weight.shape[1]
+    bf = jnp.bfloat16
+    return pl.pallas_call(
+        functools.partial(product_kernel, first),
+        out_shape=jax.ShapeDtypeStruct((count, heads, rows, part // heads), bf),
+        in_specs=[smem(), anywhere()] + [vmem()] * 8 + [anywhere()],
+        out_specs=vmem(),
+        scratch_shapes=[
+            pltpu.VMEM((rows, width), bf),
+            pltpu.VMEM((rows, part), bf),
+            pltpu.VMEM((width, count * part), bf),
+            pltpu.SemaphoreType.DMA((1 + count,)),
+        ],
+        compiler_params=pltpu.CompilerParams(vmem_limit_bytes=VMEM_LIMIT),
+        cost_estimate=pl.CostEstimate(flops=2 * count * rows * width * part, bytes_accessed=2 * (count + 1) * width * part, transcendentals=0),
+    )(facts, latents, *blocks, modul, weight)
 
 
 def attend_kernel(shape, allowed, query, *rest):
@@ -366,28 +375,13 @@
     two_c = across(jnp.concatenate([low[cut:], high[: rows - cut]]))
 
     modul = jnp.concatenate([lax.dynamic_index_in_dim(mod_table, step_index[f] - 1, 0) for f in range(frames)])
-    kv, modulated = pl.pallas_call(
-        qkv_kernel,
-        out_shape=[jax.ShapeDtypeStruct((2, heads, rows, size), bf), jax.ShapeDtypeStruct((rows, width), bf)],
-        in_specs=[smem(), anywhere()] + [vmem()] * 8 + [anywhere()],
-        out_specs=[vmem()] * 2,
-        scratch_shapes=[pltpu.VMEM((rows, part), bf), pltpu.VMEM((2, width, part), bf), pltpu.SemaphoreType.DMA((3,))],
-        compiler_params=pltpu.CompilerParams(vmem_limit_bytes=VMEM_LIMIT),
-        cost_estimate=pl.CostEstimate(flops=4 * rows * width * part, bytes_accessed=6 * width * part, transcendentals=0),
-    )(facts, latents, far, low, high, far_opp, two_a, two_b, two_c, modul, qkv_weight)
+    blocks = (far, low, high, far_opp, two_a, two_b, two_c)
+    kv = products(1, 2, heads, facts, latents, blocks, modul, qkv_weight)
 
     upper2 = shifted(kv, -2)
     lower2 = shifted(kv, 2)
     partner = flipped(kv, 1)
-    query = pl.pallas_call(
-        query_kernel,
-        out_shape=jax.ShapeDtypeStruct((heads, rows, size), bf),
-        in_specs=[anywhere()] * 2,
-        out_specs=vmem(),
-        scratch_shapes=[pltpu.VMEM((rows, width), bf), pltpu.VMEM((width, part), bf), pltpu.SemaphoreType.DMA((2,))],
-        compiler_params=pltpu.CompilerParams(vmem_limit_bytes=VMEM_LIMIT),
-        cost_estimate=pl.CostEstimate(flops=2 * rows * width * part, bytes_accessed=2 * width * part, transcendentals=0),
-    )(modulated, qkv_weight)
+    query = products(0, 1, heads, facts, latents, blocks, modul, qkv_weight)[0]
 
     state = attend((2, 5), facts, query, (kv, partner))
     upper2, lower2, *state = lax.optimization_barrier((upper2, lower2, *state))

time: 125 us -> 124 us (level)
  local copies, waits for them, and re-layouts: 5.63 us -> 3.67 us
    unnamed x8 -> x6, local copies, waits for them, and re-layouts: 1.91 us -> 0.02 us
  transfers between devices with their start and end apart: 27 -> 27, of which waited for: 9 -> 9; matrix products, arithmetic and copies ran while one was open for 4% -> 4% of each run, Pallas kernels for 12% -> 14%
where the time goes in v4:
time: 124 us; the launch traced here: 123 us
  waiting for transfers between devices  47.2 us (38%)
  starting transfers between devices  37.4 us (30%)
  Pallas kernels  29.7 us (24%)
  between operations  4.18 us (3%)
  local copies, waits for them, and re-layouts  3.67 us (3%)
    ppermute x13, waiting for transfers between devices, ring(): lax.ppermute(value, 'mp', [(s, s // 4 * 4 + (s + distance) % 4) for s in...  18.2 us
    ppermute x13, starting transfers between devices, ring(): lax.ppermute(value, 'mp', [(s, s // 4 * 4 + (s + distance) % 4) for s in...  17.6 us
    ppermute x7, waiting for transfers between devices, flipped(): lax.ppermute(value, 'queue', [(s, s ^ bit) for s in range(lax.axis_size('...  16.5 us
    pallas_call x2, Pallas kernels, products(): pl.pallas_call(functools.partial(product_kernel, first), out_shape=jax.Sh...  11.7 us
    ppermute x2, waiting for transfers between devices, shifted(): lax.ppermute(value, 'queue', [(s, (s + distance) % count) for s in range(...  8.98 us
    ppermute x2, starting transfers between devices, shifted(): lax.ppermute(value, 'queue', [(s, (s + distance) % count) for s in range(...  8.53 us
    pallas_call x3, Pallas kernels, attend(): pl.pallas_call(functools.partial(attend_kernel, (blocks, not state, last)...  8.31 us
    ppermute x5, starting transfers between devices, across(): return lax.ppermute(value, 'mp', [(s, s ^ 4) for s in range(8)])  5.71 us
  transfers between devices with their start and end apart: 27, of which 9 were waited for; matrix products, arithmetic and copies ran while one was open for 4% of the time, Pallas kernels for 14%

profile of v4, /device:TPU:6, one launch (start us, length us, event | category | flops | bytes accessed | tf_op | source)
XLA Modules:
  0.0 123.3 jit_solution(695774525814287557)
XLA Ops:
  0.6 0.9 collective-permute-start.2
  1.5 2.4 %collective-permute-start.1 = (bf16[512,384]{1,0:T(8,128)(2,1)}, bf16[512,384]{1,0:T(8,128)(2,1)S(1)}, u32[]{:S(2)}, u32[]{:S(2)}) collective-permute-start(bf16[512,384]{1,0:T(8,128)(2,1)} %latents.3), channel_id=1, source_target_pairs={{0,1},{1,2},{2,3},{3,0},{4,5},{5,6},{6,7},{7,4},{8,9},{9,10},{10,1... | collective-permute-start | bytes 1179656 | tf_op jit(solution)/shard_map/ppermute | solution.py:20
  3.9 1.6 %collective-permute-start = (bf16[512,384]{1,0:T(8,128)(2,1)}, bf16[512,384]{1,0:T(8,128)(2,1)S(1)}, u32[]{:S(2)}, u32[]{:S(2)}) collective-permute-start(bf16[512,384]{1,0:T(8,128)(2,1)} %latents.3), channel_id=1, source_target_pairs={{0,4},{1,5},{2,6},{3,7},{4,0},{5,1},{6,2},{7,3},{8,12},{9,13},{10,... | collective-permute-start | bytes 1179656 | tf_op jit(solution)/shard_map/ppermute | solution.py:24
  6.3 0.7 and_convert_fusion
  7.0 1.4 %fusion.2 = (s32[1]{0:T(128)}, s32[1]{0:T(128)}, s32[1]{0:T(128)}) fusion(s32[2]{0:T(128)} %param.9, s32[]{:T(128)S(6)} %select_n.28), kind=kLoop, calls=%fused_computation.14 | loop fusion | bytes 28 | tf_op jit(solution)/shard_map/slice | solution.py:364
  11.1 1.3 %concatenate.15.place.allowed.marks.facts = s32[85]{0:T(128)S(1)} concatenate(s32[1]{0:T(128)} %bitcast, s32[1]{0:T(128)} %bitcast.1, s32[1]{0:T(128)} %bitcast.2, s32[1]{0:T(128)} %bitcast.3, s32[1]{0:T(128)} %bitcast.4, s32[1]{0:T(128)} %bitcast.5, s32[1]{0:T(128)} %bitcast.6, s32[1]{0:T(128)} %bitcast.7, s32[60]{0:T(128)S(1)} %reshape.87, s32[1]{0:T(128)} %bitcast.9, ...), dimensions={0} | concatenate | bytes 680 | tf_op jit(solution)/shard_map/concatenate | solution.py:367
  12.4 0.7 constant_dynamic-slice_fusion.1
  13.3 1.5 %collective-permute-start.6 = (bf16[896,384]{1,0:T(8,128)(2,1)S(1)}, bf16[896,384]{1,0:T(8,128)(2,1)S(1)}, u32[]{:S(2)}, u32[]{:S(2)}) collective-permute-start(bf16[896,384]{1,0:T(8,128)(2,1)S(1)} %pad_maximum_fusion), channel_id=1, source_target_pairs={{0,4},{1,5},{2,6},{3,7},{4,0},{5,1},{6,2},{7,3},{8,12},{9,13},{10,... | collective-permute-start | bytes 2064392 | tf_op jit(solution)/shard_map/ppermute | solution.py:24
  14.9 3.0 %collective-permute-start.4 = (bf16[320,384]{1,0:T(8,128)(2,1)S(1)}, bf16[320,384]{1,0:T(8,128)(2,1)S(1)}, u32[]{:S(2)}, u32[]{:S(2)}) collective-permute-start(bf16[320,384]{1,0:T(8,128)(2,1)S(1)} %pad_maximum_fusion.1), channel_id=1, source_target_pairs={{0,1},{1,2},{2,3},{3,0},{4,5},{5,6},{6,7},{7,4},{8,9},{9,10},{10,1... | collective-permute-start | bytes 737288 | tf_op jit(solution)/shard_map/ppermute | solution.py:20
  18.1 0.9 collective-permute-start.5
  19.0 11.1 %collective-permute-done.4.two_a = bf16[320,384]{1,0:T(8,128)(2,1)S(1)} collective-permute-done((bf16[320,384]{1,0:T(8,128)(2,1)S(1)}, bf16[320,384]{1,0:T(8,128)(2,1)S(1)}, u32[]{:S(2)}, u32[]{:S(2)}) %collective-permute-start.4) | collective-permute-done | bytes 245792 | tf_op jit(solution)/shard_map/ppermute | solution.py:20
  30.1 3.6 %collective-permute-done.5.two_b = bf16[320,384]{1,0:T(8,128)(2,1)S(1)} collective-permute-done((bf16[320,384]{1,0:T(8,128)(2,1)S(1)}, bf16[320,384]{1,0:T(8,128)(2,1)S(1)}, u32[]{:S(2)}, u32[]{:S(2)}) %collective-permute-start.5) | collective-permute-done | bytes 245792 | tf_op jit(solution)/shard_map/ppermute | solution.py:20
  33.7 6.3 %shard_map.96.rest_0_ = bf16[2,3,512,128]{3,2,1,0:T(8,128)(2,1)S(1)} custom-call(s32[85]{0:T(128)S(1)} %concatenate.15.place.allowed.marks.facts, bf16[512,384]{1,0:T(8,128)(2,1)S(1)} %copy-done.1, bf16[512,384]{1,0:T(8,128)(2,1)S(1)} %collective-permute-done.far, bf16[512,384]{1,0:T(8,128)(2,1)S(1)} %collective-permute-done.1.low, ...), custom_call_target="tpu_custom_call" | custom-call | flops 2415919104 | bytes 7077888 | tf_op jit(solution)/shard_map/pallas_call | solution.py:104
  40.1 2.0 %collective-permute-start.8 = (bf16[2,3,512,128]{3,2,1,0:T(8,128)(2,1)S(1)}, bf16[2,3,512,128]{3,2,1,0:T(8,128)(2,1)S(1)}, u32[]{:S(2)}, u32[]{:S(2)}) collective-permute-start(bf16[2,3,512,128]{3,2,1,0:T(8,128)(2,1)S(1)} %shard_map.96.rest_0_), channel_id=1, source_target_pairs={{0,16},{8,24},{16,32},{24,40},{32,48},{40,56},{48,64},{56,72},{64,... | collective-permute-start | bytes 2359304 | tf_op jit(solution)/shard_map/ppermute | solution.py:29
  42.1 6.5 %collective-permute-start.7 = (bf16[2,3,512,128]{3,2,1,0:T(8,128)(2,1)S(1)}, bf16[2,3,512,128]{3,2,1,0:T(8,128)(2,1)S(1)}, u32[]{:S(2)}, u32[]{:S(2)}) collective-permute-start(bf16[2,3,512,128]{3,2,1,0:T(8,128)(2,1)S(1)} %shard_map.96.rest_0_), channel_id=1, source_target_pairs={{0,240},{8,248},{16,0},{24,8},{32,16},{40,24},{48,32},{56,40},{64,... | collective-permute-start | bytes 2359304 | tf_op jit(solution)/shard_map/ppermute | solution.py:29
  48.7 5.4 %shard_map.95 = bf16[1,3,512,128]{3,2,1,0:T(8,128)(2,1)S(1)} custom-call(s32[85]{0:T(128)S(1)} %concatenate.15.place.allowed.marks.facts, bf16[512,384]{1,0:T(8,128)(2,1)S(1)} %copy-done.1, bf16[512,384]{1,0:T(8,128)(2,1)S(1)} %collective-permute-done.far, bf16[512,384]{1,0:T(8,128)(2,1)S(1)} %collective-permute-done.1.low, ...), custom_call_target="tpu_custom_call" | custom-call | flops 1207959552 | bytes 4718592 | tf_op jit(solution)/shard_map/pallas_call | solution.py:104
  54.1 3.4 %shard_map.97 = (f32[3,512,128]{2,1,0:T(8,128)S(1)}, f32[3,512,256]{2,1,0:T(8,128)S(1)}) custom-call(s32[85]{0:T(128)S(1)} %concatenate.15.place.allowed.marks.facts, bf16[3,512,128]{2,1,0:T(8,128)(2,1)S(1)} %bitcast.31, bf16[2,3,512,128]{3,2,1,0:T(8,128)(2,1)S(1)} %shard_map.96.rest_0_, bf16[2,3,512,128]{3,2,1,0:T(8,128)(2,1)S(1)} %collective-permute-done.9.rest_1_), custom_call_target="tpu_custom_call" | custom-call | flops 1207959552 | bytes 1048576 | tf_op jit(solution)/shard_map/pallas_call | solution.py:177
  57.5 9.0 %collective-permute-done.8.rest_1_ = bf16[2,3,512,128]{3,2,1,0:T(8,128)(2,1)S(1)} collective-permute-done((bf16[2,3,512,128]{3,2,1,0:T(8,128)(2,1)S(1)}, bf16[2,3,512,128]{3,2,1,0:T(8,128)(2,1)S(1)}, u32[]{:S(2)}, u32[]{:S(2)}) %collective-permute-start.8) | collective-permute-done | bytes 786464 | tf_op jit(solution)/shard_map/ppermute | solution.py:29
  66.7 2.8 %shard_map.98 = (f32[3,512,128]{2,1,0:T(8,128)S(1)}, f32[3,512,256]{2,1,0:T(8,128)S(1)}) custom-call(s32[85]{0:T(128)S(1)} %concatenate.15.place.allowed.marks.facts, bf16[3,512,128]{2,1,0:T(8,128)(2,1)S(1)} %bitcast.32, bf16[2,3,512,128]{3,2,1,0:T(8,128)(2,1)S(1)} %collective-permute-done.7.rest_0_, ...), custom_call_target="tpu_custom_call" | custom-call | flops 1207959552 | bytes 1048576 | tf_op jit(solution)/shard_map/pallas_call | solution.py:177
  69.5 2.1 %shard_map.99.attended = bf16[512,384]{1,0:T(8,128)(2,1)S(1)} custom-call(s32[85]{0:T(128)S(1)} %concatenate.15.place.allowed.marks.facts, bf16[3,512,128]{2,1,0:T(8,128)(2,1)S(1)} %bitcast.33, bf16[2,3,512,128]{3,2,1,0:T(8,128)(2,1)S(1)} %collective-permute-done.10.rest_0_, f32[3,512,128]{2,1,0:T(8,128)S(1)} %get-tuple-element.51.rest_1_, ...), custom_call_target="tpu_custom_call" | custom-call | flops 603979776 | bytes 524288 | tf_op jit(solution)/shard_map/pallas_call | solution.py:177
  71.7 1.7 %shard_map.100 = (bf16[512,384]{1,0:T(8,128)(2,1)S(1)}, bf16[320,384]{1,0:T(8,128)(2,1)S(1)}, bf16[320,384]{1,0:T(8,128)(2,1)S(1)}, bf16[896,384]{1,0:T(8,128)(2,1)S(1)}) custom-call(s32[85]{0:T(128)S(1)} %concatenate.15.place.allowed.marks.facts, bf16[512,384]{1,0:T(8,128)(2,1)S(1)} %shard_map.99.attended, bf16[384,3072]{1,0:T(8,128)(2,1)S(1)} %copy-done), custom_call_target="tpu_custom_call" | custom-call | flops 603979776 | bytes 3538944 | tf_op jit(solution)/shard_map/pallas_call | solution.py:237
  73.3 0.4 collective-permute-start.14
  73.8 0.7 shard_map.101
  74.4 0.5 collective-permute-start.15
  74.9 0.5 collective-permute-start.11
  75.4 1.2 collective-permute-start.12
  76.5 2.1 %collective-permute-start.13 = (bf16[320,384]{1,0:T(8,128)(2,1)S(1)}, bf16[320,384]{1,0:T(8,128)(2,1)S(1)}, u32[]{:S(2)}, u32[]{:S(2)}) collective-permute-start(bf16[320,384]{1,0:T(8,128)(2,1)S(1)} %get-tuple-element.55), channel_id=1, source_target_pairs={{0,1},{1,2},{2,3},{3,0},{4,5},{5,6},{6,7},{7,4},{8,9},{9,10},{10,1... | collective-permute-start | bytes 737288 | tf_op jit(solution)/shard_map/ppermute | solution.py:20
  78.6 0.6 shard_map.102
  79.3 4.8 %collective-permute-done.16.got = bf16[8,8,896]{2,1,0:T(8,128)(2,1)S(1)} collective-permute-done((bf16[8,8,896]{2,1,0:T(8,128)(2,1)S(1)}, bf16[8,8,896]{2,1,0:T(8,128)(2,1)S(1)}, u32[]{:S(2)}, u32[]{:S(2)}) %collective-permute-start.16) | collective-permute-done | bytes 114720 | tf_op jit(solution)/shard_map/ppermute | solution.py:33
  84.1 0.6 shard_map.103
  84.7 1.0 collective-permute-start.17
  85.7 4.2 %collective-permute-done.17.got = bf16[4,8,896]{2,1,0:T(8,128)(2,1)S(1)} collective-permute-done((bf16[4,8,896]{2,1,0:T(8,128)(2,1)S(1)}, bf16[4,8,896]{2,1,0:T(8,128)(2,1)S(1)}, u32[]{:S(2)}, u32[]{:S(2)}) %collective-permute-start.17) | collective-permute-done | bytes 57376 | tf_op jit(solution)/shard_map/ppermute | solution.py:33
  89.9 0.6 shard_map.104
  90.5 2.6 %collective-permute-start.18 = (bf16[2,8,896]{2,1,0:T(8,128)(2,1)S(1)}, bf16[2,8,896]{2,1,0:T(8,128)(2,1)S(1)}, u32[]{:S(2)}, u32[]{:S(2)}) collective-permute-start(bf16[2,8,896]{2,1,0:T(8,128)(2,1)S(1)} %get-tuple-element.64), channel_id=1, source_target_pairs={{0,96},{8,104},{16,112},{24,120},{32,64},{40,72},{48,80},{56,88},{... | collective-permute-start | bytes 86024 | tf_op jit(solution)/shard_map/ppermute | solution.py:33
  93.1 3.5 %collective-permute-done.18.got = bf16[2,8,896]{2,1,0:T(8,128)(2,1)S(1)} collective-permute-done((bf16[2,8,896]{2,1,0:T(8,128)(2,1)S(1)}, bf16[2,8,896]{2,1,0:T(8,128)(2,1)S(1)}, u32[]{:S(2)}, u32[]{:S(2)}) %collective-permute-start.18) | collective-permute-done | bytes 28704 | tf_op jit(solution)/shard_map/ppermute | solution.py:33
  96.6 1.7 %shard_map.105 = (bf16[512,384]{1,0:T(8,128)(2,1)S(1)}, bf16[512,384]{1,0:T(8,128)(2,1)S(1)}, bf16[512,384]{1,0:T(8,128)(2,1)S(1)}, bf16[512,384]{1,0:T(8,128)(2,1)S(1)}) custom-call(s32[85]{0:T(128)S(1)} %concatenate.15.place.allowed.marks.facts, bf16[512,384]{1,0:T(8,128)(2,1)S(1)} %shard_map.99.attended, bf16[384,3072]{1,0:T(8,128)(2,1)S(1)} %copy-done, ...), custom_call_target="tpu_custom_call" | custom-call | flops 603979776 | bytes 3538944 | tf_op jit(solution)/shard_map/pallas_call | solution.py:237
  98.3 1.8 %collective-permute-start.19 = (bf16[512,384]{1,0:T(8,128)(2,1)S(1)}, bf16[512,384]{1,0:T(8,128)(2,1)S(1)}, u32[]{:S(2)}, u32[]{:S(2)}) collective-permute-start(bf16[512,384]{1,0:T(8,128)(2,1)S(1)} %get-tuple-element.70), channel_id=1, source_target_pairs={{0,4},{1,5},{2,6},{3,7},{4,0},{5,1},{6,2},{7,3},{8,12},{9,13},{10,... | collective-permute-start | bytes 1179656 | tf_op jit(solution)/shard_map/ppermute | solution.py:24
  100.2 3.2 %collective-permute-start.21 = (bf16[512,384]{1,0:T(8,128)(2,1)S(1)}, bf16[512,384]{1,0:T(8,128)(2,1)S(1)}, u32[]{:S(2)}, u32[]{:S(2)}) collective-permute-start(bf16[512,384]{1,0:T(8,128)(2,1)S(1)} %get-tuple-element.72), channel_id=1, source_target_pairs={{0,1},{1,2},{2,3},{3,0},{4,5},{5,6},{6,7},{7,4},{8,9},{9,10},{10,1... | collective-permute-start | bytes 1179656 | tf_op jit(solution)/shard_map/ppermute | solution.py:20
  103.4 0.6 shard_map.106
  103.9 1.3 %collective-permute-start.22 = (bf16[1,8,896]{2,1,0:T(8,128)(2,1)S(1)}, bf16[1,8,896]{2,1,0:T(8,128)(2,1)S(1)}, u32[]{:S(2)}, u32[]{:S(2)}) collective-permute-start(bf16[1,8,896]{2,1,0:T(8,128)(2,1)S(1)} %get-tuple-element.76), channel_id=1, source_target_pairs={{0,128},{8,136},{16,144},{24,152},{32,160},{40,168},{48,176},{56,1... | collective-permute-start | bytes 43016 | tf_op jit(solution)/shard_map/ppermute | solution.py:33
  105.2 4.0 %collective-permute-done.22.got = bf16[1,8,896]{2,1,0:T(8,128)(2,1)S(1)} collective-permute-done((bf16[1,8,896]{2,1,0:T(8,128)(2,1)S(1)}, bf16[1,8,896]{2,1,0:T(8,128)(2,1)S(1)}, u32[]{:S(2)}, u32[]{:S(2)}) %collective-permute-start.22) | collective-permute-done | bytes 14368 | tf_op jit(solution)/shard_map/ppermute | solution.py:33
  109.2 1.0 shard_map.107
  110.2 0.4 collective-permute-start.23
  110.6 3.5 %collective-permute-done.23.far = bf16[4,8,384]{2,1,0:T(8,128)(2,1)S(1)} collective-permute-done((bf16[4,8,384]{2,1,0:T(8,128)(2,1)S(1)}, bf16[4,8,384]{2,1,0:T(8,128)(2,1)S(1)}, u32[]{:S(2)}, u32[]{:S(2)}) %collective-permute-start.23) | collective-permute-done | bytes 24608 | tf_op jit(solution)/shard_map/ppermute | solution.py:24
  114.2 3.2 %collective-permute-start.25 = (bf16[8,384]{1,0:T(8,128)(2,1)S(1)}, bf16[8,384]{1,0:T(8,128)(2,1)S(1)}, u32[]{:S(2)}, u32[]{:S(2)}) collective-permute-start(bf16[8,384]{1,0:T(8,128)(2,1)S(1)} %get-tuple-element.86), channel_id=1, source_target_pairs={{0,1},{1,2},{2,3},{3,0},{4,5},{5,6},{6,7},{7,4},{8,9},{9,10},{10,1... | collective-permute-start | bytes 18440 | tf_op jit(solution)/shard_map/ppermute | solution.py:20
  117.5 1.6 %shard_map.108 = bf16[512,384]{1,0:T(8,128)(2,1)} custom-call(s32[85]{0:T(128)S(1)} %concatenate.15.place.allowed.marks.facts, bf16[512,384]{1,0:T(8,128)(2,1)S(1)} %get-tuple-element.69.own, bf16[512,384]{1,0:T(8,128)(2,1)S(1)} %collective-permute-done.19.far, bf16[512,384]{1,0:T(8,128)(2,1)S(1)} %collective-permute-done.20.low, ...), custom_call_target="tpu_custom_call" | custom-call | flops 1048576 | bytes 1048576 | tf_op jit(solution)/shard_map/pallas_call | solution.py:325
  119.1 3.5 %collective-permute-done.26.opposite = bf16[8,384]{1,0:T(8,128)(2,1)S(1)} collective-permute-done((bf16[8,384]{1,0:T(8,128)(2,1)S(1)}, bf16[8,384]{1,0:T(8,128)(2,1)S(1)}, u32[]{:S(2)}, u32[]{:S(2)}) %collective-permute-start.26) | collective-permute-done | bytes 6176 | tf_op jit(solution)/shard_map/ppermute | solution.py:20
  122.6 0.7 shard_map.110
  (47 shorter events, 1.2 us)
Async XLA Ops:
  0.6 12.5 %collective-permute-start.2 = (bf16[512,384]{1,0:T(8,128)(2,1)}, bf16[512,384]{1,0:T(8,128)(2,1)S(1)}, u32[]{:S(2)}, u32[]{:S(2)}) collective-permute-start(bf16[512,384]{1,0:T(8,128)(2,1)} %latents.3), channel_id=1, source_target_pairs={{0,3},{1,0},{2,1},{3,2},{4,7},{5,4},{6,5},{7,6},{8,11},{9,8},{10,9... | collective-permute-start | bytes 1179656 | tf_op jit(solution)/shard_map/ppermute | solution.py:20
  1.5 11.6 %collective-permute-start.1 = (bf16[512,384]{1,0:T(8,128)(2,1)}, bf16[512,384]{1,0:T(8,128)(2,1)S(1)}, u32[]{:S(2)}, u32[]{:S(2)}) collective-permute-start(bf16[512,384]{1,0:T(8,128)(2,1)} %latents.3), channel_id=1, source_target_pairs={{0,1},{1,2},{2,3},{3,0},{4,5},{5,6},{6,7},{7,4},{8,9},{9,10},{10,1... | collective-permute-start | bytes 1179656 | tf_op jit(solution)/shard_map/ppermute | solution.py:20
  3.9 10.9 %collective-permute-start = (bf16[512,384]{1,0:T(8,128)(2,1)}, bf16[512,384]{1,0:T(8,128)(2,1)S(1)}, u32[]{:S(2)}, u32[]{:S(2)}) collective-permute-start(bf16[512,384]{1,0:T(8,128)(2,1)} %latents.3), channel_id=1, source_target_pairs={{0,4},{1,5},{2,6},{3,7},{4,0},{5,1},{6,2},{7,3},{8,12},{9,13},{10,... | collective-permute-start | bytes 1179656 | tf_op jit(solution)/shard_map/ppermute | solution.py:24
  13.2 20.5 %copy-start.1 = (bf16[512,384]{1,0:T(8,128)(2,1)S(1)}, bf16[512,384]{1,0:T(8,128)(2,1)}, u32[]{:S(2)}) copy-start(bf16[512,384]{1,0:T(8,128)(2,1)} %latents.3) | copy-start | bytes 1179652
  13.3 20.4 %collective-permute-start.6 = (bf16[896,384]{1,0:T(8,128)(2,1)S(1)}, bf16[896,384]{1,0:T(8,128)(2,1)S(1)}, u32[]{:S(2)}, u32[]{:S(2)}) collective-permute-start(bf16[896,384]{1,0:T(8,128)(2,1)S(1)} %pad_maximum_fusion), channel_id=1, source_target_pairs={{0,4},{1,5},{2,6},{3,7},{4,0},{5,1},{6,2},{7,3},{8,12},{9,13},{10,... | collective-permute-start | bytes 2064392 | tf_op jit(solution)/shard_map/ppermute | solution.py:24
  14.9 15.2 %collective-permute-start.4 = (bf16[320,384]{1,0:T(8,128)(2,1)S(1)}, bf16[320,384]{1,0:T(8,128)(2,1)S(1)}, u32[]{:S(2)}, u32[]{:S(2)}) collective-permute-start(bf16[320,384]{1,0:T(8,128)(2,1)S(1)} %pad_maximum_fusion.1), channel_id=1, source_target_pairs={{0,1},{1,2},{2,3},{3,0},{4,5},{5,6},{6,7},{7,4},{8,9},{9,10},{10,1... | collective-permute-start | bytes 737288 | tf_op jit(solution)/shard_map/ppermute | solution.py:20
  17.9 15.8 %collective-permute-start.3 = (bf16[512,384]{1,0:T(8,128)(2,1)S(1)}, bf16[512,384]{1,0:T(8,128)(2,1)S(1)}, u32[]{:S(2)}, u32[]{:S(2)}) collective-permute-start(bf16[512,384]{1,0:T(8,128)(2,1)S(1)} %collective-permute-done.far), channel_id=1, source_target_pairs={{0,2},{1,3},{2,0},{3,1},{4,6},{5,7},{6,4},{7,5},{8,10},{9,11},{10,... | collective-permute-start | bytes 1179656 | tf_op jit(solution)/shard_map/ppermute | solution.py:20
  18.1 15.7 %collective-permute-start.5 = (bf16[320,384]{1,0:T(8,128)(2,1)S(1)}, bf16[320,384]{1,0:T(8,128)(2,1)S(1)}, u32[]{:S(2)}, u32[]{:S(2)}) collective-permute-start(bf16[320,384]{1,0:T(8,128)(2,1)S(1)} %pad_maximum_fusion.2), channel_id=1, source_target_pairs={{0,3},{1,0},{2,1},{3,2},{4,7},{5,4},{6,5},{7,6},{8,11},{9,8},{10,9... | collective-permute-start | bytes 737288 | tf_op jit(solution)/shard_map/ppermute | solution.py:20
  40.0 14.1 %collective-permute-start.9 = (bf16[2,3,512,128]{3,2,1,0:T(8,128)(2,1)S(1)}, bf16[2,3,512,128]{3,2,1,0:T(8,128)(2,1)S(1)}, u32[]{:S(2)}, u32[]{:S(2)}) collective-permute-start(bf16[2,3,512,128]{3,2,1,0:T(8,128)(2,1)S(1)} %shard_map.96.rest_0_), channel_id=1, source_target_pairs={{0,8},{8,0},{16,24},{24,16},{32,40},{40,32},{48,56},{56,48},{64,72... | collective-permute-start | bytes 2359304 | tf_op jit(solution)/shard_map/ppermute | solution.py:33
  40.1 26.4 %collective-permute-start.8 = (bf16[2,3,512,128]{3,2,1,0:T(8,128)(2,1)S(1)}, bf16[2,3,512,128]{3,2,1,0:T(8,128)(2,1)S(1)}, u32[]{:S(2)}, u32[]{:S(2)}) collective-permute-start(bf16[2,3,512,128]{3,2,1,0:T(8,128)(2,1)S(1)} %shard_map.96.rest_0_), channel_id=1, source_target_pairs={{0,16},{8,24},{16,32},{24,40},{32,48},{40,56},{48,64},{56,72},{64,... | collective-permute-start | bytes 2359304 | tf_op jit(solution)/shard_map/ppermute | solution.py:29
  42.1 24.4 %collective-permute-start.7 = (bf16[2,3,512,128]{3,2,1,0:T(8,128)(2,1)S(1)}, bf16[2,3,512,128]{3,2,1,0:T(8,128)(2,1)S(1)}, u32[]{:S(2)}, u32[]{:S(2)}) collective-permute-start(bf16[2,3,512,128]{3,2,1,0:T(8,128)(2,1)S(1)} %shard_map.96.rest_0_), channel_id=1, source_target_pairs={{0,240},{8,248},{16,0},{24,8},{32,16},{40,24},{48,32},{56,40},{64,... | collective-permute-start | bytes 2359304 | tf_op jit(solution)/shard_map/ppermute | solution.py:29
  66.6 2.9 %collective-permute-start.10 = (bf16[2,3,512,128]{3,2,1,0:T(8,128)(2,1)S(1)}, bf16[2,3,512,128]{3,2,1,0:T(8,128)(2,1)S(1)}, u32[]{:S(2)}, u32[]{:S(2)}) collective-permute-start(bf16[2,3,512,128]{3,2,1,0:T(8,128)(2,1)S(1)} %broadcast_select_fusion), channel_id=1, source_target_pairs={{0,8},{8,0},{16,24},{24,16},{32,40},{40,32},{48,56},{56,48},{64,72... | collective-permute-start | bytes 2359304 | tf_op jit(solution)/shard_map/ppermute | solution.py:33
  69.5 2.2 %copy-start = (bf16[384,3072]{1,0:T(8,128)(2,1)S(1)}, bf16[384,3072]{1,0:T(8,128)(2,1)}, u32[]{:S(2)}) copy-start(bf16[384,3072]{1,0:T(8,128)(2,1)} %weight.5) | copy-start | bytes 7077892
  73.3 23.2 %collective-permute-start.14 = (bf16[896,384]{1,0:T(8,128)(2,1)S(1)}, bf16[896,384]{1,0:T(8,128)(2,1)S(1)}, u32[]{:S(2)}, u32[]{:S(2)}) collective-permute-start(bf16[896,384]{1,0:T(8,128)(2,1)S(1)} %get-tuple-element.56), channel_id=1, source_target_pairs={{0,4},{1,5},{2,6},{3,7},{4,0},{5,1},{6,2},{7,3},{8,12},{9,13},{10,... | collective-permute-start | bytes 2064392 | tf_op jit(solution)/shard_map/ppermute | solution.py:24
  74.4 4.2 %collective-permute-start.15 = (bf16[16,8,896]{2,1,0:T(8,128)(2,1)S(1)}, bf16[16,8,896]{2,1,0:T(8,128)(2,1)S(1)}, u32[]{:S(2)}, u32[]{:S(2)}) collective-permute-start(bf16[16,8,896]{2,1,0:T(8,128)(2,1)S(1)} %get-tuple-element.59), channel_id=1, source_target_pairs={{0,8},{8,0},{16,24},{24,16},{32,40},{40,32},{48,56},{56,48},{64,72... | collective-permute-start | bytes 688136 | tf_op jit(solution)/shard_map/ppermute | solution.py:33
  74.9 18.2 %collective-permute-start.11 = (bf16[512,384]{1,0:T(8,128)(2,1)S(1)}, bf16[512,384]{1,0:T(8,128)(2,1)S(1)}, u32[]{:S(2)}, u32[]{:S(2)}) collective-permute-start(bf16[512,384]{1,0:T(8,128)(2,1)S(1)} %get-tuple-element.53), channel_id=1, source_target_pairs={{0,2},{1,3},{2,0},{3,1},{4,6},{5,7},{6,4},{7,5},{8,10},{9,11},{10,... | collective-permute-start | bytes 1179656 | tf_op jit(solution)/shard_map/ppermute | solution.py:20
  75.4 17.7 %collective-permute-start.12 = (bf16[320,384]{1,0:T(8,128)(2,1)S(1)}, bf16[320,384]{1,0:T(8,128)(2,1)S(1)}, u32[]{:S(2)}, u32[]{:S(2)}) collective-permute-start(bf16[320,384]{1,0:T(8,128)(2,1)S(1)} %get-tuple-element.54), channel_id=1, source_target_pairs={{0,3},{1,0},{2,1},{3,2},{4,7},{5,4},{6,5},{7,6},{8,11},{9,8},{10,9... | collective-permute-start | bytes 737288 | tf_op jit(solution)/shard_map/ppermute | solution.py:20
  76.5 16.6 %collective-permute-start.13 = (bf16[320,384]{1,0:T(8,128)(2,1)S(1)}, bf16[320,384]{1,0:T(8,128)(2,1)S(1)}, u32[]{:S(2)}, u32[]{:S(2)}) collective-permute-start(bf16[320,384]{1,0:T(8,128)(2,1)S(1)} %get-tuple-element.55), channel_id=1, source_target_pairs={{0,1},{1,2},{2,3},{3,0},{4,5},{5,6},{6,7},{7,4},{8,9},{9,10},{10,1... | collective-permute-start | bytes 737288 | tf_op jit(solution)/shard_map/ppermute | solution.py:20
  79.2 4.9 %collective-permute-start.16 = (bf16[8,8,896]{2,1,0:T(8,128)(2,1)S(1)}, bf16[8,8,896]{2,1,0:T(8,128)(2,1)S(1)}, u32[]{:S(2)}, u32[]{:S(2)}) collective-permute-start(bf16[8,8,896]{2,1,0:T(8,128)(2,1)S(1)} %get-tuple-element.61), channel_id=1, source_target_pairs={{0,16},{8,24},{16,0},{24,8},{32,48},{40,56},{48,32},{56,40},{64,80... | collective-permute-start | bytes 344072 | tf_op jit(solution)/shard_map/ppermute | solution.py:33
  84.7 5.3 %collective-permute-start.17 = (bf16[4,8,896]{2,1,0:T(8,128)(2,1)S(1)}, bf16[4,8,896]{2,1,0:T(8,128)(2,1)S(1)}, u32[]{:S(2)}, u32[]{:S(2)}) collective-permute-start(bf16[4,8,896]{2,1,0:T(8,128)(2,1)S(1)} %get-tuple-element.63), channel_id=1, source_target_pairs={{0,32},{8,40},{16,48},{24,56},{32,0},{40,8},{48,16},{56,24},{64,96... | collective-permute-start | bytes 172040 | tf_op jit(solution)/shard_map/ppermute | solution.py:33
  90.5 6.1 %collective-permute-start.18 = (bf16[2,8,896]{2,1,0:T(8,128)(2,1)S(1)}, bf16[2,8,896]{2,1,0:T(8,128)(2,1)S(1)}, u32[]{:S(2)}, u32[]{:S(2)}) collective-permute-start(bf16[2,8,896]{2,1,0:T(8,128)(2,1)S(1)} %get-tuple-element.64), channel_id=1, source_target_pairs={{0,96},{8,104},{16,112},{24,120},{32,64},{40,72},{48,80},{56,88},{... | collective-permute-start | bytes 86024 | tf_op jit(solution)/shard_map/ppermute | solution.py:33
  98.3 19.1 %copy-start.2 = (bf16[50,384]{1,0:T(8,128)(2,1)S(1)}, bf16[50,384]{1,0:T(8,128)(2,1)}, u32[]{:S(2)}) copy-start(bf16[50,384]{1,0:T(8,128)(2,1)} %gates.3) | copy-start | bytes 115204
  98.3 15.8 %collective-permute-start.19 = (bf16[512,384]{1,0:T(8,128)(2,1)S(1)}, bf16[512,384]{1,0:T(8,128)(2,1)S(1)}, u32[]{:S(2)}, u32[]{:S(2)}) collective-permute-start(bf16[512,384]{1,0:T(8,128)(2,1)S(1)} %get-tuple-element.70), channel_id=1, source_target_pairs={{0,4},{1,5},{2,6},{3,7},{4,0},{5,1},{6,2},{7,3},{8,12},{9,13},{10,... | collective-permute-start | bytes 1179656 | tf_op jit(solution)/shard_map/ppermute | solution.py:24
  100.1 14.0 %collective-permute-start.20 = (bf16[512,384]{1,0:T(8,128)(2,1)S(1)}, bf16[512,384]{1,0:T(8,128)(2,1)S(1)}, u32[]{:S(2)}, u32[]{:S(2)}) collective-permute-start(bf16[512,384]{1,0:T(8,128)(2,1)S(1)} %get-tuple-element.71), channel_id=1, source_target_pairs={{0,3},{1,0},{2,1},{3,2},{4,7},{5,4},{6,5},{7,6},{8,11},{9,8},{10,9... | collective-permute-start | bytes 1179656 | tf_op jit(solution)/shard_map/ppermute | solution.py:20
  100.2 13.9 %collective-permute-start.21 = (bf16[512,384]{1,0:T(8,128)(2,1)S(1)}, bf16[512,384]{1,0:T(8,128)(2,1)S(1)}, u32[]{:S(2)}, u32[]{:S(2)}) collective-permute-start(bf16[512,384]{1,0:T(8,128)(2,1)S(1)} %get-tuple-element.72), channel_id=1, source_target_pairs={{0,1},{1,2},{2,3},{3,0},{4,5},{5,6},{6,7},{7,4},{8,9},{9,10},{10,1... | collective-permute-start | bytes 1179656 | tf_op jit(solution)/shard_map/ppermute | solution.py:20
  103.9 5.3 %collective-permute-start.22 = (bf16[1,8,896]{2,1,0:T(8,128)(2,1)S(1)}, bf16[1,8,896]{2,1,0:T(8,128)(2,1)S(1)}, u32[]{:S(2)}, u32[]{:S(2)}) collective-permute-start(bf16[1,8,896]{2,1,0:T(8,128)(2,1)S(1)} %get-tuple-element.76), channel_id=1, source_target_pairs={{0,128},{8,136},{16,144},{24,152},{32,160},{40,168},{48,176},{56,1... | collective-permute-start | bytes 43016 | tf_op jit(solution)/shard_map/ppermute | solution.py:33
  110.2 3.9 %collective-permute-start.23 = (bf16[4,8,384]{2,1,0:T(8,128)(2,1)S(1)}, bf16[4,8,384]{2,1,0:T(8,128)(2,1)S(1)}, u32[]{:S(2)}, u32[]{:S(2)}) collective-permute-start(bf16[4,8,384]{2,1,0:T(8,128)(2,1)S(1)} %get-tuple-element.77), channel_id=1, source_target_pairs={{0,4},{1,5},{2,6},{3,7},{4,0},{5,1},{6,2},{7,3},{8,12},{9,13},{10,... | collective-permute-start | bytes 73736 | tf_op jit(solution)/shard_map/ppermute | solution.py:24
  114.1 4.9 %collective-permute-start.24 = (bf16[8,384]{1,0:T(8,128)(2,1)S(1)}, bf16[8,384]{1,0:T(8,128)(2,1)S(1)}, u32[]{:S(2)}, u32[]{:S(2)}) collective-permute-start(bf16[8,384]{1,0:T(8,128)(2,1)S(1)} %get-tuple-element.85), channel_id=1, source_target_pairs={{0,3},{1,0},{2,1},{3,2},{4,7},{5,4},{6,5},{7,6},{8,11},{9,8},{10,9... | collective-permute-start | bytes 18440 | tf_op jit(solution)/shard_map/ppermute | solution.py:20
  114.2 4.8 %collective-permute-start.25 = (bf16[8,384]{1,0:T(8,128)(2,1)S(1)}, bf16[8,384]{1,0:T(8,128)(2,1)S(1)}, u32[]{:S(2)}, u32[]{:S(2)}) collective-permute-start(bf16[8,384]{1,0:T(8,128)(2,1)S(1)} %get-tuple-element.86), channel_id=1, source_target_pairs={{0,1},{1,2},{2,3},{3,0},{4,5},{5,6},{6,7},{7,4},{8,9},{9,10},{10,1... | collective-permute-start | bytes 18440 | tf_op jit(solution)/shard_map/ppermute | solution.py:20
  117.5 5.1 %collective-permute-start.26 = (bf16[8,384]{1,0:T(8,128)(2,1)S(1)}, bf16[8,384]{1,0:T(8,128)(2,1)S(1)}, u32[]{:S(2)}, u32[]{:S(2)}) collective-permute-start(bf16[8,384]{1,0:T(8,128)(2,1)S(1)} %get-tuple-element.87), channel_id=1, source_target_pairs={{0,2},{1,3},{2,0},{3,1},{4,6},{5,7},{6,4},{7,5},{8,10},{9,11},{10,... | collective-permute-start | bytes 18440 | tf_op jit(solution)/shard_map/ppermute | solution.py:20

commit v5 on v4

--- a/solution.py
+++ b/solution.py
@@ -194,18 +194,19 @@
     return total
 
 
-def product(place, slot, left, weight):
+def product(place, slots, left, weight):
     part = weight.shape[0]
-    columns = pl.ds(pl.multiple_of(place[slot] * part, 128), part)
-    return jnp.dot(left, weight[:, columns], preferred_element_type=jnp.float32).astype(jnp.bfloat16)
+    columns = [weight[:, pl.ds(pl.multiple_of(place[slot] * part, 128), part)] for slot in slots]
+    result = jnp.dot(left, jnp.concatenate(columns, axis=1), preferred_element_type=jnp.float32).astype(jnp.bfloat16)
+    return [result[:, i * part : (i + 1) * part] for i in range(len(slots))]
 
 
 def first_kernel(cut, place, attended, weight, far_opp, two_a, two_b, two_c):
     rows = attended.shape[0]
     half = rows // 2
     left = attended[...]
-    far_opp[...] = product(place, 7, left, weight)
-    opp, far_low, far_high = (product(place, slot, left, weight) for slot in (4, 5, 6))
+    far_opp[...], opp = product(place, (7, 4), left, weight)
+    far_low, far_high = product(place, (5, 6), left, weight)
     two_a[:half] = opp[:half]
     two_a[half:] = far_low[:cut]
     two_b[:half] = opp[half:]
@@ -219,7 +220,8 @@
     half = rows // 2
     bf = jnp.bfloat16
     left = attended[...]
-    far, low, high = (product(place, slot, left, weight) for slot in (1, 2, 3))
+    far, low = product(place, (1, 2), left, weight)
+    high, own[...] = product(place, (3, 0), left, weight)
     sum_far[:cut] = added(far[:cut], got_opp[:cut], got_a[half:]).astype(bf)
     sum_far[cut : rows - cut] = added(far[cut : rows - cut], got_opp[cut : rows - cut]).astype(bf)
     sum_far[rows - cut :] = added(far[rows - cut :], got_opp[rows - cut :], got_b[half:]).astype(bf)
@@ -229,7 +231,6 @@
     sum_high[:half] = added(high[:half], got_c[rows - cut : rows - cut + half]).astype(bf)
     sum_high[half : rows - cut] = added(high[half : rows - cut], got_b[: half - cut], got_c[rows - cut + half :]).astype(bf)
     sum_high[rows - cut :] = added(high[rows - cut :], got_b[half - cut : half]).astype(bf)
-    own[...] = product(place, 0, left, weight)
 
 
 def summed(kernel, place, attended, weight, terms, heights):

time: 124 us -> 123 us (level)
  no operation moved by 1% of the time
where the time goes in v5:
time: 123 us
  waiting for transfers between devices  47.2 us (38%)
  starting transfers between devices  37.4 us (30%)
  Pallas kernels  29.4 us (24%)
  between operations  4.18 us (3%)
  local copies, waits for them, and re-layouts  3.67 us (3%)
    ppermute x13, waiting for transfers between devices, ring(): lax.ppermute(value, 'mp', [(s, s // 4 * 4 + (s + distance) % 4) for s in...  18.2 us
    ppermute x13, starting transfers between devices, ring(): lax.ppermute(value, 'mp', [(s, s // 4 * 4 + (s + distance) % 4) for s in...  17.6 us
    ppermute x7, waiting for transfers between devices, flipped(): lax.ppermute(value, 'queue', [(s, s ^ bit) for s in range(lax.axis_size('...  16.5 us
    pallas_call x2, Pallas kernels, products(): pl.pallas_call(functools.partial(product_kernel, first), out_shape=jax.Sh...  11.7 us
    ppermute x2, waiting for transfers between devices, shifted(): lax.ppermute(value, 'queue', [(s, (s + distance) % count) for s in range(...  8.98 us
    ppermute x2, starting transfers between devices, shifted(): lax.ppermute(value, 'queue', [(s, (s + distance) % count) for s in range(...  8.53 us
    pallas_call x3, Pallas kernels, attend(): pl.pallas_call(functools.partial(attend_kernel, (blocks, not state, last)...  8.31 us
    ppermute x7, starting transfers between devices, flipped(): lax.ppermute(value, 'queue', [(s, s ^ bit) for s in range(lax.axis_size('...  5.84 us
  transfers between devices with their start and end apart: 27, of which 9 were waited for; matrix products, arithmetic and copies ran while one was open for 4% of the time, Pallas kernels for 14%

profile of v5, /device:TPU:6, one launch (start us, length us, event | category | flops | bytes accessed | tf_op | source)
XLA Modules:
  0.0 123.0 jit_solution(14333552490383811563)
XLA Ops:
  0.6 0.9 collective-permute-start.2
  1.5 2.4 %collective-permute-start.1 = (bf16[512,384]{1,0:T(8,128)(2,1)}, bf16[512,384]{1,0:T(8,128)(2,1)S(1)}, u32[]{:S(2)}, u32[]{:S(2)}) collective-permute-start(bf16[512,384]{1,0:T(8,128)(2,1)} %latents.3), channel_id=1, source_target_pairs={{0,1},{1,2},{2,3},{3,0},{4,5},{5,6},{6,7},{7,4},{8,9},{9,10},{10,1... | collective-permute-start | bytes 1179656 | tf_op jit(solution)/shard_map/ppermute | solution.py:20
  3.9 1.6 %collective-permute-start = (bf16[512,384]{1,0:T(8,128)(2,1)}, bf16[512,384]{1,0:T(8,128)(2,1)S(1)}, u32[]{:S(2)}, u32[]{:S(2)}) collective-permute-start(bf16[512,384]{1,0:T(8,128)(2,1)} %latents.3), channel_id=1, source_target_pairs={{0,4},{1,5},{2,6},{3,7},{4,0},{5,1},{6,2},{7,3},{8,12},{9,13},{10,... | collective-permute-start | bytes 1179656 | tf_op jit(solution)/shard_map/ppermute | solution.py:24
  6.3 0.7 and_convert_fusion
  7.0 1.4 %fusion.2 = (s32[1]{0:T(128)}, s32[1]{0:T(128)}, s32[1]{0:T(128)}) fusion(s32[2]{0:T(128)} %param.9, s32[]{:T(128)S(6)} %select_n.28), kind=kLoop, calls=%fused_computation.14 | loop fusion | bytes 28 | tf_op jit(solution)/shard_map/slice | solution.py:365
  11.1 1.3 %concatenate.15.place.allowed.marks.facts = s32[85]{0:T(128)S(1)} concatenate(s32[1]{0:T(128)} %bitcast, s32[1]{0:T(128)} %bitcast.1, s32[1]{0:T(128)} %bitcast.2, s32[1]{0:T(128)} %bitcast.3, s32[1]{0:T(128)} %bitcast.4, s32[1]{0:T(128)} %bitcast.5, s32[1]{0:T(128)} %bitcast.6, s32[1]{0:T(128)} %bitcast.7, s32[60]{0:T(128)S(1)} %reshape.87, s32[1]{0:T(128)} %bitcast.9, ...), dimensions={0} | concatenate | bytes 680 | tf_op jit(solution)/shard_map/concatenate | solution.py:368
  12.4 0.7 constant_dynamic-slice_fusion.1
  13.3 1.5 %collective-permute-start.6 = (bf16[896,384]{1,0:T(8,128)(2,1)S(1)}, bf16[896,384]{1,0:T(8,128)(2,1)S(1)}, u32[]{:S(2)}, u32[]{:S(2)}) collective-permute-start(bf16[896,384]{1,0:T(8,128)(2,1)S(1)} %pad_maximum_fusion), channel_id=1, source_target_pairs={{0,4},{1,5},{2,6},{3,7},{4,0},{5,1},{6,2},{7,3},{8,12},{9,13},{10,... | collective-permute-start | bytes 2064392 | tf_op jit(solution)/shard_map/ppermute | solution.py:24
  14.9 3.0 %collective-permute-start.4 = (bf16[320,384]{1,0:T(8,128)(2,1)S(1)}, bf16[320,384]{1,0:T(8,128)(2,1)S(1)}, u32[]{:S(2)}, u32[]{:S(2)}) collective-permute-start(bf16[320,384]{1,0:T(8,128)(2,1)S(1)} %pad_maximum_fusion.1), channel_id=1, source_target_pairs={{0,1},{1,2},{2,3},{3,0},{4,5},{5,6},{6,7},{7,4},{8,9},{9,10},{10,1... | collective-permute-start | bytes 737288 | tf_op jit(solution)/shard_map/ppermute | solution.py:20
  18.1 0.9 collective-permute-start.5
  19.0 11.1 %collective-permute-done.4.two_a = bf16[320,384]{1,0:T(8,128)(2,1)S(1)} collective-permute-done((bf16[320,384]{1,0:T(8,128)(2,1)S(1)}, bf16[320,384]{1,0:T(8,128)(2,1)S(1)}, u32[]{:S(2)}, u32[]{:S(2)}) %collective-permute-start.4) | collective-permute-done | bytes 245792 | tf_op jit(solution)/shard_map/ppermute | solution.py:20
  30.1 3.6 %collective-permute-done.5.two_b = bf16[320,384]{1,0:T(8,128)(2,1)S(1)} collective-permute-done((bf16[320,384]{1,0:T(8,128)(2,1)S(1)}, bf16[320,384]{1,0:T(8,128)(2,1)S(1)}, u32[]{:S(2)}, u32[]{:S(2)}) %collective-permute-start.5) | collective-permute-done | bytes 245792 | tf_op jit(solution)/shard_map/ppermute | solution.py:20
  33.7 6.3 %shard_map.96.rest_0_ = bf16[2,3,512,128]{3,2,1,0:T(8,128)(2,1)S(1)} custom-call(s32[85]{0:T(128)S(1)} %concatenate.15.place.allowed.marks.facts, bf16[512,384]{1,0:T(8,128)(2,1)S(1)} %copy-done.1, bf16[512,384]{1,0:T(8,128)(2,1)S(1)} %collective-permute-done.far, bf16[512,384]{1,0:T(8,128)(2,1)S(1)} %collective-permute-done.1.low, ...), custom_call_target="tpu_custom_call" | custom-call | flops 2415919104 | bytes 7077888 | tf_op jit(solution)/shard_map/pallas_call | solution.py:104
  40.1 2.0 %collective-permute-start.8 = (bf16[2,3,512,128]{3,2,1,0:T(8,128)(2,1)S(1)}, bf16[2,3,512,128]{3,2,1,0:T(8,128)(2,1)S(1)}, u32[]{:S(2)}, u32[]{:S(2)}) collective-permute-start(bf16[2,3,512,128]{3,2,1,0:T(8,128)(2,1)S(1)} %shard_map.96.rest_0_), channel_id=1, source_target_pairs={{0,16},{8,24},{16,32},{24,40},{32,48},{40,56},{48,64},{56,72},{64,... | collective-permute-start | bytes 2359304 | tf_op jit(solution)/shard_map/ppermute | solution.py:29
  42.1 6.5 %collective-permute-start.7 = (bf16[2,3,512,128]{3,2,1,0:T(8,128)(2,1)S(1)}, bf16[2,3,512,128]{3,2,1,0:T(8,128)(2,1)S(1)}, u32[]{:S(2)}, u32[]{:S(2)}) collective-permute-start(bf16[2,3,512,128]{3,2,1,0:T(8,128)(2,1)S(1)} %shard_map.96.rest_0_), channel_id=1, source_target_pairs={{0,240},{8,248},{16,0},{24,8},{32,16},{40,24},{48,32},{56,40},{64,... | collective-permute-start | bytes 2359304 | tf_op jit(solution)/shard_map/ppermute | solution.py:29
  48.7 5.4 %shard_map.95 = bf16[1,3,512,128]{3,2,1,0:T(8,128)(2,1)S(1)} custom-call(s32[85]{0:T(128)S(1)} %concatenate.15.place.allowed.marks.facts, bf16[512,384]{1,0:T(8,128)(2,1)S(1)} %copy-done.1, bf16[512,384]{1,0:T(8,128)(2,1)S(1)} %collective-permute-done.far, bf16[512,384]{1,0:T(8,128)(2,1)S(1)} %collective-permute-done.1.low, ...), custom_call_target="tpu_custom_call" | custom-call | flops 1207959552 | bytes 4718592 | tf_op jit(solution)/shard_map/pallas_call | solution.py:104
  54.1 3.4 %shard_map.97 = (f32[3,512,128]{2,1,0:T(8,128)S(1)}, f32[3,512,256]{2,1,0:T(8,128)S(1)}) custom-call(s32[85]{0:T(128)S(1)} %concatenate.15.place.allowed.marks.facts, bf16[3,512,128]{2,1,0:T(8,128)(2,1)S(1)} %bitcast.31, bf16[2,3,512,128]{3,2,1,0:T(8,128)(2,1)S(1)} %shard_map.96.rest_0_, bf16[2,3,512,128]{3,2,1,0:T(8,128)(2,1)S(1)} %collective-permute-done.9.rest_1_), custom_call_target="tpu_custom_call" | custom-call | flops 1207959552 | bytes 1048576 | tf_op jit(solution)/shard_map/pallas_call | solution.py:177
  57.5 9.0 %collective-permute-done.8.rest_1_ = bf16[2,3,512,128]{3,2,1,0:T(8,128)(2,1)S(1)} collective-permute-done((bf16[2,3,512,128]{3,2,1,0:T(8,128)(2,1)S(1)}, bf16[2,3,512,128]{3,2,1,0:T(8,128)(2,1)S(1)}, u32[]{:S(2)}, u32[]{:S(2)}) %collective-permute-start.8) | collective-permute-done | bytes 786464 | tf_op jit(solution)/shard_map/ppermute | solution.py:29
  66.7 2.8 %shard_map.98 = (f32[3,512,128]{2,1,0:T(8,128)S(1)}, f32[3,512,256]{2,1,0:T(8,128)S(1)}) custom-call(s32[85]{0:T(128)S(1)} %concatenate.15.place.allowed.marks.facts, bf16[3,512,128]{2,1,0:T(8,128)(2,1)S(1)} %bitcast.32, bf16[2,3,512,128]{3,2,1,0:T(8,128)(2,1)S(1)} %collective-permute-done.7.rest_0_, ...), custom_call_target="tpu_custom_call" | custom-call | flops 1207959552 | bytes 1048576 | tf_op jit(solution)/shard_map/pallas_call | solution.py:177
  69.5 2.1 %shard_map.99.attended = bf16[512,384]{1,0:T(8,128)(2,1)S(1)} custom-call(s32[85]{0:T(128)S(1)} %concatenate.15.place.allowed.marks.facts, bf16[3,512,128]{2,1,0:T(8,128)(2,1)S(1)} %bitcast.33, bf16[2,3,512,128]{3,2,1,0:T(8,128)(2,1)S(1)} %collective-permute-done.10.rest_0_, f32[3,512,128]{2,1,0:T(8,128)S(1)} %get-tuple-element.51.rest_1_, ...), custom_call_target="tpu_custom_call" | custom-call | flops 603979776 | bytes 524288 | tf_op jit(solution)/shard_map/pallas_call | solution.py:177
  71.7 1.5 %shard_map.100 = (bf16[512,384]{1,0:T(8,128)(2,1)S(1)}, bf16[320,384]{1,0:T(8,128)(2,1)S(1)}, bf16[320,384]{1,0:T(8,128)(2,1)S(1)}, bf16[896,384]{1,0:T(8,128)(2,1)S(1)}) custom-call(s32[85]{0:T(128)S(1)} %concatenate.15.place.allowed.marks.facts, bf16[512,384]{1,0:T(8,128)(2,1)S(1)} %shard_map.99.attended, bf16[384,3072]{1,0:T(8,128)(2,1)S(1)} %copy-done), custom_call_target="tpu_custom_call" | custom-call | flops 603979776 | bytes 3538944 | tf_op jit(solution)/shard_map/pallas_call | solution.py:238
  73.2 0.2 collective-permute-start.14
  73.4 0.7 shard_map.101
  74.1 0.7 collective-permute-start.15
  74.8 0.5 collective-permute-start.11
  75.2 1.2 collective-permute-start.12
  76.4 2.1 %collective-permute-start.13 = (bf16[320,384]{1,0:T(8,128)(2,1)S(1)}, bf16[320,384]{1,0:T(8,128)(2,1)S(1)}, u32[]{:S(2)}, u32[]{:S(2)}) collective-permute-start(bf16[320,384]{1,0:T(8,128)(2,1)S(1)} %get-tuple-element.55), channel_id=1, source_target_pairs={{0,1},{1,2},{2,3},{3,0},{4,5},{5,6},{6,7},{7,4},{8,9},{9,10},{10,1... | collective-permute-start | bytes 737288 | tf_op jit(solution)/shard_map/ppermute | solution.py:20
  78.5 0.6 shard_map.102
  79.2 4.8 %collective-permute-done.16.got = bf16[8,8,896]{2,1,0:T(8,128)(2,1)S(1)} collective-permute-done((bf16[8,8,896]{2,1,0:T(8,128)(2,1)S(1)}, bf16[8,8,896]{2,1,0:T(8,128)(2,1)S(1)}, u32[]{:S(2)}, u32[]{:S(2)}) %collective-permute-start.16) | collective-permute-done | bytes 114720 | tf_op jit(solution)/shard_map/ppermute | solution.py:33
  84.0 0.6 shard_map.103
  84.5 1.0 collective-permute-start.17
  85.6 4.2 %collective-permute-done.17.got = bf16[4,8,896]{2,1,0:T(8,128)(2,1)S(1)} collective-permute-done((bf16[4,8,896]{2,1,0:T(8,128)(2,1)S(1)}, bf16[4,8,896]{2,1,0:T(8,128)(2,1)S(1)}, u32[]{:S(2)}, u32[]{:S(2)}) %collective-permute-start.17) | collective-permute-done | bytes 57376 | tf_op jit(solution)/shard_map/ppermute | solution.py:33
  89.8 0.6 shard_map.104
  90.4 2.6 %collective-permute-start.18 = (bf16[2,8,896]{2,1,0:T(8,128)(2,1)S(1)}, bf16[2,8,896]{2,1,0:T(8,128)(2,1)S(1)}, u32[]{:S(2)}, u32[]{:S(2)}) collective-permute-start(bf16[2,8,896]{2,1,0:T(8,128)(2,1)S(1)} %get-tuple-element.64), channel_id=1, source_target_pairs={{0,96},{8,104},{16,112},{24,120},{32,64},{40,72},{48,80},{56,88},{... | collective-permute-start | bytes 86024 | tf_op jit(solution)/shard_map/ppermute | solution.py:33
  93.0 3.5 %collective-permute-done.18.got = bf16[2,8,896]{2,1,0:T(8,128)(2,1)S(1)} collective-permute-done((bf16[2,8,896]{2,1,0:T(8,128)(2,1)S(1)}, bf16[2,8,896]{2,1,0:T(8,128)(2,1)S(1)}, u32[]{:S(2)}, u32[]{:S(2)}) %collective-permute-start.18) | collective-permute-done | bytes 28704 | tf_op jit(solution)/shard_map/ppermute | solution.py:33
  96.4 1.6 %shard_map.105 = (bf16[512,384]{1,0:T(8,128)(2,1)S(1)}, bf16[512,384]{1,0:T(8,128)(2,1)S(1)}, bf16[512,384]{1,0:T(8,128)(2,1)S(1)}, bf16[512,384]{1,0:T(8,128)(2,1)S(1)}) custom-call(s32[85]{0:T(128)S(1)} %concatenate.15.place.allowed.marks.facts, bf16[512,384]{1,0:T(8,128)(2,1)S(1)} %shard_map.99.attended, bf16[384,3072]{1,0:T(8,128)(2,1)S(1)} %copy-done, ...), custom_call_target="tpu_custom_call" | custom-call | flops 603979776 | bytes 3538944 | tf_op jit(solution)/shard_map/pallas_call | solution.py:238
  98.1 1.8 %collective-permute-start.19 = (bf16[512,384]{1,0:T(8,128)(2,1)S(1)}, bf16[512,384]{1,0:T(8,128)(2,1)S(1)}, u32[]{:S(2)}, u32[]{:S(2)}) collective-permute-start(bf16[512,384]{1,0:T(8,128)(2,1)S(1)} %get-tuple-element.70), channel_id=1, source_target_pairs={{0,4},{1,5},{2,6},{3,7},{4,0},{5,1},{6,2},{7,3},{8,12},{9,13},{10,... | collective-permute-start | bytes 1179656 | tf_op jit(solution)/shard_map/ppermute | solution.py:24
  99.9 3.2 %collective-permute-start.21 = (bf16[512,384]{1,0:T(8,128)(2,1)S(1)}, bf16[512,384]{1,0:T(8,128)(2,1)S(1)}, u32[]{:S(2)}, u32[]{:S(2)}) collective-permute-start(bf16[512,384]{1,0:T(8,128)(2,1)S(1)} %get-tuple-element.72), channel_id=1, source_target_pairs={{0,1},{1,2},{2,3},{3,0},{4,5},{5,6},{6,7},{7,4},{8,9},{9,10},{10,1... | collective-permute-start | bytes 1179656 | tf_op jit(solution)/shard_map/ppermute | solution.py:20
  103.1 0.6 shard_map.106
  103.7 1.3 %collective-permute-start.22 = (bf16[1,8,896]{2,1,0:T(8,128)(2,1)S(1)}, bf16[1,8,896]{2,1,0:T(8,128)(2,1)S(1)}, u32[]{:S(2)}, u32[]{:S(2)}) collective-permute-start(bf16[1,8,896]{2,1,0:T(8,128)(2,1)S(1)} %get-tuple-element.76), channel_id=1, source_target_pairs={{0,128},{8,136},{16,144},{24,152},{32,160},{40,168},{48,176},{56,1... | collective-permute-start | bytes 43016 | tf_op jit(solution)/shard_map/ppermute | solution.py:33
  104.9 4.0 %collective-permute-done.22.got = bf16[1,8,896]{2,1,0:T(8,128)(2,1)S(1)} collective-permute-done((bf16[1,8,896]{2,1,0:T(8,128)(2,1)S(1)}, bf16[1,8,896]{2,1,0:T(8,128)(2,1)S(1)}, u32[]{:S(2)}, u32[]{:S(2)}) %collective-permute-start.22) | collective-permute-done | bytes 14368 | tf_op jit(solution)/shard_map/ppermute | solution.py:33
  109.0 1.0 shard_map.107
  110.0 0.4 collective-permute-start.23
  110.3 3.5 %collective-permute-done.23.far = bf16[4,8,384]{2,1,0:T(8,128)(2,1)S(1)} collective-permute-done((bf16[4,8,384]{2,1,0:T(8,128)(2,1)S(1)}, bf16[4,8,384]{2,1,0:T(8,128)(2,1)S(1)}, u32[]{:S(2)}, u32[]{:S(2)}) %collective-permute-start.23) | collective-permute-done | bytes 24608 | tf_op jit(solution)/shard_map/ppermute | solution.py:24
  114.0 3.2 %collective-permute-start.25 = (bf16[8,384]{1,0:T(8,128)(2,1)S(1)}, bf16[8,384]{1,0:T(8,128)(2,1)S(1)}, u32[]{:S(2)}, u32[]{:S(2)}) collective-permute-start(bf16[8,384]{1,0:T(8,128)(2,1)S(1)} %get-tuple-element.86), channel_id=1, source_target_pairs={{0,1},{1,2},{2,3},{3,0},{4,5},{5,6},{6,7},{7,4},{8,9},{9,10},{10,1... | collective-permute-start | bytes 18440 | tf_op jit(solution)/shard_map/ppermute | solution.py:20
  117.2 1.6 %shard_map.108 = bf16[512,384]{1,0:T(8,128)(2,1)} custom-call(s32[85]{0:T(128)S(1)} %concatenate.15.place.allowed.marks.facts, bf16[512,384]{1,0:T(8,128)(2,1)S(1)} %get-tuple-element.69.own, bf16[512,384]{1,0:T(8,128)(2,1)S(1)} %collective-permute-done.19.far, bf16[512,384]{1,0:T(8,128)(2,1)S(1)} %collective-permute-done.20.low, ...), custom_call_target="tpu_custom_call" | custom-call | flops 1048576 | bytes 1048576 | tf_op jit(solution)/shard_map/pallas_call | solution.py:326
  118.8 3.5 %collective-permute-done.26.opposite = bf16[8,384]{1,0:T(8,128)(2,1)S(1)} collective-permute-done((bf16[8,384]{1,0:T(8,128)(2,1)S(1)}, bf16[8,384]{1,0:T(8,128)(2,1)S(1)}, u32[]{:S(2)}, u32[]{:S(2)}) %collective-permute-start.26) | collective-permute-done | bytes 6176 | tf_op jit(solution)/shard_map/ppermute | solution.py:20
  122.3 0.7 shard_map.110
  (47 shorter events, 1.2 us)
Async XLA Ops:
  0.6 12.5 %collective-permute-start.2 = (bf16[512,384]{1,0:T(8,128)(2,1)}, bf16[512,384]{1,0:T(8,128)(2,1)S(1)}, u32[]{:S(2)}, u32[]{:S(2)}) collective-permute-start(bf16[512,384]{1,0:T(8,128)(2,1)} %latents.3), channel_id=1, source_target_pairs={{0,3},{1,0},{2,1},{3,2},{4,7},{5,4},{6,5},{7,6},{8,11},{9,8},{10,9... | collective-permute-start | bytes 1179656 | tf_op jit(solution)/shard_map/ppermute | solution.py:20
  1.5 11.6 %collective-permute-start.1 = (bf16[512,384]{1,0:T(8,128)(2,1)}, bf16[512,384]{1,0:T(8,128)(2,1)S(1)}, u32[]{:S(2)}, u32[]{:S(2)}) collective-permute-start(bf16[512,384]{1,0:T(8,128)(2,1)} %latents.3), channel_id=1, source_target_pairs={{0,1},{1,2},{2,3},{3,0},{4,5},{5,6},{6,7},{7,4},{8,9},{9,10},{10,1... | collective-permute-start | bytes 1179656 | tf_op jit(solution)/shard_map/ppermute | solution.py:20
  3.9 10.9 %collective-permute-start = (bf16[512,384]{1,0:T(8,128)(2,1)}, bf16[512,384]{1,0:T(8,128)(2,1)S(1)}, u32[]{:S(2)}, u32[]{:S(2)}) collective-permute-start(bf16[512,384]{1,0:T(8,128)(2,1)} %latents.3), channel_id=1, source_target_pairs={{0,4},{1,5},{2,6},{3,7},{4,0},{5,1},{6,2},{7,3},{8,12},{9,13},{10,... | collective-permute-start | bytes 1179656 | tf_op jit(solution)/shard_map/ppermute | solution.py:24
  13.2 20.5 %copy-start.1 = (bf16[512,384]{1,0:T(8,128)(2,1)S(1)}, bf16[512,384]{1,0:T(8,128)(2,1)}, u32[]{:S(2)}) copy-start(bf16[512,384]{1,0:T(8,128)(2,1)} %latents.3) | copy-start | bytes 1179652
  13.3 20.4 %collective-permute-start.6 = (bf16[896,384]{1,0:T(8,128)(2,1)S(1)}, bf16[896,384]{1,0:T(8,128)(2,1)S(1)}, u32[]{:S(2)}, u32[]{:S(2)}) collective-permute-start(bf16[896,384]{1,0:T(8,128)(2,1)S(1)} %pad_maximum_fusion), channel_id=1, source_target_pairs={{0,4},{1,5},{2,6},{3,7},{4,0},{5,1},{6,2},{7,3},{8,12},{9,13},{10,... | collective-permute-start | bytes 2064392 | tf_op jit(solution)/shard_map/ppermute | solution.py:24
  14.9 15.2 %collective-permute-start.4 = (bf16[320,384]{1,0:T(8,128)(2,1)S(1)}, bf16[320,384]{1,0:T(8,128)(2,1)S(1)}, u32[]{:S(2)}, u32[]{:S(2)}) collective-permute-start(bf16[320,384]{1,0:T(8,128)(2,1)S(1)} %pad_maximum_fusion.1), channel_id=1, source_target_pairs={{0,1},{1,2},{2,3},{3,0},{4,5},{5,6},{6,7},{7,4},{8,9},{9,10},{10,1... | collective-permute-start | bytes 737288 | tf_op jit(solution)/shard_map/ppermute | solution.py:20
  17.9 15.8 %collective-permute-start.3 = (bf16[512,384]{1,0:T(8,128)(2,1)S(1)}, bf16[512,384]{1,0:T(8,128)(2,1)S(1)}, u32[]{:S(2)}, u32[]{:S(2)}) collective-permute-start(bf16[512,384]{1,0:T(8,128)(2,1)S(1)} %collective-permute-done.far), channel_id=1, source_target_pairs={{0,2},{1,3},{2,0},{3,1},{4,6},{5,7},{6,4},{7,5},{8,10},{9,11},{10,... | collective-permute-start | bytes 1179656 | tf_op jit(solution)/shard_map/ppermute | solution.py:20
  18.1 15.7 %collective-permute-start.5 = (bf16[320,384]{1,0:T(8,128)(2,1)S(1)}, bf16[320,384]{1,0:T(8,128)(2,1)S(1)}, u32[]{:S(2)}, u32[]{:S(2)}) collective-permute-start(bf16[320,384]{1,0:T(8,128)(2,1)S(1)} %pad_maximum_fusion.2), channel_id=1, source_target_pairs={{0,3},{1,0},{2,1},{3,2},{4,7},{5,4},{6,5},{7,6},{8,11},{9,8},{10,9... | collective-permute-start | bytes 737288 | tf_op jit(solution)/shard_map/ppermute | solution.py:20
  40.0 14.1 %collective-permute-start.9 = (bf16[2,3,512,128]{3,2,1,0:T(8,128)(2,1)S(1)}, bf16[2,3,512,128]{3,2,1,0:T(8,128)(2,1)S(1)}, u32[]{:S(2)}, u32[]{:S(2)}) collective-permute-start(bf16[2,3,512,128]{3,2,1,0:T(8,128)(2,1)S(1)} %shard_map.96.rest_0_), channel_id=1, source_target_pairs={{0,8},{8,0},{16,24},{24,16},{32,40},{40,32},{48,56},{56,48},{64,72... | collective-permute-start | bytes 2359304 | tf_op jit(solution)/shard_map/ppermute | solution.py:33
  40.1 26.4 %collective-permute-start.8 = (bf16[2,3,512,128]{3,2,1,0:T(8,128)(2,1)S(1)}, bf16[2,3,512,128]{3,2,1,0:T(8,128)(2,1)S(1)}, u32[]{:S(2)}, u32[]{:S(2)}) collective-permute-start(bf16[2,3,512,128]{3,2,1,0:T(8,128)(2,1)S(1)} %shard_map.96.rest_0_), channel_id=1, source_target_pairs={{0,16},{8,24},{16,32},{24,40},{32,48},{40,56},{48,64},{56,72},{64,... | collective-permute-start | bytes 2359304 | tf_op jit(solution)/shard_map/ppermute | solution.py:29
  42.1 24.4 %collective-permute-start.7 = (bf16[2,3,512,128]{3,2,1,0:T(8,128)(2,1)S(1)}, bf16[2,3,512,128]{3,2,1,0:T(8,128)(2,1)S(1)}, u32[]{:S(2)}, u32[]{:S(2)}) collective-permute-start(bf16[2,3,512,128]{3,2,1,0:T(8,128)(2,1)S(1)} %shard_map.96.rest_0_), channel_id=1, source_target_pairs={{0,240},{8,248},{16,0},{24,8},{32,16},{40,24},{48,32},{56,40},{64,... | collective-permute-start | bytes 2359304 | tf_op jit(solution)/shard_map/ppermute | solution.py:29
  66.6 2.9 %collective-permute-start.10 = (bf16[2,3,512,128]{3,2,1,0:T(8,128)(2,1)S(1)}, bf16[2,3,512,128]{3,2,1,0:T(8,128)(2,1)S(1)}, u32[]{:S(2)}, u32[]{:S(2)}) collective-permute-start(bf16[2,3,512,128]{3,2,1,0:T(8,128)(2,1)S(1)} %broadcast_select_fusion), channel_id=1, source_target_pairs={{0,8},{8,0},{16,24},{24,16},{32,40},{40,32},{48,56},{56,48},{64,72... | collective-permute-start | bytes 2359304 | tf_op jit(solution)/shard_map/ppermute | solution.py:33
  69.5 2.2 %copy-start = (bf16[384,3072]{1,0:T(8,128)(2,1)S(1)}, bf16[384,3072]{1,0:T(8,128)(2,1)}, u32[]{:S(2)}) copy-start(bf16[384,3072]{1,0:T(8,128)(2,1)} %weight.5) | copy-start | bytes 7077892
  73.2 23.2 %collective-permute-start.14 = (bf16[896,384]{1,0:T(8,128)(2,1)S(1)}, bf16[896,384]{1,0:T(8,128)(2,1)S(1)}, u32[]{:S(2)}, u32[]{:S(2)}) collective-permute-start(bf16[896,384]{1,0:T(8,128)(2,1)S(1)} %get-tuple-element.56), channel_id=1, source_target_pairs={{0,4},{1,5},{2,6},{3,7},{4,0},{5,1},{6,2},{7,3},{8,12},{9,13},{10,... | collective-permute-start | bytes 2064392 | tf_op jit(solution)/shard_map/ppermute | solution.py:24
  74.1 4.4 %collective-permute-start.15 = (bf16[16,8,896]{2,1,0:T(8,128)(2,1)S(1)}, bf16[16,8,896]{2,1,0:T(8,128)(2,1)S(1)}, u32[]{:S(2)}, u32[]{:S(2)}) collective-permute-start(bf16[16,8,896]{2,1,0:T(8,128)(2,1)S(1)} %get-tuple-element.59), channel_id=1, source_target_pairs={{0,8},{8,0},{16,24},{24,16},{32,40},{40,32},{48,56},{56,48},{64,72... | collective-permute-start | bytes 688136 | tf_op jit(solution)/shard_map/ppermute | solution.py:33
  74.8 18.2 %collective-permute-start.11 = (bf16[512,384]{1,0:T(8,128)(2,1)S(1)}, bf16[512,384]{1,0:T(8,128)(2,1)S(1)}, u32[]{:S(2)}, u32[]{:S(2)}) collective-permute-start(bf16[512,384]{1,0:T(8,128)(2,1)S(1)} %get-tuple-element.53), channel_id=1, source_target_pairs={{0,2},{1,3},{2,0},{3,1},{4,6},{5,7},{6,4},{7,5},{8,10},{9,11},{10,... | collective-permute-start | bytes 1179656 | tf_op jit(solution)/shard_map/ppermute | solution.py:20
  75.2 17.7 %collective-permute-start.12 = (bf16[320,384]{1,0:T(8,128)(2,1)S(1)}, bf16[320,384]{1,0:T(8,128)(2,1)S(1)}, u32[]{:S(2)}, u32[]{:S(2)}) collective-permute-start(bf16[320,384]{1,0:T(8,128)(2,1)S(1)} %get-tuple-element.54), channel_id=1, source_target_pairs={{0,3},{1,0},{2,1},{3,2},{4,7},{5,4},{6,5},{7,6},{8,11},{9,8},{10,9... | collective-permute-start | bytes 737288 | tf_op jit(solution)/shard_map/ppermute | solution.py:20
  76.4 16.6 %collective-permute-start.13 = (bf16[320,384]{1,0:T(8,128)(2,1)S(1)}, bf16[320,384]{1,0:T(8,128)(2,1)S(1)}, u32[]{:S(2)}, u32[]{:S(2)}) collective-permute-start(bf16[320,384]{1,0:T(8,128)(2,1)S(1)} %get-tuple-element.55), channel_id=1, source_target_pairs={{0,1},{1,2},{2,3},{3,0},{4,5},{5,6},{6,7},{7,4},{8,9},{9,10},{10,1... | collective-permute-start | bytes 737288 | tf_op jit(solution)/shard_map/ppermute | solution.py:20
  79.1 4.9 %collective-permute-start.16 = (bf16[8,8,896]{2,1,0:T(8,128)(2,1)S(1)}, bf16[8,8,896]{2,1,0:T(8,128)(2,1)S(1)}, u32[]{:S(2)}, u32[]{:S(2)}) collective-permute-start(bf16[8,8,896]{2,1,0:T(8,128)(2,1)S(1)} %get-tuple-element.61), channel_id=1, source_target_pairs={{0,16},{8,24},{16,0},{24,8},{32,48},{40,56},{48,32},{56,40},{64,80... | collective-permute-start | bytes 344072 | tf_op jit(solution)/shard_map/ppermute | solution.py:33
  84.5 5.3 %collective-permute-start.17 = (bf16[4,8,896]{2,1,0:T(8,128)(2,1)S(1)}, bf16[4,8,896]{2,1,0:T(8,128)(2,1)S(1)}, u32[]{:S(2)}, u32[]{:S(2)}) collective-permute-start(bf16[4,8,896]{2,1,0:T(8,128)(2,1)S(1)} %get-tuple-element.63), channel_id=1, source_target_pairs={{0,32},{8,40},{16,48},{24,56},{32,0},{40,8},{48,16},{56,24},{64,96... | collective-permute-start | bytes 172040 | tf_op jit(solution)/shard_map/ppermute | solution.py:33
  90.4 6.1 %collective-permute-start.18 = (bf16[2,8,896]{2,1,0:T(8,128)(2,1)S(1)}, bf16[2,8,896]{2,1,0:T(8,128)(2,1)S(1)}, u32[]{:S(2)}, u32[]{:S(2)}) collective-permute-start(bf16[2,8,896]{2,1,0:T(8,128)(2,1)S(1)} %get-tuple-element.64), channel_id=1, source_target_pairs={{0,96},{8,104},{16,112},{24,120},{32,64},{40,72},{48,80},{56,88},{... | collective-permute-start | bytes 86024 | tf_op jit(solution)/shard_map/ppermute | solution.py:33
  98.0 19.1 %copy-start.2 = (bf16[50,384]{1,0:T(8,128)(2,1)S(1)}, bf16[50,384]{1,0:T(8,128)(2,1)}, u32[]{:S(2)}) copy-start(bf16[50,384]{1,0:T(8,128)(2,1)} %gates.3) | copy-start | bytes 115204
  98.1 15.8 %collective-permute-start.19 = (bf16[512,384]{1,0:T(8,128)(2,1)S(1)}, bf16[512,384]{1,0:T(8,128)(2,1)S(1)}, u32[]{:S(2)}, u32[]{:S(2)}) collective-permute-start(bf16[512,384]{1,0:T(8,128)(2,1)S(1)} %get-tuple-element.70), channel_id=1, source_target_pairs={{0,4},{1,5},{2,6},{3,7},{4,0},{5,1},{6,2},{7,3},{8,12},{9,13},{10,... | collective-permute-start | bytes 1179656 | tf_op jit(solution)/shard_map/ppermute | solution.py:24
  99.9 14.0 %collective-permute-start.20 = (bf16[512,384]{1,0:T(8,128)(2,1)S(1)}, bf16[512,384]{1,0:T(8,128)(2,1)S(1)}, u32[]{:S(2)}, u32[]{:S(2)}) collective-permute-start(bf16[512,384]{1,0:T(8,128)(2,1)S(1)} %get-tuple-element.71), channel_id=1, source_target_pairs={{0,3},{1,0},{2,1},{3,2},{4,7},{5,4},{6,5},{7,6},{8,11},{9,8},{10,9... | collective-permute-start | bytes 1179656 | tf_op jit(solution)/shard_map/ppermute | solution.py:20
  99.9 13.9 %collective-permute-start.21 = (bf16[512,384]{1,0:T(8,128)(2,1)S(1)}, bf16[512,384]{1,0:T(8,128)(2,1)S(1)}, u32[]{:S(2)}, u32[]{:S(2)}) collective-permute-start(bf16[512,384]{1,0:T(8,128)(2,1)S(1)} %get-tuple-element.72), channel_id=1, source_target_pairs={{0,1},{1,2},{2,3},{3,0},{4,5},{5,6},{6,7},{7,4},{8,9},{9,10},{10,1... | collective-permute-start | bytes 1179656 | tf_op jit(solution)/shard_map/ppermute | solution.py:20
  103.7 5.3 %collective-permute-start.22 = (bf16[1,8,896]{2,1,0:T(8,128)(2,1)S(1)}, bf16[1,8,896]{2,1,0:T(8,128)(2,1)S(1)}, u32[]{:S(2)}, u32[]{:S(2)}) collective-permute-start(bf16[1,8,896]{2,1,0:T(8,128)(2,1)S(1)} %get-tuple-element.76), channel_id=1, source_target_pairs={{0,128},{8,136},{16,144},{24,152},{32,160},{40,168},{48,176},{56,1... | collective-permute-start | bytes 43016 | tf_op jit(solution)/shard_map/ppermute | solution.py:33
  110.0 3.9 %collective-permute-start.23 = (bf16[4,8,384]{2,1,0:T(8,128)(2,1)S(1)}, bf16[4,8,384]{2,1,0:T(8,128)(2,1)S(1)}, u32[]{:S(2)}, u32[]{:S(2)}) collective-permute-start(bf16[4,8,384]{2,1,0:T(8,128)(2,1)S(1)} %get-tuple-element.77), channel_id=1, source_target_pairs={{0,4},{1,5},{2,6},{3,7},{4,0},{5,1},{6,2},{7,3},{8,12},{9,13},{10,... | collective-permute-start | bytes 73736 | tf_op jit(solution)/shard_map/ppermute | solution.py:24
  113.9 4.9 %collective-permute-start.24 = (bf16[8,384]{1,0:T(8,128)(2,1)S(1)}, bf16[8,384]{1,0:T(8,128)(2,1)S(1)}, u32[]{:S(2)}, u32[]{:S(2)}) collective-permute-start(bf16[8,384]{1,0:T(8,128)(2,1)S(1)} %get-tuple-element.85), channel_id=1, source_target_pairs={{0,3},{1,0},{2,1},{3,2},{4,7},{5,4},{6,5},{7,6},{8,11},{9,8},{10,9... | collective-permute-start | bytes 18440 | tf_op jit(solution)/shard_map/ppermute | solution.py:20
  114.0 4.8 %collective-permute-start.25 = (bf16[8,384]{1,0:T(8,128)(2,1)S(1)}, bf16[8,384]{1,0:T(8,128)(2,1)S(1)}, u32[]{:S(2)}, u32[]{:S(2)}) collective-permute-start(bf16[8,384]{1,0:T(8,128)(2,1)S(1)} %get-tuple-element.86), channel_id=1, source_target_pairs={{0,1},{1,2},{2,3},{3,0},{4,5},{5,6},{6,7},{7,4},{8,9},{9,10},{10,1... | collective-permute-start | bytes 18440 | tf_op jit(solution)/shard_map/ppermute | solution.py:20
  117.2 5.1 %collective-permute-start.26 = (bf16[8,384]{1,0:T(8,128)(2,1)S(1)}, bf16[8,384]{1,0:T(8,128)(2,1)S(1)}, u32[]{:S(2)}, u32[]{:S(2)}) collective-permute-start(bf16[8,384]{1,0:T(8,128)(2,1)S(1)} %get-tuple-element.87), channel_id=1, source_target_pairs={{0,2},{1,3},{2,0},{3,1},{4,6},{5,7},{6,4},{7,5},{8,10},{9,11},{10,... | collective-permute-start | bytes 18440 | tf_op jit(solution)/shard_map/ppermute | solution.py:20
